TPU v7x, 32 devices: a whole 2x2x4 slice. The times are simulated.
32 devices in a mesh: shard: 4 (over x, core), rep: 8 (over z, y).
Axes of the slice: x: 2, y: 2, z: 4, core: 2. Of those that a mesh axis runs over, the one named last changes fastest.
Arguments:
- grads: bfloat16 [4, 8, 262144], P('shard', 'rep'), may hold values from -5000 to 5000
- momentum_codes: int32 [262144], P(('shard', 'rep')), may hold values from -127 to 127
- variance_codes: int32 [262144], P(('shard', 'rep')), may hold values from 16 to 255
- momentum_scale: float32 [160], P(('shard', 'rep')), may hold values from 0.5 to 4, as said below
- variance_scale: float32 [160], P(('shard', 'rep')), may hold values from 1 to 4, as said below
- master: float32 [262144], P(('shard', 'rep')), may hold values from -2.5 to 2.5
- step: int32 [1], replicated, may hold values from 1 to 19
Outputs:
- new_master: float32 [262144], P(('shard', 'rep'))
- weights: bfloat16 [262144], P('shard')
- update: float32 [262144], P(('shard', 'rep'))
- momentum_norm: float32 [262144], P(('shard', 'rep'))
- variance_norm: float32 [262144], P(('shard', 'rep'))
- momentum_absmax: float32 [160], P(('shard', 'rep'))
- variance_absmax: float32 [160], P(('shard', 'rep'))
Inputs may be any that keep to these rules, and one draw needn't show every extreme that they name: `momentum_scale`: A block touched by two neighbouring devices has the same value in both devices' slots. `variance_scale`: A block touched by two neighbouring devices has the same value in both devices' slots.
All inputs are finite; a program needn't handle non-finite values.
Results may differ from a plain program's by a relative error of at most 0.0004.
Values may be sent and summed in bfloat16 or wider, within the bound.
No kernel may reach another device: no remote copies, remote signals or barrier semaphores. Data moves between devices by JAX's collectives and lax.ppermute only.
A program may use at most 64 MiB of HBM per device.

v0:
```python
import jax
import jax.numpy as jnp
from jax import lax
from jax.sharding import PartitionSpec as P

BLOCK = 2048


def extended(block, sides, width):
    for axis, dim in sides:
        count = lax.axis_size(axis)
        forward = [(i, i + 1) for i in range(count - 1)]
        backward = [(target, source) for source, target in forward]
        low = lax.ppermute(
            lax.slice_in_dim(block, block.shape[dim] - width, None, axis=dim), axis, forward
        )
        high = lax.ppermute(lax.slice_in_dim(block, 0, width, axis=dim), axis, backward)
        block = jnp.concatenate([low, block, high], axis=dim)
    return block


def on_device(grads, momentum_codes, variance_codes, momentum_scale, variance_scale, master, step):
    own_len = master.shape[0]
    slot_count = momentum_scale.shape[0]
    block_len = BLOCK
    half_len = block_len // 2
    shard_count = lax.axis_size("shard")
    rep_count = lax.axis_size("rep")
    grad_terms = grads.reshape(-1).astype(jnp.float32)
    partial_sum = lax.psum_scatter(grad_terms, "shard", scatter_dimension=0, tiled=True)
    gsum = lax.psum_scatter(partial_sum, "rep", scatter_dimension=0, tiled=True)
    norm_sq = lax.psum(jnp.sum(gsum * gsum), ("shard", "rep"))
    total_params = own_len * shard_count * rep_count
    clip_factor = jnp.minimum(1.0, float(total_params) ** 0.5 / (jnp.sqrt(norm_sq) + 1e-06))
    scaled = gsum * clip_factor

    def spread(scale_table):
        return jnp.repeat(scale_table, block_len)[half_len : half_len + own_len]

    m_old = momentum_codes.astype(jnp.float32) / 127.0 * spread(momentum_scale)
    v_old = variance_codes.astype(jnp.float32) / 255.0 * spread(variance_scale)
    momentum = 0.9 * m_old + 0.1 * scaled
    variance = 0.95 * v_old + 0.05 * scaled * scaled
    count = step[0].astype(jnp.float32)
    first_fix = 1.0 - jnp.power(jnp.float32(0.9), count)
    second_fix = 1.0 - jnp.power(jnp.float32(0.95), count)
    update = momentum / first_fix / (jnp.sqrt(variance / second_fix) + 1e-08)
    new_master = master * (1.0 - 0.0001 * 0.1) - 0.0001 * update
    weights = lax.all_gather(new_master.astype(jnp.bfloat16), "rep", axis=0, tiled=True)

    def slot_max(values):
        padded = jnp.pad(jnp.abs(values), (half_len, half_len))
        return jnp.max(padded.reshape(slot_count, block_len), axis=1)

    m_table = slot_max(momentum)
    v_table = slot_max(variance)
    own_edge = jnp.stack(
        [jnp.stack([m_table[0], v_table[0]]), jnp.stack([m_table[-1], v_table[-1]])]
    )
    rim_vals = extended(own_edge, ((("shard", "rep"), 0),), 1)
    m_table = m_table.at[0].max(rim_vals[0, 0]).at[-1].max(rim_vals[3, 0])
    v_table = v_table.at[0].max(rim_vals[0, 1]).at[-1].max(rim_vals[3, 1])
    momentum_norm = momentum / (spread(m_table) + 1e-06)
    variance_norm = variance / (spread(v_table) + 1e-06)
    return (new_master, weights, update, momentum_norm, variance_norm, m_table, v_table)


def solution(mesh):
    in_specs = (
        P("shard", "rep", None),
        P(("shard", "rep")),
        P(("shard", "rep")),
        P(("shard", "rep")),
        P(("shard", "rep")),
        P(("shard", "rep")),
        P(),
    )
    out_specs = (
        P(("shard", "rep")),
        P("shard"),
        P(("shard", "rep")),
        P(("shard", "rep")),
        P(("shard", "rep")),
        P(("shard", "rep")),
        P(("shard", "rep")),
    )
    return jax.shard_map(
        on_device, mesh=mesh, in_specs=in_specs, out_specs=out_specs, check_vma=False
    )
```

profile of v0, /device:TPU:0, one launch (start us, length us, event | category | flops | bytes accessed | tf_op | source)
XLA Modules:
  0.0 228.2 jit_solution(9442840896526550554)
XLA Ops:
  7.2 0.0 all-reduce.7.cloned.1.call-start
  7.2 2.9 %convert_element_type.28 = f32[1,1,262144]{2,1,0:T(1,128)} convert(bf16[1,1,262144]{2,1,0:T(2,128)(2,1)} %param.15) | non-fusion elementwise | flops 262144 | bytes 1572864 | tf_op jit(solution)/shard_map/convert_element_type | solution.py:29
  10.1 0.0 all-reduce.7.cloned.1.call-update
  10.2 0.0 all-reduce.9.cloned.1.call-start
  10.2 0.0 copy-start.8
  10.2 0.6 copy-done.8
  10.9 0.6 dynamic-slice.24
  12.1 37.1 %all-reduce.7.cloned.1.call-done = f32[262144]{0:T(1024)} async-done(((f32[262144]{0:T(1024)}), f32[262144]{0:T(1024)}) %all-reduce.7.cloned.1.call-update) | async-done | bytes 1048592
  49.2 1.7 dynamic-slice.25
  50.9 0.0 copy-start.7
  50.9 0.0 all-reduce.9.cloned.1.call-update
  50.9 0.6 copy-done.7
  51.5 0.0 copy-start.5
  51.5 0.6 dynamic-slice.26
  52.1 0.1 copy-done.5
  52.2 0.1 broadcast_in_dim.13
  52.3 0.0 copy-start.6
  52.3 0.6 copy-done.6
  52.9 0.1 broadcast_in_dim.12
  53.0 0.0 copy-start.1
  53.0 0.0 copy-start
  54.4 69.4 %all-reduce.9.cloned.1.call-done = f32[65536]{0:T(1024)} async-done(((f32[65536]{0:T(1024)}), f32[65536]{0:T(1024)}) %all-reduce.9.cloned.1.call-update) | async-done | bytes 262160
  123.9 1.4 multiply_reduce_fusion
  125.2 39.8 %psum.7 = f32[]{:T(128)} all-reduce(f32[]{:T(128)} %multiply_reduce_fusion), channel_id=1, replica_groups=mesh['shard'=4,'rep'=8] {'shard','rep'}, use_global_device_ids=true, to_apply=%region_3.0 | all-reduce | flops 1 | bytes 8 | tf_op jit(solution)/shard_map/psum | solution.py:32
  165.7 0.0 copy-done.1
  165.7 0.0 copy-done
  165.8 0.8 fusion.6
  166.6 0.1 reduce_max.19
  166.7 0.6 slice.84
  167.3 0.1 reduce_max.18
  167.4 0.6 slice.83
  168.0 1.4 maximum_bitcast_fusion
  169.4 4.4 %collective-permute-start = (f32[1,2]{1,0:T(1,128)S(1)}, f32[1,2]{1,0:T(1,128)S(1)}, u32[]{:S(2)}, u32[]{:S(2)}) collective-permute-start(f32[1,2]{1,0:T(1,128)S(1)} %maximum_bitcast_fusion), channel_id=1, source_target_pairs={{0,1},{1,2},{2,3},{3,4},{4,5},{5,6},{6,7},{7,8},{8,9},{9,10},{10,1... | collective-permute-start | bytes 32 | tf_op jit(solution)/shard_map/ppermute | solution.py:14
  173.8 1.3 collective-permute-done
  175.0 0.6 fusion.12
  175.6 1.8 constant_dynamic-update-slice_fusion.2
  177.4 1.4 maximum_bitcast_fusion.1
  178.8 1.3 collective-permute-start.1
  180.1 4.4 %collective-permute-done.1 = f32[1,2]{1,0:T(1,128)S(1)} collective-permute-done((f32[1,2]{1,0:T(1,128)S(1)}, f32[1,2]{1,0:T(1,128)S(1)}, u32[]{:S(2)}, u32[]{:S(2)}) %collective-permute-start.1) | collective-permute-done | bytes 40 | tf_op jit(solution)/shard_map/ppermute | solution.py:17
  184.5 0.6 fusion.11
  185.0 0.8 constant_dynamic-update-slice_fusion
  185.8 0.0 copy-start.3
  185.8 0.1 broadcast_in_dim.15
  185.9 0.4 copy-done.3
  186.4 0.8 constant_dynamic-update-slice_fusion.1
  187.2 0.0 copy-start.4
  187.2 0.1 broadcast_in_dim.14
  187.2 0.4 copy-done.4
  187.7 0.0 copy-start.2
  187.7 0.7 copy-done.2
  188.4 0.7 fusion.10
  189.1 31.6 %all_gather.3 = bf16[65536]{0:T(1024)(128)(2,1)S(1)} all-gather(bf16[8192]{0:T(1024)(128)(2,1)S(1)} %get-tuple-element.59), channel_id=1, replica_groups=mesh['shard'=4,'rep'=8] {'rep'}, dimensions={0}, use_global_device_ids=true | all-gather | bytes 147456 | tf_op jit(solution)/shard_map/all_gather | solution.py:49
  220.7 0.7 copy.22
  (8 shorter events, 0.1 us)
Async XLA Ops:
  7.2 42.0 %all-reduce.7.cloned.1.call-start = ((), (), s32[]{:S(2)}) async-start(), calls=%async_computation | async-start | bytes 2097152
  10.2 113.7 %all-reduce.9.cloned.1.call-start = ((), (), s32[]{:S(2)}) async-start(), calls=%async_computation.1 | async-start | bytes 524288
  10.2 0.7 copy-start.8
  50.9 0.7 copy-start.7
  51.5 0.7 copy-start.5
  52.3 0.7 copy-start.6
  53.0 112.7 %copy-start.1 = (s32[8192]{0:T(1024)S(1)}, s32[8192]{0:T(1024)}, u32[]{:S(2)}) copy-start(s32[8192]{0:T(1024)} %param.16) | copy-start | bytes 98308
  53.0 112.7 %copy-start = (s32[8192]{0:T(1024)S(1)}, s32[8192]{0:T(1024)}, u32[]{:S(2)}) copy-start(s32[8192]{0:T(1024)} %param.17) | copy-start | bytes 98308
  169.4 5.6 %collective-permute-start = (f32[1,2]{1,0:T(1,128)S(1)}, f32[1,2]{1,0:T(1,128)S(1)}, u32[]{:S(2)}, u32[]{:S(2)}) collective-permute-start(f32[1,2]{1,0:T(1,128)S(1)} %maximum_bitcast_fusion), channel_id=1, source_target_pairs={{0,1},{1,2},{2,3},{3,4},{4,5},{5,6},{6,7},{7,8},{8,9},{9,10},{10,1... | collective-permute-start | bytes 32 | tf_op jit(solution)/shard_map/ppermute | solution.py:14
  178.8 5.7 %collective-permute-start.1 = (f32[1,2]{1,0:T(1,128)S(1)}, f32[1,2]{1,0:T(1,128)S(1)}, u32[]{:S(2)}, u32[]{:S(2)}) collective-permute-start(f32[1,2]{1,0:T(1,128)S(1)} %maximum_bitcast_fusion.1), channel_id=1, source_target_pairs={{1,0},{2,1},{3,2},{4,3},{5,4},{6,5},{7,6},{8,7},{9,8},{10,9},{11,1... | collective-permute-start | bytes 32 | tf_op jit(solution)/shard_map/ppermute | solution.py:17
  185.8 0.5 copy-start.3
  187.2 0.5 copy-start.4
  187.7 0.8 copy-start.2
Sparse Core Ops, SparseCore 0:
  10.4 38.8 all-reduce.6
  52.9 70.8 all-reduce.8
where the time goes:
time: 230 us; the launch traced here: 228 us
  waiting for transfers between devices  112 us (49%)
  blocking collectives  71.4 us (31%)
  between operations  16.9 us (7%)
  other arithmetic  12.2 us (5%)
  local copies, waits for them, and re-layouts  9.82 us (4%)
  starting transfers between devices  5.72 us (2%)
    unnamed x4, waiting for transfers between devices  107 us
    psum x1, blocking collectives, on_device(): norm_sq = lax.psum(jnp.sum(gsum * gsum), ('shard', 'rep'))  39.8 us
    all_gather x1, blocking collectives, on_device(): lax.all_gather(new_master.astype(jnp.bfloat16), 'rep', axis=0, tiled=True)  31.6 us
    unnamed x22, local copies, waits for them, and re-layouts  7.1 us
  transfers between devices with their start and end apart: 4, of which 4 were waited for; matrix products, arithmetic and copies ran while one was open for 1% of the time, Pallas kernels for 0%

commit v1 on v0

v1 whole, which is shorter than its diff:
```python
import functools

import jax
import jax.numpy as jnp
from jax import lax
from jax.experimental import pallas as pl
from jax.experimental.pallas import tpu as pltpu
from jax.sharding import PartitionSpec as P

BLOCK = 2048
LANES = 128
EDGE = BLOCK // 2 // LANES
ALL = ("shard", "rep")
BF16 = jnp.bfloat16
F32 = jnp.float32
VMEM = pl.BlockSpec(memory_space=pltpu.VMEM)
SMEM = pl.BlockSpec(memory_space=pltpu.SMEM)
ANY = pl.BlockSpec(memory_space=pl.ANY)


class Plan:
    def __init__(self, own_len):
        self.shards = lax.axis_size("shard")
        self.reps = lax.axis_size("rep")
        self.devices = self.shards * self.reps
        self.xs = self.shards // 2
        self.zs = self.reps // 2
        self.groups = self.xs * 2
        self.rows = own_len // LANES

    def swap(self, value, core=0, z=0, group=0):
        x, y = group >> 1, group & 1
        mask = ((x << 1) | core) * self.reps + ((z << 1) | y)
        return lax.ppermute(value, ALL, [(i, i ^ mask) for i in range(self.devices)])


def place():
    shard, rep = lax.axis_index("shard"), lax.axis_index("rep")
    return shard // 2, shard % 2, rep // 2, rep % 2


def tree(values):
    values = list(values)
    while len(values) > 1:
        values = [a + b for a, b in zip(values[::2], values[1::2])]
    return values[0]


def call(kernel, outs, ins, in_specs=None, out_specs=None, scratch=(), limit=16):
    return pl.pallas_call(
        kernel,
        out_shape=outs,
        in_specs=in_specs or [VMEM] * len(ins),
        out_specs=out_specs or jax.tree.map(lambda _: VMEM, outs),
        scratch_shapes=list(scratch),
        compiler_params=pltpu.CompilerParams(vmem_limit_bytes=limit * 1024 * 1024),
    )(*ins)


def half_kernel(flip, count, length, x_ref, o_ref, buf, sem):
    _, core, _, _ = place()
    want = (core + flip) % 2
    rows = length // LANES
    copies = []
    for k in range(count):
        start = pl.multiple_of((2 * k + want) * length, length)
        copies.append(pltpu.make_async_copy(x_ref.at[:, pl.ds(start, length)], buf.at[k], sem.at[k]))
        copies[-1].start()
    for k in range(count):
        copies[k].wait()
        o_ref[pl.ds(k * rows, rows), :] = buf[k].astype(F32).reshape(rows, LANES).astype(BF16)


def half(plan, grads, flip):
    length = plan.reps * plan.rows * LANES
    return call(
        functools.partial(half_kernel, flip, plan.xs, length),
        jax.ShapeDtypeStruct((plan.xs * length // LANES, LANES), BF16),
        [grads],
        in_specs=[ANY],
        scratch=[pltpu.VMEM((plan.xs, 1, length), BF16), pltpu.SemaphoreType.DMA((plan.xs,))],
    )


def pair_kernel(plan, mine_ref, other_ref, *outs):
    x, _, _, y = place()
    for k, out in enumerate(outs):
        to_x, to_y = x ^ (k >> 1), y ^ (k & 1)
        for z in range(plan.zs):
            start = pl.multiple_of((to_x * plan.reps + 2 * z + to_y) * plan.rows, plan.rows)
            rows = pl.ds(start, plan.rows)
            out[pl.ds(z * plan.rows, plan.rows), :] = mine_ref[rows, :].astype(F32) + other_ref[rows, :].astype(F32)


def sum_kernel(*refs):
    refs[-1][...] = tree([r[...] for r in refs[:-1]])


def state_kernel(plan, mc_ref, vc_ref, ms_ref, vs_ref, master_ref, o_ref):
    slots = ms_ref.shape[0]
    for j in range(slots):
        low, high = max(0, (2 * j - 1) * EDGE), min(plan.rows, (2 * j + 1) * EDGE)
        o_ref[low:high, :] = mc_ref[low:high, :].astype(F32) / 127.0 * ms_ref[j]
        o_ref[plan.rows + low : plan.rows + high, :] = vc_ref[low:high, :].astype(F32) / 255.0 * vs_ref[j]
    o_ref[2 * plan.rows :, :] = master_ref[...]


def order_kernel(plan, *refs):
    _, _, z, _ = place()
    for k, ref in enumerate(refs[:-1]):
        refs[-1][z ^ k] = ref[...]


def total_kernel(plan, *refs):
    parts, (state_ref, sum_ref, send_ref) = refs[: plan.zs], refs[plan.zs :]
    _, _, _, y = place()
    total = tree([r[...] for r in parts])
    sum_ref[...] = total
    send_ref[0:8, :] = jnp.sum((total * total).reshape(-1, 8, LANES), axis=0)

    def edge(z, start):
        send_ref[8 : 8 + EDGE, :] = sum_ref[z * plan.rows + start : z * plan.rows + start + EDGE, :]
        for k in range(2):
            at = k * plan.rows + start
            send_ref[8 + (k + 1) * EDGE : 8 + (k + 2) * EDGE, :] = state_ref[z, at : at + EDGE, :]

    @pl.when(y == 0)
    def _():
        edge(0, 0)

    @pl.when(y == 1)
    def _():
        edge(plan.zs - 1, plan.rows - EDGE)


def core_kernel(mine_ref, other_ref, norm_ref, relay_ref):
    norm = mine_ref[0:8, :] + other_ref[0:8, :]
    norm_ref[...] = norm
    relay_ref[0:8, :] = norm
    relay_ref[8:, :] = other_ref[8:, :]


def main_kernel(plan, total_params, *refs):
    norms, refs = refs[: plan.groups], refs[plan.groups :]
    (sum_mine, sum_other, state_mine, state_other, fix_ref) = refs[:5]
    (master_out, weights_out, update_out, mn_out, vn_out, mt_out, vt_out) = refs[5:12]
    m_buf, v_buf, far = refs[12:]
    x, core, z, y = place()
    rows = plan.rows
    slots = mt_out.shape[0]
    norm_sq = jnp.sum(tree([r[0:8, :] for r in norms]), keepdims=True)
    clip = jnp.minimum(1.0, float(total_params) ** 0.5 / (jnp.sqrt(norm_sq) + 1e-06))
    first_fix, second_fix = fix_ref[0], fix_ref[1]

    def moments(grad, m_old, v_old):
        scaled = grad * clip
        return 0.9 * m_old + 0.1 * scaled, 0.95 * v_old + 0.05 * scaled * scaled

    def step(grad, state):
        m, v = moments(grad, state[0:rows], state[rows : 2 * rows])
        update = m / first_fix / (jnp.sqrt(v / second_fix) + 1e-08)
        return m, v, update, state[2 * rows :] * (1.0 - 0.0001 * 0.1) - 0.0001 * update

    for k in range(plan.zs):
        at = pl.ds(k * rows, rows)
        for flip, (sums, states) in enumerate(((sum_mine, state_mine), (sum_other, state_other))):
            out = step(sums[at, :], states[k])[3]
            start = pl.multiple_of((2 * k + (y ^ flip)) * rows, rows)
            weights_out[pl.ds(start, rows), :] = out.astype(BF16)

    m, v, update, master = step(sum_mine[pl.ds(pl.multiple_of(z * rows, rows), rows), :], state_mine[z])
    update_out[...] = update
    master_out[...] = master
    m_buf[...] = m
    v_buf[...] = v

    far[...] = jnp.zeros_like(far)

    def near(side, at_z, start):
        grad = sum_other[pl.ds(pl.multiple_of(at_z * rows + start, EDGE), EDGE), :]
        low = state_other[at_z, start : start + EDGE, :]
        high = state_other[at_z, rows + start : rows + start + EDGE, :]
        em, ev = moments(grad, low, high)
        far[side, 0], far[side, 1] = jnp.abs(em), jnp.abs(ev)

    def across(side, shard):
        for k in range(1, plan.groups, 2):
            @pl.when((shard >= 0) & (shard < plan.shards) & ((x ^ (k >> 1)) == shard // 2))
            def _():
                em, ev = moments(*(norms[k][8 + j * EDGE : 8 + (j + 1) * EDGE, :] for j in range(3)))
                far[side, 0], far[side, 1] = jnp.abs(em), jnp.abs(ev)

    shard = 2 * x + core

    @pl.when(y == 0)
    def _():
        near(1, z, 0)

        @pl.when(z > 0)
        def _():
            near(0, z - 1, rows - EDGE)

        @pl.when(z == 0)
        def _():
            across(0, shard - 1)

    @pl.when(y == 1)
    def _():
        near(0, z, rows - EDGE)

        @pl.when(z < plan.zs - 1)
        def _():
            near(1, z + 1, 0)

        @pl.when(z == plan.zs - 1)
        def _():
            across(1, shard + 1)

    for j in range(slots):
        low, high = max(0, (2 * j - 1) * EDGE), min(rows, (2 * j + 1) * EDGE)
        for which, (buf, table, norm_out) in enumerate(((m_buf, mt_out, mn_out), (v_buf, vt_out, vn_out))):
            values = buf[low:high, :]
            top = jnp.max(jnp.abs(values).reshape(-1, 8, LANES), axis=0)
            if j == 0:
                top = jnp.maximum(top, far[0, which])
            if j == slots - 1:
                top = jnp.maximum(top, far[1, which])
            top = jnp.max(top, keepdims=True)
            table[j] = top[0, 0]
            norm_out[low:high, :] = values / (top + 1e-06)


def on_device(grads, momentum_codes, variance_codes, momentum_scale, variance_scale, master, step):
    own_len = master.shape[0]
    slots = momentum_scale.shape[0]
    plan = Plan(own_len)
    rows, zs, groups = plan.rows, plan.zs, plan.groups
    struct = jax.ShapeDtypeStruct

    flat = grads.reshape(1, -1)
    arrived = plan.swap(half(plan, flat, 1), core=1)
    mine = half(plan, flat, 0)
    blocks = call(
        functools.partial(pair_kernel, plan), [struct((zs * rows, LANES), F32)] * groups, [mine, arrived]
    )
    arrived = [plan.swap(blocks[k], group=k) for k in range(1, groups)]
    part = call(sum_kernel, struct((zs * rows, LANES), F32), [blocks[0], *arrived])

    count = step[0].astype(F32)
    fixes = 1.0 - jnp.power(jnp.array([0.9, 0.95], F32), count)
    shape = (rows, LANES)
    state = call(
        functools.partial(state_kernel, plan),
        struct((3 * rows, LANES), F32),
        [momentum_codes.reshape(shape), variance_codes.reshape(shape), momentum_scale, variance_scale, master.reshape(shape)],
        in_specs=[VMEM, VMEM, SMEM, SMEM, VMEM],
    )
    states = [state] + [plan.swap(state, z=k) for k in range(1, zs)]
    state_mine = call(functools.partial(order_kernel, plan), struct((zs, 3 * rows, LANES), F32), states)
    state_other = plan.swap(state_mine, group=1)

    parts = [part] + [plan.swap(part, z=k) for k in range(1, zs)]
    send_rows = 8 + 3 * EDGE
    sum_mine, send = call(
        functools.partial(total_kernel, plan),
        [struct((zs * rows, LANES), F32), struct((send_rows, LANES), F32)],
        [*parts, state_mine],
    )
    sum_other = plan.swap(sum_mine, group=1)

    norm, relay = call(
        core_kernel, [struct((8, LANES), F32), struct((send_rows, LANES), F32)], [send, plan.swap(send, core=1)]
    )
    norms = [norm] + [plan.swap(relay if k % 2 else norm, group=k) for k in range(1, groups)]

    total_params = own_len * plan.devices
    own = struct((rows, LANES), F32)
    table = struct((slots,), F32)
    ins = [*norms, sum_mine, sum_other, state_mine, state_other, fixes]
    new_master, weights, update, mn, vn, mt, vt = call(
        functools.partial(main_kernel, plan, total_params),
        [own, struct((plan.reps * rows, LANES), BF16), own, own, own, table, table],
        ins,
        in_specs=[VMEM] * (len(ins) - 1) + [SMEM],
        out_specs=[VMEM] * 5 + [SMEM] * 2,
        scratch=[pltpu.VMEM(shape, F32), pltpu.VMEM(shape, F32), pltpu.VMEM((2, 2, EDGE, LANES), F32)],
    )
    return (
        new_master.reshape(-1),
        weights.reshape(-1),
        update.reshape(-1),
        mn.reshape(-1),
        vn.reshape(-1),
        mt,
        vt,
    )


def solution(mesh):
    own = P(ALL)
    in_specs = (P("shard", "rep", None), own, own, own, own, own, P())
    out_specs = (own, P("shard"), own, own, own, own, own)
    return jax.shard_map(on_device, mesh=mesh, in_specs=in_specs, out_specs=out_specs, check_vma=False)
```

time: 230 us -> 45.2 us (0.20)
  waiting for transfers between devices: 112 us -> 17.9 us
  blocking collectives: 71.4 us -> 0 us
  between operations: 16.9 us -> 1.39 us
  starting transfers between devices: 5.72 us -> 20.9 us
  other arithmetic: 12.2 us -> 0.02 us
  local copies, waits for them, and re-layouts: 9.82 us -> 2.04 us
  Pallas kernels: 0 us -> 2.82 us
    unnamed x4 -> x0, waiting for transfers between devices: 107 us -> none
    psum x1 -> x0, blocking collectives: 39.8 us -> none  [on_device(): norm_sq = lax.psum(jnp.sum(gsum * gsum), ('shard', 'rep'))]
    all_gather x1 -> x0, blocking collectives: 31.6 us -> none  [on_device(): lax.all_gather(new_master.astype(jnp.bfloat16), 'rep', axis=0, tiled=True)]
    ppermute x2 -> x16, starting transfers between devices: 5.64 us -> 20.9 us  [swap(): lax.ppermute(value, ALL, [(i, i ^ mask) for i in range(self.devices)])]
    ppermute x2 -> x16, waiting for transfers between devices: 5.64 us -> 17.9 us  [swap(): lax.ppermute(value, ALL, [(i, i ^ mask) for i in range(self.devices)])]
    another operation x5 -> x0, other arithmetic: 6.13 us -> none  [the longest x2 2.73 us: on_device(): jnp.stack([jnp.stack([m_table[0], v_table[0]]), jnp.stack([m_table[-1], v...]
    unnamed x22 -> x16, local copies, waits for them, and re-layouts: 7.1 us -> 2.04 us
    convert_element_type x2 -> x0, other arithmetic: 3.6 us -> none  [the longest x1 2.92 us: on_device(): grad_terms = grads.reshape(-1).astype(jnp.float32)]
  transfers between devices with their start and end apart: 4 -> 16, of which waited for: 4 -> 4; matrix products, arithmetic and copies ran while one was open for 1% -> 0% of each run, Pallas kernels for 0% -> 2%
where the time goes in v1:
time: 45.2 us; the launch traced here: 45 us
  starting transfers between devices  20.9 us (46%)
  waiting for transfers between devices  17.9 us (40%)
  Pallas kernels  2.82 us (6%)
  local copies, waits for them, and re-layouts  2.04 us (5%)
  between operations  1.39 us (3%)
    ppermute x16, starting transfers between devices, swap(): lax.ppermute(value, ALL, [(i, i ^ mask) for i in range(self.devices)])  20.9 us
    ppermute x16, waiting for transfers between devices, swap(): lax.ppermute(value, ALL, [(i, i ^ mask) for i in range(self.devices)])  17.9 us
    pallas_call x9, Pallas kernels, call(): pl.pallas_call(kernel, out_shape=outs, in_specs=in_specs or [VMEM] * len(...  2.82 us
    unnamed x16, local copies, waits for them, and re-layouts  2.04 us
  transfers between devices with their start and end apart: 16, of which 4 were waited for; matrix products, arithmetic and copies ran while one was open for 0% of the time, Pallas kernels for 2%

profile of v1, /device:TPU:0, one launch (start us, length us, event | category | flops | bytes accessed | tf_op | source)
XLA Modules:
  0.0 45.0 jit_solution(18051408702922066212)
XLA Ops:
  0.6 0.0 copy-start
  0.6 1.2 %copy-done = bf16[1,1,262144]{2,1,0:T(2,128)(2,1)S(1)} copy-done((bf16[1,1,262144]{2,1,0:T(2,128)(2,1)S(1)}, bf16[1,1,262144]{2,1,0:T(2,128)(2,1)}, u32[]{:S(2)}) %copy-start) | copy-done | bytes 524312
  1.9 0.0 copy-start.2
  1.9 0.0 copy-start.3
  1.9 0.0 copy-start.4
  1.9 0.0 copy-start.1
  1.9 0.2 shard_map.136
  2.1 0.5 %collective-permute-start = (bf16[1024,128]{1,0:T(8,128)(2,1)S(1)}, bf16[1024,128]{1,0:T(8,128)(2,1)S(1)}, u32[]{:S(2)}, u32[]{:S(2)}) collective-permute-start(bf16[1024,128]{1,0:T(8,128)(2,1)S(1)} %shard_map.136), channel_id=1, source_target_pairs={{0,8},{1,9},{2,10},{3,11},{4,12},{5,13},{6,14},{7,15},{8,0},{9,1},... | collective-permute-start | bytes 786440 | tf_op jit(solution)/shard_map/ppermute | solution.py:34
  2.6 0.0 copy-start.5
  2.6 0.0 copy-start.6
  2.6 0.0 copy-done.2
  2.6 0.0 copy-done.3
  2.6 0.0 copy-done.4
  2.6 0.6 %copy-done.5 = f32[5]{0:T(128)S(1)} copy-done((f32[5]{0:T(128)S(1)}, f32[5]{0:T(128)}, u32[]{:S(2)}) %copy-start.5) | copy-done | bytes 44
  3.2 0.0 copy-done.6
  3.2 0.6 %shard_map.139.refs_0_ = f32[192,128]{1,0:T(8,128)S(1)} custom-call(s32[64,128]{1,0:T(8,128)S(1)} %bitcast.12, s32[64,128]{1,0:T(8,128)S(1)} %bitcast.13, f32[5]{0:T(128)S(1)} %copy-done.5, f32[5]{0:T(128)S(1)} %copy-done.6, f32[64,128]{1,0:T(8,128)S(1)} %bitcast.14), custom_call_target="tpu_custom_call" | custom-call | tf_op jit(solution)/shard_map/pallas_call | solution.py:50
  3.8 2.7 %collective-permute-start.7 = (f32[192,128]{1,0:T(8,128)S(1)}, f32[192,128]{1,0:T(8,128)S(1)}, u32[]{:S(2)}, u32[]{:S(2)}) collective-permute-start(f32[192,128]{1,0:T(8,128)S(1)} %shard_map.139.refs_0_), channel_id=1, source_target_pairs={{0,2},{1,3},{2,0},{3,1},{4,6},{5,7},{6,4},{7,5},{8,10},{9,11},{10,... | collective-permute-start | bytes 294920 | tf_op jit(solution)/shard_map/ppermute | solution.py:34
  6.5 0.0 copy-done.1
  6.5 0.2 shard_map.135.mine_ref
  6.7 0.0 collective-permute-done.other_ref
  6.7 0.1 shard_map.137
  6.8 1.6 %collective-permute-start.1 = (f32[256,128]{1,0:T(8,128)S(1)}, f32[256,128]{1,0:T(8,128)S(1)}, u32[]{:S(2)}, u32[]{:S(2)}) collective-permute-start(f32[256,128]{1,0:T(8,128)S(1)} %get-tuple-element.23), channel_id=1, source_target_pairs={{0,1},{1,0},{2,3},{3,2},{4,5},{5,4},{6,7},{7,6},{8,9},{9,8},{10,11... | collective-permute-start | bytes 393224 | tf_op jit(solution)/shard_map/ppermute | solution.py:34
  8.4 1.5 %collective-permute-start.2 = (f32[256,128]{1,0:T(8,128)S(1)}, f32[256,128]{1,0:T(8,128)S(1)}, u32[]{:S(2)}, u32[]{:S(2)}) collective-permute-start(f32[256,128]{1,0:T(8,128)S(1)} %get-tuple-element.24), channel_id=1, source_target_pairs={{0,16},{1,17},{2,18},{3,19},{4,20},{5,21},{6,22},{7,23},{8,24},{9,... | collective-permute-start | bytes 393224 | tf_op jit(solution)/shard_map/ppermute | solution.py:34
  9.9 0.5 %collective-permute-start.3 = (f32[256,128]{1,0:T(8,128)S(1)}, f32[256,128]{1,0:T(8,128)S(1)}, u32[]{:S(2)}, u32[]{:S(2)}) collective-permute-start(f32[256,128]{1,0:T(8,128)S(1)} %get-tuple-element.25), channel_id=1, source_target_pairs={{0,17},{1,16},{2,19},{3,18},{4,21},{5,20},{6,23},{7,22},{8,25},{9,... | collective-permute-start | bytes 393224 | tf_op jit(solution)/shard_map/ppermute | solution.py:34
  10.4 2.6 %collective-permute-start.8 = (f32[192,128]{1,0:T(8,128)S(1)}, f32[192,128]{1,0:T(8,128)S(1)}, u32[]{:S(2)}, u32[]{:S(2)}) collective-permute-start(f32[192,128]{1,0:T(8,128)S(1)} %shard_map.139.refs_0_), channel_id=1, source_target_pairs={{0,4},{1,5},{2,6},{3,7},{4,0},{5,1},{6,2},{7,3},{8,12},{9,13},{10,... | collective-permute-start | bytes 294920 | tf_op jit(solution)/shard_map/ppermute | solution.py:34
  12.9 0.0 collective-permute-done.7.refs_1_
  13.0 0.7 %collective-permute-start.9 = (f32[192,128]{1,0:T(8,128)S(1)}, f32[192,128]{1,0:T(8,128)S(1)}, u32[]{:S(2)}, u32[]{:S(2)}) collective-permute-start(f32[192,128]{1,0:T(8,128)S(1)} %shard_map.139.refs_0_), channel_id=1, source_target_pairs={{0,6},{1,7},{2,4},{3,5},{4,2},{5,3},{6,0},{7,1},{8,14},{9,15},{10,... | collective-permute-start | bytes 294920 | tf_op jit(solution)/shard_map/ppermute | solution.py:34
  13.7 5.9 %collective-permute-done.8.refs_2_ = f32[192,128]{1,0:T(8,128)S(1)} collective-permute-done((f32[192,128]{1,0:T(8,128)S(1)}, f32[192,128]{1,0:T(8,128)S(1)}, u32[]{:S(2)}, u32[]{:S(2)}) %collective-permute-start.8) | collective-permute-done | bytes 98336 | tf_op jit(solution)/shard_map/ppermute | solution.py:34
  19.6 0.0 collective-permute-done.9.refs_3_
  19.7 2.1 %collective-permute-start.15 = (f32[4,192,128]{2,1,0:T(8,128)S(1)}, f32[4,192,128]{2,1,0:T(8,128)S(1)}, u32[]{:S(2)}, u32[]{:S(2)}) collective-permute-start(f32[4,192,128]{2,1,0:T(8,128)S(1)} %shard_map.140.refs_4_.refs_6_), channel_id=1, source_target_pairs={{0,1},{1,0},{2,3},{3,2},{4,5},{5,4},{6,7},{7,6},{8,9},{9,8},{10,11... | collective-permute-start | bytes 1179656 | tf_op jit(solution)/shard_map/ppermute | solution.py:34
  21.8 0.0 collective-permute-done.1.refs_1_
  21.8 0.0 collective-permute-done.2.refs_2_
  21.8 0.0 collective-permute-done.3.refs_3_
  21.8 2.0 %collective-permute-start.4 = (f32[256,128]{1,0:T(8,128)S(1)}, f32[256,128]{1,0:T(8,128)S(1)}, u32[]{:S(2)}, u32[]{:S(2)}) collective-permute-start(f32[256,128]{1,0:T(8,128)S(1)} %shard_map.138.refs_0_), channel_id=1, source_target_pairs={{0,2},{1,3},{2,0},{3,1},{4,6},{5,7},{6,4},{7,5},{8,10},{9,11},{10,... | collective-permute-start | bytes 393224 | tf_op jit(solution)/shard_map/ppermute | solution.py:34
  23.8 1.5 %collective-permute-start.5 = (f32[256,128]{1,0:T(8,128)S(1)}, f32[256,128]{1,0:T(8,128)S(1)}, u32[]{:S(2)}, u32[]{:S(2)}) collective-permute-start(f32[256,128]{1,0:T(8,128)S(1)} %shard_map.138.refs_0_), channel_id=1, source_target_pairs={{0,4},{1,5},{2,6},{3,7},{4,0},{5,1},{6,2},{7,3},{8,12},{9,13},{10,... | collective-permute-start | bytes 393224 | tf_op jit(solution)/shard_map/ppermute | solution.py:34
  25.3 1.1 %collective-permute-start.6 = (f32[256,128]{1,0:T(8,128)S(1)}, f32[256,128]{1,0:T(8,128)S(1)}, u32[]{:S(2)}, u32[]{:S(2)}) collective-permute-start(f32[256,128]{1,0:T(8,128)S(1)} %shard_map.138.refs_0_), channel_id=1, source_target_pairs={{0,6},{1,7},{2,4},{3,5},{4,2},{5,3},{6,0},{7,1},{8,14},{9,15},{10,... | collective-permute-start | bytes 393224 | tf_op jit(solution)/shard_map/ppermute | solution.py:34
  26.4 1.4 %collective-permute-done.4.refs_1_ = f32[256,128]{1,0:T(8,128)S(1)} collective-permute-done((f32[256,128]{1,0:T(8,128)S(1)}, f32[256,128]{1,0:T(8,128)S(1)}, u32[]{:S(2)}, u32[]{:S(2)}) %collective-permute-start.4) | collective-permute-done | bytes 131104 | tf_op jit(solution)/shard_map/ppermute | solution.py:34
  27.7 7.6 %collective-permute-done.5.refs_2_ = f32[256,128]{1,0:T(8,128)S(1)} collective-permute-done((f32[256,128]{1,0:T(8,128)S(1)}, f32[256,128]{1,0:T(8,128)S(1)}, u32[]{:S(2)}, u32[]{:S(2)}) %collective-permute-start.5) | collective-permute-done | bytes 131104 | tf_op jit(solution)/shard_map/ppermute | solution.py:34
  35.4 0.0 collective-permute-done.6.refs_3_
  35.4 0.1 shard_map.141
  35.4 0.1 collective-permute-start.10
  36.2 0.5 %collective-permute-start.14 = (f32[256,128]{1,0:T(8,128)S(1)}, f32[256,128]{1,0:T(8,128)S(1)}, u32[]{:S(2)}, u32[]{:S(2)}) collective-permute-start(f32[256,128]{1,0:T(8,128)S(1)} %get-tuple-element.29.refs_4_), channel_id=1, source_target_pairs={{0,1},{1,0},{2,3},{3,2},{4,5},{5,4},{6,7},{7,6},{8,9},{9,8},{10,11... | collective-permute-start | bytes 393224 | tf_op jit(solution)/shard_map/ppermute | solution.py:34
  36.7 0.0 collective-permute-done.10.other_ref
  36.7 1.5 %collective-permute-start.11 = (f32[32,128]{1,0:T(8,128)S(1)}, f32[32,128]{1,0:T(8,128)S(1)}, u32[]{:S(2)}, u32[]{:S(2)}) collective-permute-start(f32[32,128]{1,0:T(8,128)S(1)} %get-tuple-element.28), channel_id=1, source_target_pairs={{0,1},{1,0},{2,3},{3,2},{4,5},{5,4},{6,7},{7,6},{8,9},{9,8},{10,11... | collective-permute-start | bytes 49160 | tf_op jit(solution)/shard_map/ppermute | solution.py:34
  38.3 1.4 %collective-permute-start.13 = (f32[32,128]{1,0:T(8,128)S(1)}, f32[32,128]{1,0:T(8,128)S(1)}, u32[]{:S(2)}, u32[]{:S(2)}) collective-permute-start(f32[32,128]{1,0:T(8,128)S(1)} %get-tuple-element.28), channel_id=1, source_target_pairs={{0,17},{1,16},{2,19},{3,18},{4,21},{5,20},{6,23},{7,22},{8,25},{9,... | collective-permute-start | bytes 49160 | tf_op jit(solution)/shard_map/ppermute | solution.py:34
  39.7 0.0 copy-start.7
  39.7 0.5 %collective-permute-start.12 = (f32[8,128]{1,0:T(8,128)S(1)}, f32[8,128]{1,0:T(8,128)S(1)}, u32[]{:S(2)}, u32[]{:S(2)}) collective-permute-start(f32[8,128]{1,0:T(8,128)S(1)} %get-tuple-element.27.refs_0_), channel_id=1, source_target_pairs={{0,16},{1,17},{2,18},{3,19},{4,20},{5,21},{6,22},{7,23},{8,24},{9,... | collective-permute-start | bytes 12296 | tf_op jit(solution)/shard_map/ppermute | solution.py:34
  40.2 0.1 copy-done.7
  40.4 0.0 collective-permute-done.15.refs_7_
  40.4 2.9 %collective-permute-done.12.refs_2_ = f32[8,128]{1,0:T(8,128)S(1)} collective-permute-done((f32[8,128]{1,0:T(8,128)S(1)}, f32[8,128]{1,0:T(8,128)S(1)}, u32[]{:S(2)}, u32[]{:S(2)}) %collective-permute-start.12) | collective-permute-done | bytes 4128 | tf_op jit(solution)/shard_map/ppermute | solution.py:34
  43.3 0.0 collective-permute-done.11.refs_1_
  43.3 0.0 collective-permute-done.13.refs_3_
  43.3 0.0 collective-permute-done.14.refs_5_
  43.3 1.7 %shard_map.143 = (f32[64,128]{1,0:T(8,128)}, bf16[512,128]{1,0:T(8,128)(2,1)}, f32[64,128]{1,0:T(8,128)}, f32[64,128]{1,0:T(8,128)}, f32[64,128]{1,0:T(8,128)}, /*index=5*/f32[5]{0:T(128)}, f32[5]{0:T(128)}) custom-call(f32[8,128]{1,0:T(8,128)S(1)} %get-tuple-element.27.refs_0_, f32[32,128]{1,0:T(8,128)S(1)} %collective-permute-done.11.refs_1_, ...), custom_call_target="tpu_custom_call" | custom-call | tf_op jit(solution)/shard_map/pallas_call | solution.py:50
  (4 shorter events, 0.1 us)
Async XLA Ops:
  0.6 1.2 %copy-start = (bf16[1,1,262144]{2,1,0:T(2,128)(2,1)S(1)}, bf16[1,1,262144]{2,1,0:T(2,128)(2,1)}, u32[]{:S(2)}) copy-start(bf16[1,1,262144]{2,1,0:T(2,128)(2,1)} %param.8) | copy-start | bytes 1572868
  1.9 0.8 %copy-start.2 = (s32[8192]{0:T(1024)S(1)}, s32[8192]{0:T(1024)}, u32[]{:S(2)}) copy-start(s32[8192]{0:T(1024)} %param.9) | copy-start | bytes 98308
  1.9 0.8 %copy-start.3 = (s32[8192]{0:T(1024)S(1)}, s32[8192]{0:T(1024)}, u32[]{:S(2)}) copy-start(s32[8192]{0:T(1024)} %param.10) | copy-start | bytes 98308
  1.9 0.8 %copy-start.4 = (f32[8192]{0:T(1024)S(1)}, f32[8192]{0:T(1024)}, u32[]{:S(2)}) copy-start(f32[8192]{0:T(1024)} %param.13) | copy-start | bytes 98308
  1.9 4.7 %copy-start.1 = (bf16[1,1,262144]{2,1,0:T(2,128)(2,1)S(1)}, bf16[1,1,262144]{2,1,0:T(2,128)(2,1)}, u32[]{:S(2)}) copy-start(bf16[1,1,262144]{2,1,0:T(2,128)(2,1)} %param.8) | copy-start | bytes 1572868
  2.1 4.7 %collective-permute-start = (bf16[1024,128]{1,0:T(8,128)(2,1)S(1)}, bf16[1024,128]{1,0:T(8,128)(2,1)S(1)}, u32[]{:S(2)}, u32[]{:S(2)}) collective-permute-start(bf16[1024,128]{1,0:T(8,128)(2,1)S(1)} %shard_map.136), channel_id=1, source_target_pairs={{0,8},{1,9},{2,10},{3,11},{4,12},{5,13},{6,14},{7,15},{8,0},{9,1},... | collective-permute-start | bytes 786440 | tf_op jit(solution)/shard_map/ppermute | solution.py:34
  2.6 0.7 %copy-start.5 = (f32[5]{0:T(128)S(1)}, f32[5]{0:T(128)}, u32[]{:S(2)}) copy-start(f32[5]{0:T(128)} %ms_ref.1) | copy-start | bytes 64
  2.6 0.7 %copy-start.6 = (f32[5]{0:T(128)S(1)}, f32[5]{0:T(128)}, u32[]{:S(2)}) copy-start(f32[5]{0:T(128)} %vs_ref.1) | copy-start | bytes 64
  3.8 9.1 %collective-permute-start.7 = (f32[192,128]{1,0:T(8,128)S(1)}, f32[192,128]{1,0:T(8,128)S(1)}, u32[]{:S(2)}, u32[]{:S(2)}) collective-permute-start(f32[192,128]{1,0:T(8,128)S(1)} %shard_map.139.refs_0_), channel_id=1, source_target_pairs={{0,2},{1,3},{2,0},{3,1},{4,6},{5,7},{6,4},{7,5},{8,10},{9,11},{10,... | collective-permute-start | bytes 294920 | tf_op jit(solution)/shard_map/ppermute | solution.py:34
  6.8 15.0 %collective-permute-start.1 = (f32[256,128]{1,0:T(8,128)S(1)}, f32[256,128]{1,0:T(8,128)S(1)}, u32[]{:S(2)}, u32[]{:S(2)}) collective-permute-start(f32[256,128]{1,0:T(8,128)S(1)} %get-tuple-element.23), channel_id=1, source_target_pairs={{0,1},{1,0},{2,3},{3,2},{4,5},{5,4},{6,7},{7,6},{8,9},{9,8},{10,11... | collective-permute-start | bytes 393224 | tf_op jit(solution)/shard_map/ppermute | solution.py:34
  8.4 13.4 %collective-permute-start.2 = (f32[256,128]{1,0:T(8,128)S(1)}, f32[256,128]{1,0:T(8,128)S(1)}, u32[]{:S(2)}, u32[]{:S(2)}) collective-permute-start(f32[256,128]{1,0:T(8,128)S(1)} %get-tuple-element.24), channel_id=1, source_target_pairs={{0,16},{1,17},{2,18},{3,19},{4,20},{5,21},{6,22},{7,23},{8,24},{9,... | collective-permute-start | bytes 393224 | tf_op jit(solution)/shard_map/ppermute | solution.py:34
  9.9 11.9 %collective-permute-start.3 = (f32[256,128]{1,0:T(8,128)S(1)}, f32[256,128]{1,0:T(8,128)S(1)}, u32[]{:S(2)}, u32[]{:S(2)}) collective-permute-start(f32[256,128]{1,0:T(8,128)S(1)} %get-tuple-element.25), channel_id=1, source_target_pairs={{0,17},{1,16},{2,19},{3,18},{4,21},{5,20},{6,23},{7,22},{8,25},{9,... | collective-permute-start | bytes 393224 | tf_op jit(solution)/shard_map/ppermute | solution.py:34
  10.4 9.3 %collective-permute-start.8 = (f32[192,128]{1,0:T(8,128)S(1)}, f32[192,128]{1,0:T(8,128)S(1)}, u32[]{:S(2)}, u32[]{:S(2)}) collective-permute-start(f32[192,128]{1,0:T(8,128)S(1)} %shard_map.139.refs_0_), channel_id=1, source_target_pairs={{0,4},{1,5},{2,6},{3,7},{4,0},{5,1},{6,2},{7,3},{8,12},{9,13},{10,... | collective-permute-start | bytes 294920 | tf_op jit(solution)/shard_map/ppermute | solution.py:34
  13.0 6.7 %collective-permute-start.9 = (f32[192,128]{1,0:T(8,128)S(1)}, f32[192,128]{1,0:T(8,128)S(1)}, u32[]{:S(2)}, u32[]{:S(2)}) collective-permute-start(f32[192,128]{1,0:T(8,128)S(1)} %shard_map.139.refs_0_), channel_id=1, source_target_pairs={{0,6},{1,7},{2,4},{3,5},{4,2},{5,3},{6,0},{7,1},{8,14},{9,15},{10,... | collective-permute-start | bytes 294920 | tf_op jit(solution)/shard_map/ppermute | solution.py:34
  19.7 20.7 %collective-permute-start.15 = (f32[4,192,128]{2,1,0:T(8,128)S(1)}, f32[4,192,128]{2,1,0:T(8,128)S(1)}, u32[]{:S(2)}, u32[]{:S(2)}) collective-permute-start(f32[4,192,128]{2,1,0:T(8,128)S(1)} %shard_map.140.refs_4_.refs_6_), channel_id=1, source_target_pairs={{0,1},{1,0},{2,3},{3,2},{4,5},{5,4},{6,7},{7,6},{8,9},{9,8},{10,11... | collective-permute-start | bytes 1179656 | tf_op jit(solution)/shard_map/ppermute | solution.py:34
  21.8 5.9 %collective-permute-start.4 = (f32[256,128]{1,0:T(8,128)S(1)}, f32[256,128]{1,0:T(8,128)S(1)}, u32[]{:S(2)}, u32[]{:S(2)}) collective-permute-start(f32[256,128]{1,0:T(8,128)S(1)} %shard_map.138.refs_0_), channel_id=1, source_target_pairs={{0,2},{1,3},{2,0},{3,1},{4,6},{5,7},{6,4},{7,5},{8,10},{9,11},{10,... | collective-permute-start | bytes 393224 | tf_op jit(solution)/shard_map/ppermute | solution.py:34
  23.8 11.6 %collective-permute-start.5 = (f32[256,128]{1,0:T(8,128)S(1)}, f32[256,128]{1,0:T(8,128)S(1)}, u32[]{:S(2)}, u32[]{:S(2)}) collective-permute-start(f32[256,128]{1,0:T(8,128)S(1)} %shard_map.138.refs_0_), channel_id=1, source_target_pairs={{0,4},{1,5},{2,6},{3,7},{4,0},{5,1},{6,2},{7,3},{8,12},{9,13},{10,... | collective-permute-start | bytes 393224 | tf_op jit(solution)/shard_map/ppermute | solution.py:34
  25.3 10.1 %collective-permute-start.6 = (f32[256,128]{1,0:T(8,128)S(1)}, f32[256,128]{1,0:T(8,128)S(1)}, u32[]{:S(2)}, u32[]{:S(2)}) collective-permute-start(f32[256,128]{1,0:T(8,128)S(1)} %shard_map.138.refs_0_), channel_id=1, source_target_pairs={{0,6},{1,7},{2,4},{3,5},{4,2},{5,3},{6,0},{7,1},{8,14},{9,15},{10,... | collective-permute-start | bytes 393224 | tf_op jit(solution)/shard_map/ppermute | solution.py:34
  35.4 1.3 %collective-permute-start.10 = (f32[32,128]{1,0:T(8,128)S(1)}, f32[32,128]{1,0:T(8,128)S(1)}, u32[]{:S(2)}, u32[]{:S(2)}) collective-permute-start(f32[32,128]{1,0:T(8,128)S(1)} %get-tuple-element.26.mine_ref), channel_id=1, source_target_pairs={{0,8},{1,9},{2,10},{3,11},{4,12},{5,13},{6,14},{7,15},{8,0},{9,1},... | collective-permute-start | bytes 49160 | tf_op jit(solution)/shard_map/ppermute | solution.py:34
  36.2 7.2 %collective-permute-start.14 = (f32[256,128]{1,0:T(8,128)S(1)}, f32[256,128]{1,0:T(8,128)S(1)}, u32[]{:S(2)}, u32[]{:S(2)}) collective-permute-start(f32[256,128]{1,0:T(8,128)S(1)} %get-tuple-element.29.refs_4_), channel_id=1, source_target_pairs={{0,1},{1,0},{2,3},{3,2},{4,5},{5,4},{6,7},{7,6},{8,9},{9,8},{10,11... | collective-permute-start | bytes 393224 | tf_op jit(solution)/shard_map/ppermute | solution.py:34
  36.7 6.6 %collective-permute-start.11 = (f32[32,128]{1,0:T(8,128)S(1)}, f32[32,128]{1,0:T(8,128)S(1)}, u32[]{:S(2)}, u32[]{:S(2)}) collective-permute-start(f32[32,128]{1,0:T(8,128)S(1)} %get-tuple-element.28), channel_id=1, source_target_pairs={{0,1},{1,0},{2,3},{3,2},{4,5},{5,4},{6,7},{7,6},{8,9},{9,8},{10,11... | collective-permute-start | bytes 49160 | tf_op jit(solution)/shard_map/ppermute | solution.py:34
  38.3 5.0 %collective-permute-start.13 = (f32[32,128]{1,0:T(8,128)S(1)}, f32[32,128]{1,0:T(8,128)S(1)}, u32[]{:S(2)}, u32[]{:S(2)}) collective-permute-start(f32[32,128]{1,0:T(8,128)S(1)} %get-tuple-element.28), channel_id=1, source_target_pairs={{0,17},{1,16},{2,19},{3,18},{4,21},{5,20},{6,23},{7,22},{8,25},{9,... | collective-permute-start | bytes 49160 | tf_op jit(solution)/shard_map/ppermute | solution.py:34
  39.7 0.7 %copy-start.7 = (f32[2]{0:T(128)S(1)}, f32[2]{0:T(128)}, u32[]{:S(2)}) copy-start(f32[2]{0:T(128)} %constant.4.clone) | copy-start | bytes 28
  39.7 3.6 %collective-permute-start.12 = (f32[8,128]{1,0:T(8,128)S(1)}, f32[8,128]{1,0:T(8,128)S(1)}, u32[]{:S(2)}, u32[]{:S(2)}) collective-permute-start(f32[8,128]{1,0:T(8,128)S(1)} %get-tuple-element.27.refs_0_), channel_id=1, source_target_pairs={{0,16},{1,17},{2,18},{3,19},{4,20},{5,21},{6,22},{7,23},{8,24},{9,... | collective-permute-start | bytes 12296 | tf_op jit(solution)/shard_map/ppermute | solution.py:34

commit v2 on v1

--- a/solution.py
+++ b/solution.py
@@ -16,6 +16,7 @@
 VMEM = pl.BlockSpec(memory_space=pltpu.VMEM)
 SMEM = pl.BlockSpec(memory_space=pltpu.SMEM)
 ANY = pl.BlockSpec(memory_space=pl.ANY)
+HBM = pl.BlockSpec(memory_space=pltpu.HBM)
 
 
 class Plan:
@@ -77,7 +78,7 @@
         functools.partial(half_kernel, flip, plan.xs, length),
         jax.ShapeDtypeStruct((plan.xs * length // LANES, LANES), BF16),
         [grads],
-        in_specs=[ANY],
+        in_specs=[HBM],
         scratch=[pltpu.VMEM((plan.xs, 1, length), BF16), pltpu.SemaphoreType.DMA((plan.xs,))],
     )
 
@@ -96,22 +97,39 @@
     refs[-1][...] = tree([r[...] for r in refs[:-1]])
 
 
-def state_kernel(plan, mc_ref, vc_ref, ms_ref, vs_ref, master_ref, o_ref):
-    slots = ms_ref.shape[0]
+def state_rows(plan, slots):
+    return 2 * plan.rows + -(-2 * slots // 8) * 8
+
+
+def state_kernel(plan, mc_ref, vc_ref, ms_ref, vs_ref, master_ref, _, o_ref):
+    rows, slots = plan.rows, ms_ref.shape[0]
+    o_ref[0:rows, :] = vc_ref[...].astype(F32) * 256.0 + (mc_ref[...].astype(F32) + 128.0)
+    o_ref[rows : 2 * rows, :] = master_ref[...]
     for j in range(slots):
-        low, high = max(0, (2 * j - 1) * EDGE), min(plan.rows, (2 * j + 1) * EDGE)
-        o_ref[low:high, :] = mc_ref[low:high, :].astype(F32) / 127.0 * ms_ref[j]
-        o_ref[plan.rows + low : plan.rows + high, :] = vc_ref[low:high, :].astype(F32) / 255.0 * vs_ref[j]
-    o_ref[2 * plan.rows :, :] = master_ref[...]
+        o_ref[2 * rows + j : 2 * rows + j + 1, :] = jnp.full((1, LANES), ms_ref[j], F32)
+        o_ref[2 * rows + slots + j : 2 * rows + slots + j + 1, :] = jnp.full((1, LANES), vs_ref[j], F32)
+
+
+def old_moments(plan, state, slots, low, high):
+    slot = (low + EDGE) // (2 * EDGE)
+    m_at, v_at = 2 * plan.rows + slot, 2 * plan.rows + slots + slot
+    pair = state[low:high, :]
+    v_code = jnp.floor(pair * (1.0 / 256.0))
+    m_code = pair - v_code * 256.0 - 128.0
+    return m_code / 127.0 * state[m_at : m_at + 1, :], v_code / 255.0 * state[v_at : v_at + 1, :]
+
+
+def pieces(plan, slots):
+    return [(max(0, (2 * j - 1) * EDGE), min(plan.rows, (2 * j + 1) * EDGE)) for j in range(slots)]
 
 
 def order_kernel(plan, *refs):
     _, _, z, _ = place()
-    for k, ref in enumerate(refs[:-1]):
+    for k, ref in enumerate(refs[2:-1]):
         refs[-1][z ^ k] = ref[...]
 
 
-def total_kernel(plan, *refs):
+def total_kernel(plan, slots, *refs):
     parts, (state_ref, sum_ref, send_ref) = refs[: plan.zs], refs[plan.zs :]
     _, _, _, y = place()
     total = tree([r[...] for r in parts])
@@ -120,9 +138,9 @@
 
     def edge(z, start):
         send_ref[8 : 8 + EDGE, :] = sum_ref[z * plan.rows + start : z * plan.rows + start + EDGE, :]
+        old = old_moments(plan, state_ref.at[z], slots, start, start + EDGE)
         for k in range(2):
-            at = k * plan.rows + start
-            send_ref[8 + (k + 1) * EDGE : 8 + (k + 2) * EDGE, :] = state_ref[z, at : at + EDGE, :]
+            send_ref[8 + (k + 1) * EDGE : 8 + (k + 2) * EDGE, :] = old[k]
 
     @pl.when(y == 0)
     def _():
@@ -133,18 +151,22 @@
         edge(plan.zs - 1, plan.rows - EDGE)
 
 
-def core_kernel(mine_ref, other_ref, norm_ref, relay_ref):
+def core_kernel(mine_ref, other_ref, sum_ref, norm_ref, relay_ref, wide_ref):
     norm = mine_ref[0:8, :] + other_ref[0:8, :]
     norm_ref[...] = norm
-    relay_ref[0:8, :] = norm
-    relay_ref[8:, :] = other_ref[8:, :]
+    size = relay_ref.shape[0]
+    for ref in (relay_ref, wide_ref):
+        ref[0:8, :] = norm
+        ref[8:size, :] = other_ref[8:, :]
+    wide_ref[size:, :] = sum_ref[...]
 
 
 def main_kernel(plan, total_params, *refs):
     norms, refs = refs[: plan.groups], refs[plan.groups :]
-    (sum_mine, sum_other, state_mine, state_other, fix_ref) = refs[:5]
-    (master_out, weights_out, update_out, mn_out, vn_out, mt_out, vt_out) = refs[5:12]
-    m_buf, v_buf, far = refs[12:]
+    (sum_mine, state_mine, state_other, fix_ref) = refs[:4]
+    (master_out, weights_out, update_out, mn_out, vn_out, mt_out, vt_out) = refs[4:11]
+    m_buf, v_buf, far = refs[11:]
+    sum_other = norms[1].at[pl.ds(8 + 3 * EDGE, plan.zs * plan.rows)]
     x, core, z, y = place()
     rows = plan.rows
     slots = mt_out.shape[0]
@@ -156,31 +178,32 @@
         scaled = grad * clip
         return 0.9 * m_old + 0.1 * scaled, 0.95 * v_old + 0.05 * scaled * scaled
 
-    def step(grad, state):
-        m, v = moments(grad, state[0:rows], state[rows : 2 * rows])
+    def step(grads, state, low, high):
+        m, v = moments(grads[low:high, :], *old_moments(plan, state, slots, low, high))
         update = m / first_fix / (jnp.sqrt(v / second_fix) + 1e-08)
-        return m, v, update, state[2 * rows :] * (1.0 - 0.0001 * 0.1) - 0.0001 * update
+        master = state[rows + low : rows + high, :]
+        return m, v, update, master * (1.0 - 0.0001 * 0.1) - 0.0001 * update
 
     for k in range(plan.zs):
-        at = pl.ds(k * rows, rows)
         for flip, (sums, states) in enumerate(((sum_mine, state_mine), (sum_other, state_other))):
-            out = step(sums[at, :], states[k])[3]
             start = pl.multiple_of((2 * k + (y ^ flip)) * rows, rows)
+            grads = sums.at[pl.ds(k * rows, rows)]
+            out = jnp.concatenate([step(grads, states.at[k], *piece)[3] for piece in pieces(plan, slots)], axis=0)
             weights_out[pl.ds(start, rows), :] = out.astype(BF16)
 
-    m, v, update, master = step(sum_mine[pl.ds(pl.multiple_of(z * rows, rows), rows), :], state_mine[z])
-    update_out[...] = update
-    master_out[...] = master
-    m_buf[...] = m
-    v_buf[...] = v
+    grads = sum_mine.at[pl.ds(pl.multiple_of(z * rows, rows), rows)]
+    for low, high in pieces(plan, slots):
+        m, v, update, master = step(grads, state_mine.at[z], low, high)
+        update_out[low:high, :] = update
+        master_out[low:high, :] = master
+        m_buf[low:high, :] = m
+        v_buf[low:high, :] = v
 
     far[...] = jnp.zeros_like(far)
 
     def near(side, at_z, start):
         grad = sum_other[pl.ds(pl.multiple_of(at_z * rows + start, EDGE), EDGE), :]
-        low = state_other[at_z, start : start + EDGE, :]
-        high = state_other[at_z, rows + start : rows + start + EDGE, :]
-        em, ev = moments(grad, low, high)
+        em, ev = moments(grad, *old_moments(plan, state_other.at[at_z], slots, start, start + EDGE))
         far[side, 0], far[side, 1] = jnp.abs(em), jnp.abs(ev)
 
     def across(side, shard):
@@ -216,8 +239,7 @@
         def _():
             across(1, shard + 1)
 
-    for j in range(slots):
-        low, high = max(0, (2 * j - 1) * EDGE), min(rows, (2 * j + 1) * EDGE)
+    for j, (low, high) in enumerate(pieces(plan, slots)):
         for which, (buf, table, norm_out) in enumerate(((m_buf, mt_out, mn_out), (v_buf, vt_out, vn_out))):
             values = buf[low:high, :]
             top = jnp.max(jnp.abs(values).reshape(-1, 8, LANES), axis=0)
@@ -251,32 +273,38 @@
     shape = (rows, LANES)
     state = call(
         functools.partial(state_kernel, plan),
-        struct((3 * rows, LANES), F32),
-        [momentum_codes.reshape(shape), variance_codes.reshape(shape), momentum_scale, variance_scale, master.reshape(shape)],
-        in_specs=[VMEM, VMEM, SMEM, SMEM, VMEM],
+        struct((state_rows(plan, slots), LANES), F32),
+        [momentum_codes.reshape(shape), variance_codes.reshape(shape), momentum_scale, variance_scale, master.reshape(shape), blocks[0]],
+        in_specs=[VMEM, VMEM, SMEM, SMEM, VMEM, ANY],
     )
     states = [state] + [plan.swap(state, z=k) for k in range(1, zs)]
-    state_mine = call(functools.partial(order_kernel, plan), struct((zs, 3 * rows, LANES), F32), states)
+
+    parts = [part] + [plan.swap(part, z=k) for k in range(1, zs)]
+    state_mine = call(
+        functools.partial(order_kernel, plan),
+        struct((zs, state_rows(plan, slots), LANES), F32),
+        [parts[1], fixes, *states],
+        [ANY, SMEM] + [VMEM] * zs,
+    )
     state_other = plan.swap(state_mine, group=1)
-
-    parts = [part] + [plan.swap(part, z=k) for k in range(1, zs)]
     send_rows = 8 + 3 * EDGE
     sum_mine, send = call(
-        functools.partial(total_kernel, plan),
+        functools.partial(total_kernel, plan, slots),
         [struct((zs * rows, LANES), F32), struct((send_rows, LANES), F32)],
         [*parts, state_mine],
     )
-    sum_other = plan.swap(sum_mine, group=1)
-
-    norm, relay = call(
-        core_kernel, [struct((8, LANES), F32), struct((send_rows, LANES), F32)], [send, plan.swap(send, core=1)]
-    )
-    norms = [norm] + [plan.swap(relay if k % 2 else norm, group=k) for k in range(1, groups)]
+    norm, relay, wide = call(
+        core_kernel,
+        [struct((8, LANES), F32), struct((send_rows, LANES), F32), struct((send_rows + zs * rows, LANES), F32)],
+        [send, plan.swap(send, core=1), sum_mine],
+    )
+    wide = plan.swap(wide, group=1)
+    norms = [norm, wide] + [plan.swap(relay if k % 2 else norm, group=k) for k in range(2, groups)]
 
     total_params = own_len * plan.devices
     own = struct((rows, LANES), F32)
     table = struct((slots,), F32)
-    ins = [*norms, sum_mine, sum_other, state_mine, state_other, fixes]
+    ins = [*norms, sum_mine, state_mine, state_other, fixes]
     new_master, weights, update, mn, vn, mt, vt = call(
         functools.partial(main_kernel, plan, total_params),
         [own, struct((plan.reps * rows, LANES), BF16), own, own, own, table, table],

time: 45.2 us -> 40.4 us (0.89)
  waiting for transfers between devices: 17.9 us -> 14.2 us
  starting transfers between devices: 20.9 us -> 19.4 us
  Pallas kernels: 2.82 us -> 3.34 us
    ppermute x16 -> x15, waiting for transfers between devices: 17.9 us -> 14.2 us  [swap(): lax.ppermute(value, ALL, [(i, i ^ mask) for i in range(self.devices)])]
    ppermute x16 -> x15, starting transfers between devices: 20.9 us -> 19.4 us  [swap(): lax.ppermute(value, ALL, [(i, i ^ mask) for i in range(self.devices)])]
    pallas_call x9, Pallas kernels: 2.82 us -> 3.34 us  [call(): pl.pallas_call(kernel, out_shape=outs, in_specs=in_specs or [VMEM] * len(...]
    unnamed x16 -> x14, local copies, waits for them, and re-layouts: 2.04 us -> 1.89 us
  transfers between devices with their start and end apart: 16 -> 15, of which waited for: 4 -> 6; matrix products, arithmetic and copies ran while one was open for 0% -> 0% of each run, Pallas kernels for 2% -> 3%
where the time goes in v2:
time: 40.4 us; the launch traced here: 40.3 us
  starting transfers between devices  19.4 us (48%)
  waiting for transfers between devices  14.2 us (35%)
  Pallas kernels  3.34 us (8%)
  local copies, waits for them, and re-layouts  1.89 us (5%)
  between operations  1.41 us (3%)
    ppermute x15, starting transfers between devices, swap(): lax.ppermute(value, ALL, [(i, i ^ mask) for i in range(self.devices)])  19.4 us
    ppermute x15, waiting for transfers between devices, swap(): lax.ppermute(value, ALL, [(i, i ^ mask) for i in range(self.devices)])  14.2 us
    pallas_call x9, Pallas kernels, call(): pl.pallas_call(kernel, out_shape=outs, in_specs=in_specs or [VMEM] * len(...  3.34 us
    unnamed x14, local copies, waits for them, and re-layouts  1.89 us
  transfers between devices with their start and end apart: 15, of which 6 were waited for; matrix products, arithmetic and copies ran while one was open for 0% of the time, Pallas kernels for 3%

profile of v2, /device:TPU:0, one launch (start us, length us, event | category | flops | bytes accessed | tf_op | source)
XLA Modules:
  0.0 40.3 jit_solution(7585952903523432010)
XLA Ops:
  0.6 0.0 copy-start
  0.6 1.2 %copy-done = bf16[1,1,262144]{2,1,0:T(2,128)(2,1)S(1)} copy-done((bf16[1,1,262144]{2,1,0:T(2,128)(2,1)S(1)}, bf16[1,1,262144]{2,1,0:T(2,128)(2,1)}, u32[]{:S(2)}) %copy-start) | copy-done | bytes 524312
  1.9 0.2 shard_map.136
  2.0 0.5 %collective-permute-start = (bf16[1024,128]{1,0:T(8,128)(2,1)S(1)}, bf16[1024,128]{1,0:T(8,128)(2,1)S(1)}, u32[]{:S(2)}, u32[]{:S(2)}) collective-permute-start(bf16[1024,128]{1,0:T(8,128)(2,1)S(1)} %shard_map.136), channel_id=1, source_target_pairs={{0,8},{1,9},{2,10},{3,11},{4,12},{5,13},{6,14},{7,15},{8,0},{9,1},... | collective-permute-start | bytes 786440 | tf_op jit(solution)/shard_map/ppermute | solution.py:35
  2.5 0.2 shard_map.135.mine_ref
  2.7 1.0 %collective-permute-done.other_ref = bf16[1024,128]{1,0:T(8,128)(2,1)S(1)} collective-permute-done((bf16[1024,128]{1,0:T(8,128)(2,1)S(1)}, bf16[1024,128]{1,0:T(8,128)(2,1)S(1)}, u32[]{:S(2)}, u32[]{:S(2)}) %collective-permute-start) | collective-permute-done | bytes 262176 | tf_op jit(solution)/shard_map/ppermute | solution.py:35
  3.7 0.0 copy-start.1
  3.7 0.0 copy-start.2
  3.7 0.0 copy-start.3
  3.7 0.1 shard_map.137
  3.8 3.0 %collective-permute-start.1 = (f32[256,128]{1,0:T(8,128)S(1)}, f32[256,128]{1,0:T(8,128)S(1)}, u32[]{:S(2)}, u32[]{:S(2)}) collective-permute-start(f32[256,128]{1,0:T(8,128)S(1)} %get-tuple-element.24), channel_id=1, source_target_pairs={{0,1},{1,0},{2,3},{3,2},{4,5},{5,4},{6,7},{7,6},{8,9},{9,8},{10,11... | collective-permute-start | bytes 393224 | tf_op jit(solution)/shard_map/ppermute | solution.py:35
  6.7 1.5 %collective-permute-start.2 = (f32[256,128]{1,0:T(8,128)S(1)}, f32[256,128]{1,0:T(8,128)S(1)}, u32[]{:S(2)}, u32[]{:S(2)}) collective-permute-start(f32[256,128]{1,0:T(8,128)S(1)} %get-tuple-element.25), channel_id=1, source_target_pairs={{0,16},{1,17},{2,18},{3,19},{4,20},{5,21},{6,22},{7,23},{8,24},{9,... | collective-permute-start | bytes 393224 | tf_op jit(solution)/shard_map/ppermute | solution.py:35
  8.2 0.0 collective-permute-start.3
  8.3 0.0 copy-start.4
  8.3 0.0 copy-start.5
  8.3 0.0 copy-done.1
  8.3 0.0 copy-done.2
  8.3 0.0 copy-done.3
  8.3 0.6 %copy-done.4 = f32[5]{0:T(128)S(1)} copy-done((f32[5]{0:T(128)S(1)}, f32[5]{0:T(128)}, u32[]{:S(2)}) %copy-start.4) | copy-done | bytes 44
  8.9 0.0 copy-done.5
  8.9 0.6 %shard_map.139.refs_2_ = f32[144,128]{1,0:T(8,128)S(1)} custom-call(s32[64,128]{1,0:T(8,128)S(1)} %bitcast.12, s32[64,128]{1,0:T(8,128)S(1)} %bitcast.13, f32[5]{0:T(128)S(1)} %copy-done.4, f32[5]{0:T(128)S(1)} %copy-done.5, f32[64,128]{1,0:T(8,128)S(1)} %bitcast.14, f32[256,128]{1,0:T(8,128)S(1)} %get-tuple-element.23.refs_0_._), custom_call_target="tpu_custom_call" | custom-call | tf_op jit(solution)/shard_map/pallas_call | solution.py:51
  9.5 4.1 %collective-permute-start.9 = (f32[144,128]{1,0:T(8,128)S(1)}, f32[144,128]{1,0:T(8,128)S(1)}, u32[]{:S(2)}, u32[]{:S(2)}) collective-permute-start(f32[144,128]{1,0:T(8,128)S(1)} %shard_map.139.refs_2_), channel_id=1, source_target_pairs={{0,6},{1,7},{2,4},{3,5},{4,2},{5,3},{6,0},{7,1},{8,14},{9,15},{10,... | collective-permute-start | bytes 221192 | tf_op jit(solution)/shard_map/ppermute | solution.py:35
  14.2 0.1 collective-permute-start.8
  14.3 0.0 collective-permute-done.1.refs_1_
  14.3 0.6 %collective-permute-start.7 = (f32[144,128]{1,0:T(8,128)S(1)}, f32[144,128]{1,0:T(8,128)S(1)}, u32[]{:S(2)}, u32[]{:S(2)}) collective-permute-start(f32[144,128]{1,0:T(8,128)S(1)} %shard_map.139.refs_2_), channel_id=1, source_target_pairs={{0,2},{1,3},{2,0},{3,1},{4,6},{5,7},{6,4},{7,5},{8,10},{9,11},{10,... | collective-permute-start | bytes 221192 | tf_op jit(solution)/shard_map/ppermute | solution.py:35
  14.9 0.0 collective-permute-done.2.refs_2_
  14.9 0.0 collective-permute-done.3.refs_3_
  14.9 0.0 copy-start.6
  14.9 3.9 %collective-permute-start.6 = (f32[256,128]{1,0:T(8,128)S(1)}, f32[256,128]{1,0:T(8,128)S(1)}, u32[]{:S(2)}, u32[]{:S(2)}) collective-permute-start(f32[256,128]{1,0:T(8,128)S(1)} %shard_map.138.refs_0_), channel_id=1, source_target_pairs={{0,6},{1,7},{2,4},{3,5},{4,2},{5,3},{6,0},{7,1},{8,14},{9,15},{10,... | collective-permute-start | bytes 393224 | tf_op jit(solution)/shard_map/ppermute | solution.py:35
  18.8 0.0 collective-permute-start.5
  18.8 0.0 collective-permute-done.9.refs_5_
  18.8 0.6 %collective-permute-start.4 = (f32[256,128]{1,0:T(8,128)S(1)}, f32[256,128]{1,0:T(8,128)S(1)}, u32[]{:S(2)}, u32[]{:S(2)}) collective-permute-start(f32[256,128]{1,0:T(8,128)S(1)} %shard_map.138.refs_0_), channel_id=1, source_target_pairs={{0,2},{1,3},{2,0},{3,1},{4,6},{5,7},{6,4},{7,5},{8,10},{9,11},{10,... | collective-permute-start | bytes 393224 | tf_op jit(solution)/shard_map/ppermute | solution.py:35
  19.5 0.0 copy-done.6
  19.5 5.3 %collective-permute-done.8.refs_4_ = f32[144,128]{1,0:T(8,128)S(1)} collective-permute-done((f32[144,128]{1,0:T(8,128)S(1)}, f32[144,128]{1,0:T(8,128)S(1)}, u32[]{:S(2)}, u32[]{:S(2)}) %collective-permute-start.8) | collective-permute-done | bytes 73760 | tf_op jit(solution)/shard_map/ppermute | solution.py:35
  24.7 0.0 collective-permute-done.7.refs_3_
  24.7 1.6 %collective-permute-done.4.refs_0_.refs_1_ = f32[256,128]{1,0:T(8,128)S(1)} collective-permute-done((f32[256,128]{1,0:T(8,128)S(1)}, f32[256,128]{1,0:T(8,128)S(1)}, u32[]{:S(2)}, u32[]{:S(2)}) %collective-permute-start.4) | collective-permute-done | bytes 131104 | tf_op jit(solution)/shard_map/ppermute | solution.py:35
  26.3 0.6 %shard_map.140.refs_4_.refs_5_ = f32[4,144,128]{2,1,0:T(8,128)S(1)} custom-call(f32[256,128]{1,0:T(8,128)S(1)} %collective-permute-done.4.refs_0_.refs_1_, f32[2]{0:T(128)S(1)} %power_subtract_fusion.refs_1_.refs_7_, f32[144,128]{1,0:T(8,128)S(1)} %shard_map.139.refs_2_, f32[144,128]{1,0:T(8,128)S(1)} %collective-permute-done.7.refs_3_, ...), custom_call_target="tpu_custom_call" | custom-call | tf_op jit(solution)/shard_map/pallas_call | solution.py:51
  26.9 1.5 %collective-permute-start.14 = (f32[4,144,128]{2,1,0:T(8,128)S(1)}, f32[4,144,128]{2,1,0:T(8,128)S(1)}, u32[]{:S(2)}, u32[]{:S(2)}) collective-permute-start(f32[4,144,128]{2,1,0:T(8,128)S(1)} %shard_map.140.refs_4_.refs_5_), channel_id=1, source_target_pairs={{0,1},{1,0},{2,3},{3,2},{4,5},{5,4},{6,7},{7,6},{8,9},{9,8},{10,11... | collective-permute-start | bytes 884744 | tf_op jit(solution)/shard_map/ppermute | solution.py:35
  28.4 0.0 collective-permute-done.6.refs_3_
  28.4 2.1 %collective-permute-done.5.refs_2_ = f32[256,128]{1,0:T(8,128)S(1)} collective-permute-done((f32[256,128]{1,0:T(8,128)S(1)}, f32[256,128]{1,0:T(8,128)S(1)}, u32[]{:S(2)}, u32[]{:S(2)}) %collective-permute-start.5) | collective-permute-done | bytes 131104 | tf_op jit(solution)/shard_map/ppermute | solution.py:35
  30.6 0.1 collective-permute-start.10
  30.7 1.2 %collective-permute-done.10.other_ref = f32[32,128]{1,0:T(8,128)S(1)} collective-permute-done((f32[32,128]{1,0:T(8,128)S(1)}, f32[32,128]{1,0:T(8,128)S(1)}, u32[]{:S(2)}, u32[]{:S(2)}) %collective-permute-start.10) | collective-permute-done | bytes 16416 | tf_op jit(solution)/shard_map/ppermute | solution.py:35
  31.9 1.6 %collective-permute-start.11 = (f32[288,128]{1,0:T(8,128)S(1)}, f32[288,128]{1,0:T(8,128)S(1)}, u32[]{:S(2)}, u32[]{:S(2)}) collective-permute-start(f32[288,128]{1,0:T(8,128)S(1)} %get-tuple-element.30), channel_id=1, source_target_pairs={{0,1},{1,0},{2,3},{3,2},{4,5},{5,4},{6,7},{7,6},{8,9},{9,8},{10,11... | collective-permute-start | bytes 442376 | tf_op jit(solution)/shard_map/ppermute | solution.py:35
  33.4 1.4 %collective-permute-start.13 = (f32[32,128]{1,0:T(8,128)S(1)}, f32[32,128]{1,0:T(8,128)S(1)}, u32[]{:S(2)}, u32[]{:S(2)}) collective-permute-start(f32[32,128]{1,0:T(8,128)S(1)} %get-tuple-element.31), channel_id=1, source_target_pairs={{0,17},{1,16},{2,19},{3,18},{4,21},{5,20},{6,23},{7,22},{8,25},{9,... | collective-permute-start | bytes 49160 | tf_op jit(solution)/shard_map/ppermute | solution.py:35
  34.9 0.6 %collective-permute-start.12 = (f32[8,128]{1,0:T(8,128)S(1)}, f32[8,128]{1,0:T(8,128)S(1)}, u32[]{:S(2)}, u32[]{:S(2)}) collective-permute-start(f32[8,128]{1,0:T(8,128)S(1)} %get-tuple-element.29.refs_0_), channel_id=1, source_target_pairs={{0,16},{1,17},{2,18},{3,19},{4,20},{5,21},{6,22},{7,23},{8,24},{9,... | collective-permute-start | bytes 12296 | tf_op jit(solution)/shard_map/ppermute | solution.py:35
  35.4 3.0 %collective-permute-done.12.refs_2_ = f32[8,128]{1,0:T(8,128)S(1)} collective-permute-done((f32[8,128]{1,0:T(8,128)S(1)}, f32[8,128]{1,0:T(8,128)S(1)}, u32[]{:S(2)}, u32[]{:S(2)}) %collective-permute-start.12) | collective-permute-done | bytes 4128 | tf_op jit(solution)/shard_map/ppermute | solution.py:35
  38.5 0.0 collective-permute-done.13.refs_3_
  38.5 0.0 collective-permute-done.11.refs_1_
  38.5 0.0 collective-permute-done.14.refs_6_
  38.5 1.8 %shard_map.143 = (f32[64,128]{1,0:T(8,128)}, bf16[512,128]{1,0:T(8,128)(2,1)}, f32[64,128]{1,0:T(8,128)}, f32[64,128]{1,0:T(8,128)}, f32[64,128]{1,0:T(8,128)}, /*index=5*/f32[5]{0:T(128)}, f32[5]{0:T(128)}) custom-call(f32[8,128]{1,0:T(8,128)S(1)} %get-tuple-element.29.refs_0_, f32[288,128]{1,0:T(8,128)S(1)} %collective-permute-done.11.refs_1_, ...), custom_call_target="tpu_custom_call" | custom-call | tf_op jit(solution)/shard_map/pallas_call | solution.py:51
  (4 shorter events, 0.1 us)
Async XLA Ops:
  0.6 1.2 %copy-start = (bf16[1,1,262144]{2,1,0:T(2,128)(2,1)S(1)}, bf16[1,1,262144]{2,1,0:T(2,128)(2,1)}, u32[]{:S(2)}) copy-start(bf16[1,1,262144]{2,1,0:T(2,128)(2,1)} %param.8) | copy-start | bytes 1572868
  2.0 1.7 %collective-permute-start = (bf16[1024,128]{1,0:T(8,128)(2,1)S(1)}, bf16[1024,128]{1,0:T(8,128)(2,1)S(1)}, u32[]{:S(2)}, u32[]{:S(2)}) collective-permute-start(bf16[1024,128]{1,0:T(8,128)(2,1)S(1)} %shard_map.136), channel_id=1, source_target_pairs={{0,8},{1,9},{2,10},{3,11},{4,12},{5,13},{6,14},{7,15},{8,0},{9,1},... | collective-permute-start | bytes 786440 | tf_op jit(solution)/shard_map/ppermute | solution.py:35
  3.7 4.6 %copy-start.1 = (s32[8192]{0:T(1024)S(1)}, s32[8192]{0:T(1024)}, u32[]{:S(2)}) copy-start(s32[8192]{0:T(1024)} %param.9) | copy-start | bytes 98308
  3.7 4.6 %copy-start.2 = (s32[8192]{0:T(1024)S(1)}, s32[8192]{0:T(1024)}, u32[]{:S(2)}) copy-start(s32[8192]{0:T(1024)} %param.10) | copy-start | bytes 98308
  3.7 4.6 %copy-start.3 = (f32[8192]{0:T(1024)S(1)}, f32[8192]{0:T(1024)}, u32[]{:S(2)}) copy-start(f32[8192]{0:T(1024)} %param.13) | copy-start | bytes 98308
  3.8 10.6 %collective-permute-start.1 = (f32[256,128]{1,0:T(8,128)S(1)}, f32[256,128]{1,0:T(8,128)S(1)}, u32[]{:S(2)}, u32[]{:S(2)}) collective-permute-start(f32[256,128]{1,0:T(8,128)S(1)} %get-tuple-element.24), channel_id=1, source_target_pairs={{0,1},{1,0},{2,3},{3,2},{4,5},{5,4},{6,7},{7,6},{8,9},{9,8},{10,11... | collective-permute-start | bytes 393224 | tf_op jit(solution)/shard_map/ppermute | solution.py:35
  6.7 8.2 %collective-permute-start.2 = (f32[256,128]{1,0:T(8,128)S(1)}, f32[256,128]{1,0:T(8,128)S(1)}, u32[]{:S(2)}, u32[]{:S(2)}) collective-permute-start(f32[256,128]{1,0:T(8,128)S(1)} %get-tuple-element.25), channel_id=1, source_target_pairs={{0,16},{1,17},{2,18},{3,19},{4,20},{5,21},{6,22},{7,23},{8,24},{9,... | collective-permute-start | bytes 393224 | tf_op jit(solution)/shard_map/ppermute | solution.py:35
  8.2 6.7 %collective-permute-start.3 = (f32[256,128]{1,0:T(8,128)S(1)}, f32[256,128]{1,0:T(8,128)S(1)}, u32[]{:S(2)}, u32[]{:S(2)}) collective-permute-start(f32[256,128]{1,0:T(8,128)S(1)} %get-tuple-element.26), channel_id=1, source_target_pairs={{0,17},{1,16},{2,19},{3,18},{4,21},{5,20},{6,23},{7,22},{8,25},{9,... | collective-permute-start | bytes 393224 | tf_op jit(solution)/shard_map/ppermute | solution.py:35
  8.3 0.7 %copy-start.4 = (f32[5]{0:T(128)S(1)}, f32[5]{0:T(128)}, u32[]{:S(2)}) copy-start(f32[5]{0:T(128)} %ms_ref.1) | copy-start | bytes 64
  8.3 0.7 %copy-start.5 = (f32[5]{0:T(128)S(1)}, f32[5]{0:T(128)}, u32[]{:S(2)}) copy-start(f32[5]{0:T(128)} %vs_ref.1) | copy-start | bytes 64
  9.5 9.3 %collective-permute-start.9 = (f32[144,128]{1,0:T(8,128)S(1)}, f32[144,128]{1,0:T(8,128)S(1)}, u32[]{:S(2)}, u32[]{:S(2)}) collective-permute-start(f32[144,128]{1,0:T(8,128)S(1)} %shard_map.139.refs_2_), channel_id=1, source_target_pairs={{0,6},{1,7},{2,4},{3,5},{4,2},{5,3},{6,0},{7,1},{8,14},{9,15},{10,... | collective-permute-start | bytes 221192 | tf_op jit(solution)/shard_map/ppermute | solution.py:35
  14.2 10.5 %collective-permute-start.8 = (f32[144,128]{1,0:T(8,128)S(1)}, f32[144,128]{1,0:T(8,128)S(1)}, u32[]{:S(2)}, u32[]{:S(2)}) collective-permute-start(f32[144,128]{1,0:T(8,128)S(1)} %shard_map.139.refs_2_), channel_id=1, source_target_pairs={{0,4},{1,5},{2,6},{3,7},{4,0},{5,1},{6,2},{7,3},{8,12},{9,13},{10,... | collective-permute-start | bytes 221192 | tf_op jit(solution)/shard_map/ppermute | solution.py:35
  14.3 10.4 %collective-permute-start.7 = (f32[144,128]{1,0:T(8,128)S(1)}, f32[144,128]{1,0:T(8,128)S(1)}, u32[]{:S(2)}, u32[]{:S(2)}) collective-permute-start(f32[144,128]{1,0:T(8,128)S(1)} %shard_map.139.refs_2_), channel_id=1, source_target_pairs={{0,2},{1,3},{2,0},{3,1},{4,6},{5,7},{6,4},{7,5},{8,10},{9,11},{10,... | collective-permute-start | bytes 221192 | tf_op jit(solution)/shard_map/ppermute | solution.py:35
  14.9 4.5 %copy-start.6 = (f32[2]{0:T(128)S(1)}, f32[2]{0:T(128)}, u32[]{:S(2)}) copy-start(f32[2]{0:T(128)} %constant.4.clone) | copy-start | bytes 28
  14.9 13.5 %collective-permute-start.6 = (f32[256,128]{1,0:T(8,128)S(1)}, f32[256,128]{1,0:T(8,128)S(1)}, u32[]{:S(2)}, u32[]{:S(2)}) collective-permute-start(f32[256,128]{1,0:T(8,128)S(1)} %shard_map.138.refs_0_), channel_id=1, source_target_pairs={{0,6},{1,7},{2,4},{3,5},{4,2},{5,3},{6,0},{7,1},{8,14},{9,15},{10,... | collective-permute-start | bytes 393224 | tf_op jit(solution)/shard_map/ppermute | solution.py:35
  18.8 11.8 %collective-permute-start.5 = (f32[256,128]{1,0:T(8,128)S(1)}, f32[256,128]{1,0:T(8,128)S(1)}, u32[]{:S(2)}, u32[]{:S(2)}) collective-permute-start(f32[256,128]{1,0:T(8,128)S(1)} %shard_map.138.refs_0_), channel_id=1, source_target_pairs={{0,4},{1,5},{2,6},{3,7},{4,0},{5,1},{6,2},{7,3},{8,12},{9,13},{10,... | collective-permute-start | bytes 393224 | tf_op jit(solution)/shard_map/ppermute | solution.py:35
  18.8 7.5 %collective-permute-start.4 = (f32[256,128]{1,0:T(8,128)S(1)}, f32[256,128]{1,0:T(8,128)S(1)}, u32[]{:S(2)}, u32[]{:S(2)}) collective-permute-start(f32[256,128]{1,0:T(8,128)S(1)} %shard_map.138.refs_0_), channel_id=1, source_target_pairs={{0,2},{1,3},{2,0},{3,1},{4,6},{5,7},{6,4},{7,5},{8,10},{9,11},{10,... | collective-permute-start | bytes 393224 | tf_op jit(solution)/shard_map/ppermute | solution.py:35
  26.9 11.6 %collective-permute-start.14 = (f32[4,144,128]{2,1,0:T(8,128)S(1)}, f32[4,144,128]{2,1,0:T(8,128)S(1)}, u32[]{:S(2)}, u32[]{:S(2)}) collective-permute-start(f32[4,144,128]{2,1,0:T(8,128)S(1)} %shard_map.140.refs_4_.refs_5_), channel_id=1, source_target_pairs={{0,1},{1,0},{2,3},{3,2},{4,5},{5,4},{6,7},{7,6},{8,9},{9,8},{10,11... | collective-permute-start | bytes 884744 | tf_op jit(solution)/shard_map/ppermute | solution.py:35
  30.6 1.2 %collective-permute-start.10 = (f32[32,128]{1,0:T(8,128)S(1)}, f32[32,128]{1,0:T(8,128)S(1)}, u32[]{:S(2)}, u32[]{:S(2)}) collective-permute-start(f32[32,128]{1,0:T(8,128)S(1)} %get-tuple-element.27.mine_ref), channel_id=1, source_target_pairs={{0,8},{1,9},{2,10},{3,11},{4,12},{5,13},{6,14},{7,15},{8,0},{9,1},... | collective-permute-start | bytes 49160 | tf_op jit(solution)/shard_map/ppermute | solution.py:35
  31.9 6.6 %collective-permute-start.11 = (f32[288,128]{1,0:T(8,128)S(1)}, f32[288,128]{1,0:T(8,128)S(1)}, u32[]{:S(2)}, u32[]{:S(2)}) collective-permute-start(f32[288,128]{1,0:T(8,128)S(1)} %get-tuple-element.30), channel_id=1, source_target_pairs={{0,1},{1,0},{2,3},{3,2},{4,5},{5,4},{6,7},{7,6},{8,9},{9,8},{10,11... | collective-permute-start | bytes 442376 | tf_op jit(solution)/shard_map/ppermute | solution.py:35
  33.4 5.0 %collective-permute-start.13 = (f32[32,128]{1,0:T(8,128)S(1)}, f32[32,128]{1,0:T(8,128)S(1)}, u32[]{:S(2)}, u32[]{:S(2)}) collective-permute-start(f32[32,128]{1,0:T(8,128)S(1)} %get-tuple-element.31), channel_id=1, source_target_pairs={{0,17},{1,16},{2,19},{3,18},{4,21},{5,20},{6,23},{7,22},{8,25},{9,... | collective-permute-start | bytes 49160 | tf_op jit(solution)/shard_map/ppermute | solution.py:35
  34.9 3.6 %collective-permute-start.12 = (f32[8,128]{1,0:T(8,128)S(1)}, f32[8,128]{1,0:T(8,128)S(1)}, u32[]{:S(2)}, u32[]{:S(2)}) collective-permute-start(f32[8,128]{1,0:T(8,128)S(1)} %get-tuple-element.29.refs_0_), channel_id=1, source_target_pairs={{0,16},{1,17},{2,18},{3,19},{4,20},{5,21},{6,22},{7,23},{8,24},{9,... | collective-permute-start | bytes 12296 | tf_op jit(solution)/shard_map/ppermute | solution.py:35

commit v3 on v2

v3 whole, which is shorter than its diff:
```python
import functools

import jax
import jax.numpy as jnp
from jax import lax
from jax.experimental import pallas as pl
from jax.experimental.pallas import tpu as pltpu
from jax.sharding import PartitionSpec as P

BLOCK = 2048
LANES = 128
EDGE = BLOCK // 2 // LANES
ALL = ("shard", "rep")
BF16 = jnp.bfloat16
F32 = jnp.float32
VMEM = pl.BlockSpec(memory_space=pltpu.VMEM)
SMEM = pl.BlockSpec(memory_space=pltpu.SMEM)
ANY = pl.BlockSpec(memory_space=pl.ANY)
HBM = pl.BlockSpec(memory_space=pltpu.HBM)


class Plan:
    def __init__(self, own_len):
        self.shards = lax.axis_size("shard")
        self.reps = lax.axis_size("rep")
        self.devices = self.shards * self.reps
        self.xs = self.shards // 2
        self.zs = self.reps // 2
        self.groups = self.xs * 2
        self.rows = own_len // LANES

    def swap(self, value, core=0, z=0, group=0):
        x, y = group >> 1, group & 1
        mask = ((x << 1) | core) * self.reps + ((z << 1) | y)
        return lax.ppermute(value, ALL, [(i, i ^ mask) for i in range(self.devices)])


def place():
    shard, rep = lax.axis_index("shard"), lax.axis_index("rep")
    return shard // 2, shard % 2, rep // 2, rep % 2


def tree(values):
    values = list(values)
    while len(values) > 1:
        values = [a + b for a, b in zip(values[::2], values[1::2])]
    return values[0]


def call(kernel, outs, ins, in_specs=None, out_specs=None, scratch=(), limit=16):
    limit = int(limit * 1024 * 1024)
    return pl.pallas_call(
        kernel,
        out_shape=outs,
        in_specs=in_specs or [VMEM] * len(ins),
        out_specs=out_specs or jax.tree.map(lambda _: VMEM, outs),
        scratch_shapes=list(scratch),
        compiler_params=pltpu.CompilerParams(vmem_limit_bytes=limit),
    )(*ins)


def half_kernel(flip, count, length, x_ref, o_ref, buf, sem):
    _, core, _, _ = place()
    want = (core + flip) % 2
    rows = length // LANES
    copies = []
    for k in range(count):
        start = pl.multiple_of((2 * k + want) * length, length)
        copies.append(pltpu.make_async_copy(x_ref.at[:, pl.ds(start, length)], buf.at[k], sem.at[k]))
        copies[-1].start()
    for k in range(count):
        copies[k].wait()
        o_ref[pl.ds(k * rows, rows), :] = buf[k].astype(F32).reshape(rows, LANES).astype(BF16)


def half_call(plan, kernel, outs, ins):
    length = plan.reps * plan.rows * LANES
    return call(
        kernel,
        [jax.ShapeDtypeStruct((plan.xs * length // LANES, LANES), BF16), *outs],
        ins,
        in_specs=[ANY] * len(ins),
        scratch=[
            pltpu.VMEM((plan.xs, 1, length), BF16),
            pltpu.SemaphoreType.DMA((plan.xs,)),
            *(pltpu.VMEM(x.shape, x.dtype) for x in ins[1:]),
            *([pltpu.SemaphoreType.DMA((len(ins) - 1,))] if ins[1:] else []),
        ],
        limit=53.25,
    )


def own_kernel(plan, x_ref, o_ref, buf, sem):
    half_kernel(0, plan.xs, plan.reps * plan.rows * LANES, x_ref, o_ref, buf, sem)


def other_kernel(plan, x_ref, o_ref, buf, sem):
    half_kernel(1, plan.xs, plan.reps * plan.rows * LANES, x_ref, o_ref, buf, sem)


def pair_kernel(plan, mine_ref, other_ref, *outs):
    x, _, _, y = place()
    for k, out in enumerate(outs):
        to_x, to_y = x ^ (k >> 1), y ^ (k & 1)
        for z in range(plan.zs):
            start = pl.multiple_of((to_x * plan.reps + 2 * z + to_y) * plan.rows, plan.rows)
            rows = pl.ds(start, plan.rows)
            out[pl.ds(z * plan.rows, plan.rows), :] = mine_ref[rows, :].astype(F32) + other_ref[rows, :].astype(F32)


def part_kernel(*refs):
    *terms, low_ref, high_ref = refs
    half = low_ref.shape[0]
    low_ref[...] = tree([r[:half, :] for r in terms])
    high_ref[...] = tree([r[half:, :] for r in terms])


def two_kernel(low_ref, low_other, high_ref, high_other, low_out, high_out):
    low_out[...] = low_ref[...] + low_other[...]
    high_out[...] = high_ref[...] + high_other[...]


def state_rows(plan, slots):
    return 2 * plan.rows + scale_rows(slots)


def scale_rows(slots):
    return -(-(slots + 2) // 8) * 8


def power(base, count):
    value, square = jnp.ones(count.shape, F32), jnp.full(count.shape, base, F32)
    for bit in range(8):
        value = jnp.where((count >> bit) & 1 == 1, value * square, value)
        square = square * square
    return value


def state_kernel(plan, mc_ref, vc_ref, ms_ref, vs_ref, master_ref, _, o_ref):
    o_ref = o_ref.at[0]
    rows, slots = plan.rows, ms_ref.shape[1]
    o_ref[0:rows, :] = vc_ref[...].astype(F32) * 256.0 + (mc_ref[...].astype(F32) + 128.0)
    o_ref[rows : 2 * rows, :] = master_ref[...]
    lane = lax.broadcasted_iota(jnp.int32, (1, LANES), 1)
    for j in range(slots):
        scales = jnp.where(lane < LANES // 2, ms_ref[:, j : j + 1], vs_ref[:, j : j + 1])
        o_ref[2 * rows + j : 2 * rows + j + 1, :] = scales


def old_moments(state, scales, low, high):
    slot = (low + EDGE) // (2 * EDGE)
    scale = scales[slot : slot + 1, :]
    pair = state[low:high, :]
    v_code = jnp.floor(pair * (1.0 / 256.0))
    m_code = pair - v_code * 256.0 - 128.0
    return m_code / 127.0 * scale[:, 0:1], v_code / 255.0 * scale[:, LANES // 2 : LANES // 2 + 1]


def pieces(plan, slots):
    return [(max(0, (2 * j - 1) * EDGE), min(plan.rows, (2 * j + 1) * EDGE)) for j in range(slots)]


def order_kernel(plan, slots, step_ref, _, *refs):
    *states, o_ref, send_ref = refs
    _, _, z, _ = place()
    for k, ref in enumerate(states):
        o_ref[z ^ k] = ref[0]
        send_ref[z ^ k] = ref[0, : send_ref.shape[1], :]
    count = jnp.broadcast_to(step_ref[...], (1, LANES))
    for j, base in enumerate((0.9, 0.95)):
        at = 2 * plan.rows + slots + j
        for i in range(plan.zs):
            o_ref[i, at : at + 1, :] = 1.0 - power(base, count)


def squares(values):
    return jnp.sum((values * values).reshape(-1, 8, LANES), axis=0)


def total_kernel(plan, *refs):
    low_ref, low_other, high_ref, high_other, state_ref, sum_ref, send_ref = refs
    _, _, _, y = place()
    half = low_ref.shape[0]
    low, high = low_ref[...] + low_other[...], high_ref[...] + high_other[...]
    sum_ref[:half, :] = low
    sum_ref[half:, :] = high
    send_ref[0:8, :] = squares(low) + squares(high)

    def edge(z, start):
        send_ref[8 : 8 + EDGE, :] = sum_ref[z * plan.rows + start : z * plan.rows + start + EDGE, :]
        state = state_ref.at[z]
        old = old_moments(state, state.at[2 * plan.rows :], start, start + EDGE)
        for k in range(2):
            send_ref[8 + (k + 1) * EDGE : 8 + (k + 2) * EDGE, :] = old[k]

    @pl.when(y == 0)
    def _():
        edge(0, 0)

    @pl.when(y == 1)
    def _():
        edge(plan.zs - 1, plan.rows - EDGE)


def core_kernel(plan, mine_ref, other_ref, sum_ref, state_ref, norm_ref, relay_ref, wide_ref):
    norm = mine_ref[0:8, :] + other_ref[0:8, :]
    norm_ref[...] = norm
    size = relay_ref.shape[0]
    for ref in (relay_ref, wide_ref):
        ref[0:8, :] = norm
        ref[8:size, :] = other_ref[8:, :]
    end = size + sum_ref.shape[0]
    wide_ref[size:end, :] = sum_ref[...]
    scales = state_ref.shape[1] - 2 * plan.rows
    for z in range(plan.zs):
        wide_ref[end + z * scales : end + (z + 1) * scales, :] = state_ref[z, 2 * plan.rows :, :]


def main_kernel(plan, total_params, *refs):
    norms, refs = refs[: plan.groups], refs[plan.groups :]
    (sum_mine, state_mine, state_other) = refs[:3]
    (master_out, weights_out, update_out, mn_out, vn_out, mt_out, vt_out) = refs[3:10]
    m_buf, v_buf, far = refs[10:]
    sums_at, scales_at = 8 + 3 * EDGE, 8 + 3 * EDGE + plan.zs * plan.rows
    sum_other = norms[1].at[sums_at:scales_at]
    x, core, z, y = place()
    rows = plan.rows
    slots = mt_out.shape[0]
    norm_sq = jnp.sum(tree([r[0:8, :] for r in norms]), keepdims=True)
    clip = jnp.minimum(1.0, float(total_params) ** 0.5 / (jnp.sqrt(norm_sq) + 1e-06))
    def scales_mine(k):
        return state_mine.at[k, 2 * rows :]

    def scales_other(k):
        size = scale_rows(slots)
        return norms[1].at[pl.ds(scales_at + k * size, size)]

    at = 2 * rows + slots
    first_fix, second_fix = state_mine[0, at : at + 1, :], state_mine[0, at + 1 : at + 2, :]

    def moments(grad, m_old, v_old):
        scaled = grad * clip
        return 0.9 * m_old + 0.1 * scaled, 0.95 * v_old + 0.05 * scaled * scaled

    def step(grads, state, scales, low, high):
        m, v = moments(grads[low:high, :], *old_moments(state, scales, low, high))
        update = m / first_fix / (jnp.sqrt(v / second_fix) + 1e-08)
        master = state[rows + low : rows + high, :]
        return m, v, update, master * (1.0 - 0.0001 * 0.1) - 0.0001 * update

    for k in range(plan.zs):
        sides = ((sum_mine, state_mine, scales_mine), (sum_other, state_other, scales_other))
        for flip, (sums, states, scales) in enumerate(sides):
            start = pl.multiple_of((2 * k + (y ^ flip)) * rows, rows)
            grads = sums.at[pl.ds(k * rows, rows)]
            out = jnp.concatenate([step(grads, states.at[k], scales(k), *piece)[3] for piece in pieces(plan, slots)], axis=0)
            weights_out[pl.ds(start, rows), :] = out.astype(BF16)

    grads = sum_mine.at[pl.ds(pl.multiple_of(z * rows, rows), rows)]
    for low, high in pieces(plan, slots):
        m, v, update, master = step(grads, state_mine.at[z], scales_mine(z), low, high)
        update_out[low:high, :] = update
        master_out[low:high, :] = master
        m_buf[low:high, :] = m
        v_buf[low:high, :] = v

    far[...] = jnp.zeros_like(far)

    def near(side, at_z, start):
        grad = sum_other[pl.ds(pl.multiple_of(at_z * rows + start, EDGE), EDGE), :]
        em, ev = moments(grad, *old_moments(state_other.at[at_z], scales_other(at_z), start, start + EDGE))
        far[side, 0], far[side, 1] = jnp.abs(em), jnp.abs(ev)

    def across(side, shard):
        for k in range(1, plan.groups, 2):
            @pl.when((shard >= 0) & (shard < plan.shards) & ((x ^ (k >> 1)) == shard // 2))
            def _():
                em, ev = moments(*(norms[k][8 + j * EDGE : 8 + (j + 1) * EDGE, :] for j in range(3)))
                far[side, 0], far[side, 1] = jnp.abs(em), jnp.abs(ev)

    shard = 2 * x + core

    @pl.when(y == 0)
    def _():
        near(1, z, 0)

        @pl.when(z > 0)
        def _():
            near(0, z - 1, rows - EDGE)

        @pl.when(z == 0)
        def _():
            across(0, shard - 1)

    @pl.when(y == 1)
    def _():
        near(0, z, rows - EDGE)

        @pl.when(z < plan.zs - 1)
        def _():
            near(1, z + 1, 0)

        @pl.when(z == plan.zs - 1)
        def _():
            across(1, shard + 1)

    for j, (low, high) in enumerate(pieces(plan, slots)):
        for which, (buf, table, norm_out) in enumerate(((m_buf, mt_out, mn_out), (v_buf, vt_out, vn_out))):
            values = buf[low:high, :]
            top = jnp.max(jnp.abs(values).reshape(-1, 8, LANES), axis=0)
            if j == 0:
                top = jnp.maximum(top, far[0, which])
            if j == slots - 1:
                top = jnp.maximum(top, far[1, which])
            top = jnp.max(top, keepdims=True)
            table[j] = top[0, 0]
            norm_out[low:high, :] = values / (top + 1e-06)


def on_device(grads, momentum_codes, variance_codes, momentum_scale, variance_scale, master, step):
    own_len = master.shape[0]
    slots = momentum_scale.shape[0]
    plan = Plan(own_len)
    rows, zs, groups = plan.rows, plan.zs, plan.groups
    struct = jax.ShapeDtypeStruct

    shape = (rows, LANES)
    state_shape = (state_rows(plan, slots), LANES)
    part_shape = struct((zs * rows, LANES), F32)
    half_shape = struct((zs * rows // 2, LANES), F32)

    flat = grads.reshape(1, -1)
    (send,) = half_call(plan, functools.partial(other_kernel, plan), [], [flat])
    arrived = plan.swap(send, core=1)
    (mine,) = half_call(plan, functools.partial(own_kernel, plan), [], [flat])
    blocks = call(functools.partial(pair_kernel, plan), [part_shape] * groups, [mine, arrived])

    sums = [plan.swap(blocks[k], group=k) for k in range(1, groups)]

    low, high = call(part_kernel, [half_shape] * 2, [blocks[0], *sums])

    states = call(
        functools.partial(state_kernel, plan),
        struct((1, *state_shape), F32),
        [
            momentum_codes.reshape(shape),
            variance_codes.reshape(shape),
            momentum_scale.reshape(1, slots),
            variance_scale.reshape(1, slots),
            master.reshape(shape),
            blocks[0],
        ],
        [VMEM] * 5 + [ANY],
    )
    near = [states] + [plan.swap(states, z=k) for k in range(1, zs)]

    gate = low
    bits = (zs - 1).bit_length()
    for bit in range(bits):
        high_other = plan.swap(high, z=1 << (bits - 1 - bit))
        low_other = plan.swap(low, z=1 << bit)
        if bit < bits - 1:
            low, high = call(two_kernel, [half_shape] * 2, [low, low_other, high, high_other])
    state_mine, state_send = call(
        functools.partial(order_kernel, plan, slots),
        [struct((zs, *state_shape), F32), struct((zs, 2 * rows, LANES), F32)],
        [step.reshape(1, 1), gate, *near],
        [VMEM, ANY] + [VMEM] * zs,
    )
    state_other = plan.swap(state_send, group=1)
    send_rows = 8 + 3 * EDGE
    sum_mine, send = call(
        functools.partial(total_kernel, plan),
        [part_shape, struct((send_rows, LANES), F32)],
        [low, low_other, high, high_other, state_mine],
    )

    wide_rows = send_rows + zs * (rows + scale_rows(slots))
    norm, relay, wide = call(
        functools.partial(core_kernel, plan),
        [struct((n, LANES), F32) for n in (8, send_rows, wide_rows)],
        [send, plan.swap(send, core=1), sum_mine, state_mine],
    )
    wide = plan.swap(wide, group=1)
    norms = [norm, wide] + [plan.swap(relay if k % 2 else norm, group=k) for k in range(2, groups)]

    total_params = own_len * plan.devices
    own = struct((rows, LANES), F32)
    table = struct((slots,), F32)
    ins = [*norms, sum_mine, state_mine, state_other]
    new_master, weights, update, mn, vn, mt, vt = call(
        functools.partial(main_kernel, plan, total_params),
        [own, struct((plan.reps * rows, LANES), BF16), own, own, own, table, table],
        ins,
        out_specs=[VMEM] * 5 + [SMEM] * 2,
        scratch=[pltpu.VMEM(shape, F32), pltpu.VMEM(shape, F32), pltpu.VMEM((2, 2, EDGE, LANES), F32)],
    )
    return (
        new_master.reshape(-1),
        weights.reshape(-1),
        update.reshape(-1),
        mn.reshape(-1),
        vn.reshape(-1),
        mt,
        vt,
    )


def solution(mesh):
    own = P(ALL)
    in_specs = (P("shard", "rep", None), own, own, own, own, own, P())
    out_specs = (own, P("shard"), own, own, own, own, own)
    return jax.shard_map(on_device, mesh=mesh, in_specs=in_specs, out_specs=out_specs, check_vma=False)
```

time: 40.4 us -> 37 us (0.916)
  waiting for transfers between devices: 14.2 us -> 8.37 us
  starting transfers between devices: 19.4 us -> 22.5 us
  local copies, waits for them, and re-layouts: 1.89 us -> 0.66 us
  Pallas kernels: 3.34 us -> 3.95 us
    ppermute x15 -> x16, waiting for transfers between devices: 14.2 us -> 8.37 us  [swap(): lax.ppermute(value, ALL, [(i, i ^ mask) for i in range(self.devices)])]
    ppermute x15 -> x16, starting transfers between devices: 19.4 us -> 22.5 us  [swap(): lax.ppermute(value, ALL, [(i, i ^ mask) for i in range(self.devices)])]
    unnamed x14 -> x10, local copies, waits for them, and re-layouts: 1.89 us -> 0.66 us
    pallas_call x9 -> x10, Pallas kernels: 3.34 us -> 3.95 us  [call(): pl.pallas_call(kernel, out_shape=outs, in_specs=in_specs or [VMEM] * len(...]
  transfers between devices with their start and end apart: 15 -> 16, of which waited for: 6 -> 7; matrix products, arithmetic and copies ran while one was open for 0% -> 0% of each run, Pallas kernels for 3% -> 4%
where the time goes in v3:
time: 37 us; the launch traced here: 36.9 us
  starting transfers between devices  22.5 us (61%)
  waiting for transfers between devices  8.37 us (23%)
  Pallas kernels  3.95 us (11%)
  between operations  1.38 us (4%)
  local copies, waits for them, and re-layouts  0.66 us (2%)
    ppermute x16, starting transfers between devices, swap(): lax.ppermute(value, ALL, [(i, i ^ mask) for i in range(self.devices)])  22.5 us
    ppermute x16, waiting for transfers between devices, swap(): lax.ppermute(value, ALL, [(i, i ^ mask) for i in range(self.devices)])  8.37 us
    pallas_call x10, Pallas kernels, call(): pl.pallas_call(kernel, out_shape=outs, in_specs=in_specs or [VMEM] * len(...  3.95 us
  transfers between devices with their start and end apart: 16, of which 7 were waited for; matrix products, arithmetic and copies ran while one was open for 0% of the time, Pallas kernels for 4%

profile of v3, /device:TPU:0, one launch (start us, length us, event | category | flops | bytes accessed | tf_op | source)
XLA Modules:
  0.0 36.9 jit_solution(10542485213320378550)
XLA Ops:
  0.6 1.1 %shard_map.127 = bf16[1024,128]{1,0:T(8,128)(2,1)S(1)} custom-call(bf16[1,262144]{1,0:T(2,128)(2,1)} %bitcast.18), custom_call_target="tpu_custom_call" | custom-call | tf_op jit(solution)/shard_map/pallas_call | solution.py:52
  1.8 0.5 %collective-permute-start = (bf16[1024,128]{1,0:T(8,128)(2,1)S(1)}, bf16[1024,128]{1,0:T(8,128)(2,1)S(1)}, u32[]{:S(2)}, u32[]{:S(2)}) collective-permute-start(bf16[1024,128]{1,0:T(8,128)(2,1)S(1)} %shard_map.127), channel_id=1, source_target_pairs={{0,8},{1,9},{2,10},{3,11},{4,12},{5,13},{6,14},{7,15},{8,0},{9,1},... | collective-permute-start | bytes 786440 | tf_op jit(solution)/shard_map/ppermute | solution.py:35
  2.3 1.1 %shard_map.126.mine_ref = bf16[1024,128]{1,0:T(8,128)(2,1)S(1)} custom-call(bf16[1,262144]{1,0:T(2,128)(2,1)} %bitcast.19), custom_call_target="tpu_custom_call" | custom-call | tf_op jit(solution)/shard_map/pallas_call | solution.py:52
  3.4 0.1 collective-permute-done.other_ref
  3.4 0.0 copy-start
  3.4 0.0 copy-start.1
  3.4 0.0 copy-start.2
  3.4 0.1 shard_map.128
  3.5 2.9 %collective-permute-start.1 = (f32[256,128]{1,0:T(8,128)S(1)}, f32[256,128]{1,0:T(8,128)S(1)}, u32[]{:S(2)}, u32[]{:S(2)}) collective-permute-start(f32[256,128]{1,0:T(8,128)S(1)} %get-tuple-element.30), channel_id=1, source_target_pairs={{0,1},{1,0},{2,3},{3,2},{4,5},{5,4},{6,7},{7,6},{8,9},{9,8},{10,11... | collective-permute-start | bytes 393224 | tf_op jit(solution)/shard_map/ppermute | solution.py:35
  6.5 1.5 %collective-permute-start.2 = (f32[256,128]{1,0:T(8,128)S(1)}, f32[256,128]{1,0:T(8,128)S(1)}, u32[]{:S(2)}, u32[]{:S(2)}) collective-permute-start(f32[256,128]{1,0:T(8,128)S(1)} %get-tuple-element.31), channel_id=1, source_target_pairs={{0,16},{1,17},{2,18},{3,19},{4,20},{5,21},{6,22},{7,23},{8,24},{9,... | collective-permute-start | bytes 393224 | tf_op jit(solution)/shard_map/ppermute | solution.py:35
  7.9 0.0 collective-permute-start.3
  8.0 0.0 copy-start.3
  8.0 0.0 copy-start.4
  8.0 0.0 copy-done
  8.0 0.0 copy-done.1
  8.0 0.0 copy-done.2
  8.0 0.6 %copy-done.3 = f32[5]{0:T(128)S(1)} copy-done((f32[5]{0:T(128)S(1)}, f32[5]{0:T(128)}, u32[]{:S(2)}) %copy-start.3) | copy-done | bytes 44
  8.6 0.0 copy-done.4
  8.7 0.1 shard_map.131.refs_0_
  8.7 4.1 %collective-permute-start.10 = (f32[1,136,128]{2,1,0:T(8,128)S(1)}, f32[1,136,128]{2,1,0:T(8,128)S(1)}, u32[]{:S(2)}, u32[]{:S(2)}) collective-permute-start(f32[1,136,128]{2,1,0:T(8,128)S(1)} %shard_map.131.refs_0_), channel_id=1, source_target_pairs={{0,6},{1,7},{2,4},{3,5},{4,2},{5,3},{6,0},{7,1},{8,14},{9,15},{10,... | collective-permute-start | bytes 208904 | tf_op jit(solution)/shard_map/ppermute | solution.py:35
  12.8 0.0 collective-permute-start.9
  12.8 0.0 collective-permute-done.1.refs_1_
  12.8 0.6 %collective-permute-start.8 = (f32[1,136,128]{2,1,0:T(8,128)S(1)}, f32[1,136,128]{2,1,0:T(8,128)S(1)}, u32[]{:S(2)}, u32[]{:S(2)}) collective-permute-start(f32[1,136,128]{2,1,0:T(8,128)S(1)} %shard_map.131.refs_0_), channel_id=1, source_target_pairs={{0,2},{1,3},{2,0},{3,1},{4,6},{5,7},{6,4},{7,5},{8,10},{9,11},{10,... | collective-permute-start | bytes 208904 | tf_op jit(solution)/shard_map/ppermute | solution.py:35
  13.5 0.0 collective-permute-done.2.refs_2_
  13.5 0.8 %collective-permute-done.3.refs_3_ = f32[256,128]{1,0:T(8,128)S(1)} collective-permute-done((f32[256,128]{1,0:T(8,128)S(1)}, f32[256,128]{1,0:T(8,128)S(1)}, u32[]{:S(2)}, u32[]{:S(2)}) %collective-permute-start.3) | collective-permute-done | bytes 131104 | tf_op jit(solution)/shard_map/ppermute | solution.py:35
  14.4 2.8 %collective-permute-start.5 = (f32[128,128]{1,0:T(8,128)S(1)}, f32[128,128]{1,0:T(8,128)S(1)}, u32[]{:S(2)}, u32[]{:S(2)}) collective-permute-start(f32[128,128]{1,0:T(8,128)S(1)} %get-tuple-element.34.high_ref), channel_id=1, source_target_pairs={{0,4},{1,5},{2,6},{3,7},{4,0},{5,1},{6,2},{7,3},{8,12},{9,13},{10,... | collective-permute-start | bytes 196616 | tf_op jit(solution)/shard_map/ppermute | solution.py:35
  17.2 1.6 %collective-permute-start.4 = (f32[128,128]{1,0:T(8,128)S(1)}, f32[128,128]{1,0:T(8,128)S(1)}, u32[]{:S(2)}, u32[]{:S(2)}) collective-permute-start(f32[128,128]{1,0:T(8,128)S(1)} %get-tuple-element.33.low_ref._), channel_id=1, source_target_pairs={{0,2},{1,3},{2,0},{3,1},{4,6},{5,7},{6,4},{7,5},{8,10},{9,11},{10,... | collective-permute-start | bytes 196616 | tf_op jit(solution)/shard_map/ppermute | solution.py:35
  19.4 0.0 collective-permute-done.10.refs_3_
  19.4 0.3 collective-permute-done.9.refs_2_
  19.7 0.0 collective-permute-done.8.refs_1_
  19.7 0.1 shard_map.132
  19.8 1.7 %collective-permute-start.15 = (f32[4,128,128]{2,1,0:T(8,128)S(1)}, f32[4,128,128]{2,1,0:T(8,128)S(1)}, u32[]{:S(2)}, u32[]{:S(2)}) collective-permute-start(f32[4,128,128]{2,1,0:T(8,128)S(1)} %get-tuple-element.43), channel_id=1, source_target_pairs={{0,1},{1,0},{2,3},{3,2},{4,5},{5,4},{6,7},{7,6},{8,9},{9,8},{10,11... | collective-permute-start | bytes 786440 | tf_op jit(solution)/shard_map/ppermute | solution.py:35
  21.5 0.0 collective-permute-done.5.high_other
  21.5 0.0 collective-permute-done.4.low_other
  21.5 1.4 %collective-permute-start.6 = (f32[128,128]{1,0:T(8,128)S(1)}, f32[128,128]{1,0:T(8,128)S(1)}, u32[]{:S(2)}, u32[]{:S(2)}) collective-permute-start(f32[128,128]{1,0:T(8,128)S(1)} %get-tuple-element.35.refs_0_), channel_id=1, source_target_pairs={{0,4},{1,5},{2,6},{3,7},{4,0},{5,1},{6,2},{7,3},{8,12},{9,13},{10,... | collective-permute-start | bytes 196616 | tf_op jit(solution)/shard_map/ppermute | solution.py:35
  22.8 1.7 %collective-permute-start.7 = (f32[128,128]{1,0:T(8,128)S(1)}, f32[128,128]{1,0:T(8,128)S(1)}, u32[]{:S(2)}, u32[]{:S(2)}) collective-permute-start(f32[128,128]{1,0:T(8,128)S(1)} %get-tuple-element.36.refs_2_), channel_id=1, source_target_pairs={{0,2},{1,3},{2,0},{3,1},{4,6},{5,7},{6,4},{7,5},{8,10},{9,11},{10,... | collective-permute-start | bytes 196616 | tf_op jit(solution)/shard_map/ppermute | solution.py:35
  24.6 2.2 %collective-permute-done.6.refs_1_ = f32[128,128]{1,0:T(8,128)S(1)} collective-permute-done((f32[128,128]{1,0:T(8,128)S(1)}, f32[128,128]{1,0:T(8,128)S(1)}, u32[]{:S(2)}, u32[]{:S(2)}) %collective-permute-start.6) | collective-permute-done | bytes 65568 | tf_op jit(solution)/shard_map/ppermute | solution.py:35
  26.7 0.7 %collective-permute-done.7.refs_3_ = f32[128,128]{1,0:T(8,128)S(1)} collective-permute-done((f32[128,128]{1,0:T(8,128)S(1)}, f32[128,128]{1,0:T(8,128)S(1)}, u32[]{:S(2)}, u32[]{:S(2)}) %collective-permute-start.7) | collective-permute-done | bytes 65568 | tf_op jit(solution)/shard_map/ppermute | solution.py:35
  27.4 0.1 shard_map.133
  27.5 0.1 collective-permute-start.11
  27.6 1.2 %collective-permute-done.11.other_ref = f32[32,128]{1,0:T(8,128)S(1)} collective-permute-done((f32[32,128]{1,0:T(8,128)S(1)}, f32[32,128]{1,0:T(8,128)S(1)}, u32[]{:S(2)}, u32[]{:S(2)}) %collective-permute-start.11) | collective-permute-done | bytes 16416 | tf_op jit(solution)/shard_map/ppermute | solution.py:35
  28.8 1.7 %collective-permute-start.12 = (f32[320,128]{1,0:T(8,128)S(1)}, f32[320,128]{1,0:T(8,128)S(1)}, u32[]{:S(2)}, u32[]{:S(2)}) collective-permute-start(f32[320,128]{1,0:T(8,128)S(1)} %get-tuple-element.41), channel_id=1, source_target_pairs={{0,1},{1,0},{2,3},{3,2},{4,5},{5,4},{6,7},{7,6},{8,9},{9,8},{10,11... | collective-permute-start | bytes 491528 | tf_op jit(solution)/shard_map/ppermute | solution.py:35
  30.5 1.4 %collective-permute-start.14 = (f32[32,128]{1,0:T(8,128)S(1)}, f32[32,128]{1,0:T(8,128)S(1)}, u32[]{:S(2)}, u32[]{:S(2)}) collective-permute-start(f32[32,128]{1,0:T(8,128)S(1)} %get-tuple-element.42), channel_id=1, source_target_pairs={{0,17},{1,16},{2,19},{3,18},{4,21},{5,20},{6,23},{7,22},{8,25},{9,... | collective-permute-start | bytes 49160 | tf_op jit(solution)/shard_map/ppermute | solution.py:35
  31.9 0.4 %collective-permute-start.13 = (f32[8,128]{1,0:T(8,128)S(1)}, f32[8,128]{1,0:T(8,128)S(1)}, u32[]{:S(2)}, u32[]{:S(2)}) collective-permute-start(f32[8,128]{1,0:T(8,128)S(1)} %get-tuple-element.40.refs_0_), channel_id=1, source_target_pairs={{0,16},{1,17},{2,18},{3,19},{4,20},{5,21},{6,22},{7,23},{8,24},{9,... | collective-permute-start | bytes 12296 | tf_op jit(solution)/shard_map/ppermute | solution.py:35
  32.4 3.2 %collective-permute-done.13.refs_2_ = f32[8,128]{1,0:T(8,128)S(1)} collective-permute-done((f32[8,128]{1,0:T(8,128)S(1)}, f32[8,128]{1,0:T(8,128)S(1)}, u32[]{:S(2)}, u32[]{:S(2)}) %collective-permute-start.13) | collective-permute-done | bytes 4128 | tf_op jit(solution)/shard_map/ppermute | solution.py:35
  35.5 0.0 collective-permute-done.14.refs_3_
  35.5 0.0 collective-permute-done.15.refs_6_
  35.5 0.0 collective-permute-done.12.refs_1_
  35.5 1.3 %shard_map.135 = (f32[64,128]{1,0:T(8,128)}, bf16[512,128]{1,0:T(8,128)(2,1)}, f32[64,128]{1,0:T(8,128)}, f32[64,128]{1,0:T(8,128)}, f32[64,128]{1,0:T(8,128)}, /*index=5*/f32[5]{0:T(128)}, f32[5]{0:T(128)}) custom-call(f32[8,128]{1,0:T(8,128)S(1)} %get-tuple-element.40.refs_0_, f32[320,128]{1,0:T(8,128)S(1)} %collective-permute-done.12.refs_1_, ...), custom_call_target="tpu_custom_call" | custom-call | tf_op jit(solution)/shard_map/pallas_call | solution.py:52
  (3 shorter events, 0.1 us)
Async XLA Ops:
  1.8 1.7 %collective-permute-start = (bf16[1024,128]{1,0:T(8,128)(2,1)S(1)}, bf16[1024,128]{1,0:T(8,128)(2,1)S(1)}, u32[]{:S(2)}, u32[]{:S(2)}) collective-permute-start(bf16[1024,128]{1,0:T(8,128)(2,1)S(1)} %shard_map.127), channel_id=1, source_target_pairs={{0,8},{1,9},{2,10},{3,11},{4,12},{5,13},{6,14},{7,15},{8,0},{9,1},... | collective-permute-start | bytes 786440 | tf_op jit(solution)/shard_map/ppermute | solution.py:35
  3.4 4.6 %copy-start = (s32[8192]{0:T(1024)S(1)}, s32[8192]{0:T(1024)}, u32[]{:S(2)}) copy-start(s32[8192]{0:T(1024)} %param.8) | copy-start | bytes 98308
  3.4 4.6 %copy-start.1 = (s32[8192]{0:T(1024)S(1)}, s32[8192]{0:T(1024)}, u32[]{:S(2)}) copy-start(s32[8192]{0:T(1024)} %param.9) | copy-start | bytes 98308
  3.4 4.6 %copy-start.2 = (f32[8192]{0:T(1024)S(1)}, f32[8192]{0:T(1024)}, u32[]{:S(2)}) copy-start(f32[8192]{0:T(1024)} %param.12) | copy-start | bytes 98308
  3.5 9.3 %collective-permute-start.1 = (f32[256,128]{1,0:T(8,128)S(1)}, f32[256,128]{1,0:T(8,128)S(1)}, u32[]{:S(2)}, u32[]{:S(2)}) collective-permute-start(f32[256,128]{1,0:T(8,128)S(1)} %get-tuple-element.30), channel_id=1, source_target_pairs={{0,1},{1,0},{2,3},{3,2},{4,5},{5,4},{6,7},{7,6},{8,9},{9,8},{10,11... | collective-permute-start | bytes 393224 | tf_op jit(solution)/shard_map/ppermute | solution.py:35
  6.5 7.0 %collective-permute-start.2 = (f32[256,128]{1,0:T(8,128)S(1)}, f32[256,128]{1,0:T(8,128)S(1)}, u32[]{:S(2)}, u32[]{:S(2)}) collective-permute-start(f32[256,128]{1,0:T(8,128)S(1)} %get-tuple-element.31), channel_id=1, source_target_pairs={{0,16},{1,17},{2,18},{3,19},{4,20},{5,21},{6,22},{7,23},{8,24},{9,... | collective-permute-start | bytes 393224 | tf_op jit(solution)/shard_map/ppermute | solution.py:35
  7.9 6.4 %collective-permute-start.3 = (f32[256,128]{1,0:T(8,128)S(1)}, f32[256,128]{1,0:T(8,128)S(1)}, u32[]{:S(2)}, u32[]{:S(2)}) collective-permute-start(f32[256,128]{1,0:T(8,128)S(1)} %get-tuple-element.32), channel_id=1, source_target_pairs={{0,17},{1,16},{2,19},{3,18},{4,21},{5,20},{6,23},{7,22},{8,25},{9,... | collective-permute-start | bytes 393224 | tf_op jit(solution)/shard_map/ppermute | solution.py:35
  8.0 0.7 %copy-start.3 = (f32[5]{0:T(128)S(1)}, f32[5]{0:T(128)}, u32[]{:S(2)}) copy-start(f32[5]{0:T(128)} %param.10) | copy-start | bytes 64
  8.0 0.7 %copy-start.4 = (f32[5]{0:T(128)S(1)}, f32[5]{0:T(128)}, u32[]{:S(2)}) copy-start(f32[5]{0:T(128)} %param.11) | copy-start | bytes 64
  8.7 10.6 %collective-permute-start.10 = (f32[1,136,128]{2,1,0:T(8,128)S(1)}, f32[1,136,128]{2,1,0:T(8,128)S(1)}, u32[]{:S(2)}, u32[]{:S(2)}) collective-permute-start(f32[1,136,128]{2,1,0:T(8,128)S(1)} %shard_map.131.refs_0_), channel_id=1, source_target_pairs={{0,6},{1,7},{2,4},{3,5},{4,2},{5,3},{6,0},{7,1},{8,14},{9,15},{10,... | collective-permute-start | bytes 208904 | tf_op jit(solution)/shard_map/ppermute | solution.py:35
  12.8 6.9 %collective-permute-start.9 = (f32[1,136,128]{2,1,0:T(8,128)S(1)}, f32[1,136,128]{2,1,0:T(8,128)S(1)}, u32[]{:S(2)}, u32[]{:S(2)}) collective-permute-start(f32[1,136,128]{2,1,0:T(8,128)S(1)} %shard_map.131.refs_0_), channel_id=1, source_target_pairs={{0,4},{1,5},{2,6},{3,7},{4,0},{5,1},{6,2},{7,3},{8,12},{9,13},{10,... | collective-permute-start | bytes 208904 | tf_op jit(solution)/shard_map/ppermute | solution.py:35
  12.8 6.8 %collective-permute-start.8 = (f32[1,136,128]{2,1,0:T(8,128)S(1)}, f32[1,136,128]{2,1,0:T(8,128)S(1)}, u32[]{:S(2)}, u32[]{:S(2)}) collective-permute-start(f32[1,136,128]{2,1,0:T(8,128)S(1)} %shard_map.131.refs_0_), channel_id=1, source_target_pairs={{0,2},{1,3},{2,0},{3,1},{4,6},{5,7},{6,4},{7,5},{8,10},{9,11},{10,... | collective-permute-start | bytes 208904 | tf_op jit(solution)/shard_map/ppermute | solution.py:35
  14.4 7.1 %collective-permute-start.5 = (f32[128,128]{1,0:T(8,128)S(1)}, f32[128,128]{1,0:T(8,128)S(1)}, u32[]{:S(2)}, u32[]{:S(2)}) collective-permute-start(f32[128,128]{1,0:T(8,128)S(1)} %get-tuple-element.34.high_ref), channel_id=1, source_target_pairs={{0,4},{1,5},{2,6},{3,7},{4,0},{5,1},{6,2},{7,3},{8,12},{9,13},{10,... | collective-permute-start | bytes 196616 | tf_op jit(solution)/shard_map/ppermute | solution.py:35
  17.2 4.3 %collective-permute-start.4 = (f32[128,128]{1,0:T(8,128)S(1)}, f32[128,128]{1,0:T(8,128)S(1)}, u32[]{:S(2)}, u32[]{:S(2)}) collective-permute-start(f32[128,128]{1,0:T(8,128)S(1)} %get-tuple-element.33.low_ref._), channel_id=1, source_target_pairs={{0,2},{1,3},{2,0},{3,1},{4,6},{5,7},{6,4},{7,5},{8,10},{9,11},{10,... | collective-permute-start | bytes 196616 | tf_op jit(solution)/shard_map/ppermute | solution.py:35
  19.8 15.7 %collective-permute-start.15 = (f32[4,128,128]{2,1,0:T(8,128)S(1)}, f32[4,128,128]{2,1,0:T(8,128)S(1)}, u32[]{:S(2)}, u32[]{:S(2)}) collective-permute-start(f32[4,128,128]{2,1,0:T(8,128)S(1)} %get-tuple-element.43), channel_id=1, source_target_pairs={{0,1},{1,0},{2,3},{3,2},{4,5},{5,4},{6,7},{7,6},{8,9},{9,8},{10,11... | collective-permute-start | bytes 786440 | tf_op jit(solution)/shard_map/ppermute | solution.py:35
  21.5 5.3 %collective-permute-start.6 = (f32[128,128]{1,0:T(8,128)S(1)}, f32[128,128]{1,0:T(8,128)S(1)}, u32[]{:S(2)}, u32[]{:S(2)}) collective-permute-start(f32[128,128]{1,0:T(8,128)S(1)} %get-tuple-element.35.refs_0_), channel_id=1, source_target_pairs={{0,4},{1,5},{2,6},{3,7},{4,0},{5,1},{6,2},{7,3},{8,12},{9,13},{10,... | collective-permute-start | bytes 196616 | tf_op jit(solution)/shard_map/ppermute | solution.py:35
  22.8 4.6 %collective-permute-start.7 = (f32[128,128]{1,0:T(8,128)S(1)}, f32[128,128]{1,0:T(8,128)S(1)}, u32[]{:S(2)}, u32[]{:S(2)}) collective-permute-start(f32[128,128]{1,0:T(8,128)S(1)} %get-tuple-element.36.refs_2_), channel_id=1, source_target_pairs={{0,2},{1,3},{2,0},{3,1},{4,6},{5,7},{6,4},{7,5},{8,10},{9,11},{10,... | collective-permute-start | bytes 196616 | tf_op jit(solution)/shard_map/ppermute | solution.py:35
  27.5 1.2 %collective-permute-start.11 = (f32[32,128]{1,0:T(8,128)S(1)}, f32[32,128]{1,0:T(8,128)S(1)}, u32[]{:S(2)}, u32[]{:S(2)}) collective-permute-start(f32[32,128]{1,0:T(8,128)S(1)} %get-tuple-element.38.mine_ref), channel_id=1, source_target_pairs={{0,8},{1,9},{2,10},{3,11},{4,12},{5,13},{6,14},{7,15},{8,0},{9,1},... | collective-permute-start | bytes 49160 | tf_op jit(solution)/shard_map/ppermute | solution.py:35
  28.8 6.7 %collective-permute-start.12 = (f32[320,128]{1,0:T(8,128)S(1)}, f32[320,128]{1,0:T(8,128)S(1)}, u32[]{:S(2)}, u32[]{:S(2)}) collective-permute-start(f32[320,128]{1,0:T(8,128)S(1)} %get-tuple-element.41), channel_id=1, source_target_pairs={{0,1},{1,0},{2,3},{3,2},{4,5},{5,4},{6,7},{7,6},{8,9},{9,8},{10,11... | collective-permute-start | bytes 491528 | tf_op jit(solution)/shard_map/ppermute | solution.py:35
  30.5 5.0 %collective-permute-start.14 = (f32[32,128]{1,0:T(8,128)S(1)}, f32[32,128]{1,0:T(8,128)S(1)}, u32[]{:S(2)}, u32[]{:S(2)}) collective-permute-start(f32[32,128]{1,0:T(8,128)S(1)} %get-tuple-element.42), channel_id=1, source_target_pairs={{0,17},{1,16},{2,19},{3,18},{4,21},{5,20},{6,23},{7,22},{8,25},{9,... | collective-permute-start | bytes 49160 | tf_op jit(solution)/shard_map/ppermute | solution.py:35
  31.9 3.6 %collective-permute-start.13 = (f32[8,128]{1,0:T(8,128)S(1)}, f32[8,128]{1,0:T(8,128)S(1)}, u32[]{:S(2)}, u32[]{:S(2)}) collective-permute-start(f32[8,128]{1,0:T(8,128)S(1)} %get-tuple-element.40.refs_0_), channel_id=1, source_target_pairs={{0,16},{1,17},{2,18},{3,19},{4,20},{5,21},{6,22},{7,23},{8,24},{9,... | collective-permute-start | bytes 12296 | tf_op jit(solution)/shard_map/ppermute | solution.py:35

commit v4 on v3

--- a/solution.py
+++ b/solution.py
@@ -115,9 +115,8 @@
     high_ref[...] = tree([r[half:, :] for r in terms])
 
 
-def two_kernel(low_ref, low_other, high_ref, high_other, low_out, high_out):
-    low_out[...] = low_ref[...] + low_other[...]
-    high_out[...] = high_ref[...] + high_other[...]
+def add_kernel(mine_ref, other_ref, _, o_ref):
+    o_ref[...] = mine_ref[...] + other_ref[...]
 
 
 def state_rows(plan, slots):
@@ -125,7 +124,7 @@
 
 
 def scale_rows(slots):
-    return -(-(slots + 2) // 8) * 8
+    return -(-slots // 8) * 8
 
 
 def power(base, count):
@@ -147,30 +146,36 @@
         o_ref[2 * rows + j : 2 * rows + j + 1, :] = scales
 
 
-def old_moments(state, scales, low, high):
+def decayed(state, scales, low, high):
     slot = (low + EDGE) // (2 * EDGE)
     scale = scales[slot : slot + 1, :]
     pair = state[low:high, :]
     v_code = jnp.floor(pair * (1.0 / 256.0))
-    m_code = pair - v_code * 256.0 - 128.0
-    return m_code / 127.0 * scale[:, 0:1], v_code / 255.0 * scale[:, LANES // 2 : LANES // 2 + 1]
+    m_code = pair - (v_code * 256.0 + 128.0)
+    m_scale, v_scale = scale[:, 0:1] * (0.9 / 127.0), scale[:, LANES // 2 : LANES // 2 + 1] * (0.95 / 255.0)
+    return m_code * m_scale, v_code * v_scale
 
 
 def pieces(plan, slots):
     return [(max(0, (2 * j - 1) * EDGE), min(plan.rows, (2 * j + 1) * EDGE)) for j in range(slots)]
 
 
-def order_kernel(plan, slots, step_ref, _, *refs):
+def order_kernel(plan, _, *refs):
     *states, o_ref, send_ref = refs
     _, _, z, _ = place()
     for k, ref in enumerate(states):
         o_ref[z ^ k] = ref[0]
         send_ref[z ^ k] = ref[0, : send_ref.shape[1], :]
+
+
+def token_kernel(x_ref, *refs):
+    refs[-1][...] = x_ref[0:8, :]
+
+
+def fix_kernel(step_ref, _, o_ref):
     count = jnp.broadcast_to(step_ref[...], (1, LANES))
     for j, base in enumerate((0.9, 0.95)):
-        at = 2 * plan.rows + slots + j
-        for i in range(plan.zs):
-            o_ref[i, at : at + 1, :] = 1.0 - power(base, count)
+        o_ref[j : j + 1, :] = 1.0 / (1.0 - power(base, count))
 
 
 def squares(values):
@@ -189,7 +194,7 @@
     def edge(z, start):
         send_ref[8 : 8 + EDGE, :] = sum_ref[z * plan.rows + start : z * plan.rows + start + EDGE, :]
         state = state_ref.at[z]
-        old = old_moments(state, state.at[2 * plan.rows :], start, start + EDGE)
+        old = decayed(state, state.at[2 * plan.rows :], start, start + EDGE)
         for k in range(2):
             send_ref[8 + (k + 1) * EDGE : 8 + (k + 2) * EDGE, :] = old[k]
 
@@ -218,14 +223,14 @@
 
 def main_kernel(plan, total_params, *refs):
     norms, refs = refs[: plan.groups], refs[plan.groups :]
-    (sum_mine, state_mine, state_other) = refs[:3]
-    (master_out, weights_out, update_out, mn_out, vn_out, mt_out, vt_out) = refs[3:10]
-    m_buf, v_buf, far = refs[10:]
+    (sum_mine, state_mine, state_other, fix_ref) = refs[:4]
+    (master_out, weights_out, update_out, mn_out, vn_out, mt_out, vt_out) = refs[4:11]
+    m_buf, v_buf, far = refs[11:]
     sums_at, scales_at = 8 + 3 * EDGE, 8 + 3 * EDGE + plan.zs * plan.rows
     sum_other = norms[1].at[sums_at:scales_at]
     x, core, z, y = place()
     rows = plan.rows
-    slots = mt_out.shape[0]
+    slots = mt_out.shape[1]
     norm_sq = jnp.sum(tree([r[0:8, :] for r in norms]), keepdims=True)
     clip = jnp.minimum(1.0, float(total_params) ** 0.5 / (jnp.sqrt(norm_sq) + 1e-06))
     def scales_mine(k):
@@ -235,16 +240,15 @@
         size = scale_rows(slots)
         return norms[1].at[pl.ds(scales_at + k * size, size)]
 
-    at = 2 * rows + slots
-    first_fix, second_fix = state_mine[0, at : at + 1, :], state_mine[0, at + 1 : at + 2, :]
-
-    def moments(grad, m_old, v_old):
+    first, second = fix_ref[0:1, :], fix_ref[1:2, :]
+
+    def moments(grad, m_decayed, v_decayed):
         scaled = grad * clip
-        return 0.9 * m_old + 0.1 * scaled, 0.95 * v_old + 0.05 * scaled * scaled
+        return m_decayed + 0.1 * scaled, v_decayed + 0.05 * scaled * scaled
 
     def step(grads, state, scales, low, high):
-        m, v = moments(grads[low:high, :], *old_moments(state, scales, low, high))
-        update = m / first_fix / (jnp.sqrt(v / second_fix) + 1e-08)
+        m, v = moments(grads[low:high, :], *decayed(state, scales, low, high))
+        update = m * first / (jnp.sqrt(v * second) + 1e-08)
         master = state[rows + low : rows + high, :]
         return m, v, update, master * (1.0 - 0.0001 * 0.1) - 0.0001 * update
 
@@ -268,7 +272,7 @@
 
     def near(side, at_z, start):
         grad = sum_other[pl.ds(pl.multiple_of(at_z * rows + start, EDGE), EDGE), :]
-        em, ev = moments(grad, *old_moments(state_other.at[at_z], scales_other(at_z), start, start + EDGE))
+        em, ev = moments(grad, *decayed(state_other.at[at_z], scales_other(at_z), start, start + EDGE))
         far[side, 0], far[side, 1] = jnp.abs(em), jnp.abs(ev)
 
     def across(side, shard):
@@ -304,8 +308,10 @@
         def _():
             across(1, shard + 1)
 
-    for j, (low, high) in enumerate(pieces(plan, slots)):
-        for which, (buf, table, norm_out) in enumerate(((m_buf, mt_out, mn_out), (v_buf, vt_out, vn_out))):
+    lane = lax.broadcasted_iota(jnp.int32, (1, LANES), 1)
+    for which, (buf, table, norm_out) in enumerate(((m_buf, mt_out, mn_out), (v_buf, vt_out, vn_out))):
+        line = jnp.zeros((1, LANES), F32)
+        for j, (low, high) in enumerate(pieces(plan, slots)):
             values = buf[low:high, :]
             top = jnp.max(jnp.abs(values).reshape(-1, 8, LANES), axis=0)
             if j == 0:
@@ -313,8 +319,9 @@
             if j == slots - 1:
                 top = jnp.maximum(top, far[1, which])
             top = jnp.max(top, keepdims=True)
-            table[j] = top[0, 0]
+            line = jnp.where(lane == j, top, line)
             norm_out[low:high, :] = values / (top + 1e-06)
+        table[...] = line[:, :slots]
 
 
 def on_device(grads, momentum_codes, variance_codes, momentum_scale, variance_scale, master, step):
@@ -360,12 +367,14 @@
         high_other = plan.swap(high, z=1 << (bits - 1 - bit))
         low_other = plan.swap(low, z=1 << bit)
         if bit < bits - 1:
-            low, high = call(two_kernel, [half_shape] * 2, [low, low_other, high, high_other])
+            high = call(add_kernel, half_shape, [high, high_other, low], [VMEM, VMEM, ANY])
+            low = call(add_kernel, half_shape, [low, low_other, high], [VMEM, VMEM, ANY])
+    gate = call(token_kernel, struct((8, LANES), F32), [gate, *near[2:]], [VMEM] + [ANY] * (zs - 2))
     state_mine, state_send = call(
-        functools.partial(order_kernel, plan, slots),
+        functools.partial(order_kernel, plan),
         [struct((zs, *state_shape), F32), struct((zs, 2 * rows, LANES), F32)],
-        [step.reshape(1, 1), gate, *near],
-        [VMEM, ANY] + [VMEM] * zs,
+        [gate, *near],
+        [ANY] + [VMEM] * zs,
     )
     state_other = plan.swap(state_send, group=1)
     send_rows = 8 + 3 * EDGE
@@ -384,15 +393,16 @@
     wide = plan.swap(wide, group=1)
     norms = [norm, wide] + [plan.swap(relay if k % 2 else norm, group=k) for k in range(2, groups)]
 
+    fixes = call(fix_kernel, struct((8, LANES), F32), [step.reshape(1, 1), relay], [VMEM, ANY])
+
     total_params = own_len * plan.devices
     own = struct((rows, LANES), F32)
-    table = struct((slots,), F32)
-    ins = [*norms, sum_mine, state_mine, state_other]
+    table = struct((1, slots), F32)
+    ins = [*norms, sum_mine, state_mine, state_other, fixes]
     new_master, weights, update, mn, vn, mt, vt = call(
         functools.partial(main_kernel, plan, total_params),
         [own, struct((plan.reps * rows, LANES), BF16), own, own, own, table, table],
         ins,
-        out_specs=[VMEM] * 5 + [SMEM] * 2,
         scratch=[pltpu.VMEM(shape, F32), pltpu.VMEM(shape, F32), pltpu.VMEM((2, 2, EDGE, LANES), F32)],
     )
     return (
@@ -401,8 +411,8 @@
         update.reshape(-1),
         mn.reshape(-1),
         vn.reshape(-1),
-        mt,
-        vt,
+        mt.reshape(-1),
+        vt.reshape(-1),
     )
 
 

time: 37 us -> 36.7 us (level)
  waiting for transfers between devices: 8.37 us -> 7.88 us
    ppermute x16, waiting for transfers between devices: 8.37 us -> 7.88 us  [swap(): lax.ppermute(value, ALL, [(i, i ^ mask) for i in range(self.devices)])]
    pallas_call x10 -> x13, Pallas kernels: 3.95 us -> 3.97 us  [call(): pl.pallas_call(kernel, out_shape=outs, in_specs=in_specs or [VMEM] * len(...]
  transfers between devices with their start and end apart: 16 -> 16, of which waited for: 7 -> 8; matrix products, arithmetic and copies ran while one was open for 0% -> 0% of each run, Pallas kernels for 4% -> 4%
where the time goes in v4:
time: 36.7 us; the launch traced here: 36.5 us
  starting transfers between devices  22.6 us (62%)
  waiting for transfers between devices  7.88 us (21%)
  Pallas kernels  3.97 us (11%)
  between operations  1.37 us (4%)
  local copies, waits for them, and re-layouts  0.66 us (2%)
    ppermute x16, starting transfers between devices, swap(): lax.ppermute(value, ALL, [(i, i ^ mask) for i in range(self.devices)])  22.6 us
    ppermute x16, waiting for transfers between devices, swap(): lax.ppermute(value, ALL, [(i, i ^ mask) for i in range(self.devices)])  7.88 us
    pallas_call x13, Pallas kernels, call(): pl.pallas_call(kernel, out_shape=outs, in_specs=in_specs or [VMEM] * len(...  3.97 us
  transfers between devices with their start and end apart: 16, of which 8 were waited for; matrix products, arithmetic and copies ran while one was open for 0% of the time, Pallas kernels for 4%

profile of v4, /device:TPU:0, one launch (start us, length us, event | category | flops | bytes accessed | tf_op | source)
XLA Modules:
  0.0 36.5 jit_solution(16957692388636195424)
XLA Ops:
  0.6 1.1 %shard_map.127 = bf16[1024,128]{1,0:T(8,128)(2,1)S(1)} custom-call(bf16[1,262144]{1,0:T(2,128)(2,1)} %bitcast.20), custom_call_target="tpu_custom_call" | custom-call | tf_op jit(solution)/shard_map/pallas_call | solution.py:52
  1.8 0.5 %collective-permute-start = (bf16[1024,128]{1,0:T(8,128)(2,1)S(1)}, bf16[1024,128]{1,0:T(8,128)(2,1)S(1)}, u32[]{:S(2)}, u32[]{:S(2)}) collective-permute-start(bf16[1024,128]{1,0:T(8,128)(2,1)S(1)} %shard_map.127), channel_id=1, source_target_pairs={{0,8},{1,9},{2,10},{3,11},{4,12},{5,13},{6,14},{7,15},{8,0},{9,1},... | collective-permute-start | bytes 786440 | tf_op jit(solution)/shard_map/ppermute | solution.py:35
  2.3 1.1 %shard_map.126.mine_ref = bf16[1024,128]{1,0:T(8,128)(2,1)S(1)} custom-call(bf16[1,262144]{1,0:T(2,128)(2,1)} %bitcast.21), custom_call_target="tpu_custom_call" | custom-call | tf_op jit(solution)/shard_map/pallas_call | solution.py:52
  3.4 0.1 collective-permute-done.other_ref
  3.4 0.0 copy-start
  3.4 0.0 copy-start.1
  3.4 0.0 copy-start.2
  3.4 0.1 shard_map.128
  3.5 2.9 %collective-permute-start.1 = (f32[256,128]{1,0:T(8,128)S(1)}, f32[256,128]{1,0:T(8,128)S(1)}, u32[]{:S(2)}, u32[]{:S(2)}) collective-permute-start(f32[256,128]{1,0:T(8,128)S(1)} %get-tuple-element.28), channel_id=1, source_target_pairs={{0,1},{1,0},{2,3},{3,2},{4,5},{5,4},{6,7},{7,6},{8,9},{9,8},{10,11... | collective-permute-start | bytes 393224 | tf_op jit(solution)/shard_map/ppermute | solution.py:35
  6.5 1.5 %collective-permute-start.2 = (f32[256,128]{1,0:T(8,128)S(1)}, f32[256,128]{1,0:T(8,128)S(1)}, u32[]{:S(2)}, u32[]{:S(2)}) collective-permute-start(f32[256,128]{1,0:T(8,128)S(1)} %get-tuple-element.29), channel_id=1, source_target_pairs={{0,16},{1,17},{2,18},{3,19},{4,20},{5,21},{6,22},{7,23},{8,24},{9,... | collective-permute-start | bytes 393224 | tf_op jit(solution)/shard_map/ppermute | solution.py:35
  7.9 0.0 collective-permute-start.3
  8.0 0.0 copy-start.3
  8.0 0.0 copy-start.4
  8.0 0.0 copy-done
  8.0 0.0 copy-done.1
  8.0 0.0 copy-done.2
  8.0 0.6 %copy-done.3 = f32[5]{0:T(128)S(1)} copy-done((f32[5]{0:T(128)S(1)}, f32[5]{0:T(128)}, u32[]{:S(2)}) %copy-start.3) | copy-done | bytes 44
  8.6 0.0 copy-done.4
  8.7 0.1 shard_map.132.refs_0_
  8.7 4.1 %collective-permute-start.9 = (f32[1,136,128]{2,1,0:T(8,128)S(1)}, f32[1,136,128]{2,1,0:T(8,128)S(1)}, u32[]{:S(2)}, u32[]{:S(2)}) collective-permute-start(f32[1,136,128]{2,1,0:T(8,128)S(1)} %shard_map.132.refs_0_), channel_id=1, source_target_pairs={{0,6},{1,7},{2,4},{3,5},{4,2},{5,3},{6,0},{7,1},{8,14},{9,15},{10,... | collective-permute-start | bytes 208904 | tf_op jit(solution)/shard_map/ppermute | solution.py:35
  12.8 0.0 collective-permute-start.8
  12.8 0.0 collective-permute-done.1.refs_1_
  12.8 0.6 %collective-permute-start.10 = (f32[1,136,128]{2,1,0:T(8,128)S(1)}, f32[1,136,128]{2,1,0:T(8,128)S(1)}, u32[]{:S(2)}, u32[]{:S(2)}) collective-permute-start(f32[1,136,128]{2,1,0:T(8,128)S(1)} %shard_map.132.refs_0_), channel_id=1, source_target_pairs={{0,2},{1,3},{2,0},{3,1},{4,6},{5,7},{6,4},{7,5},{8,10},{9,11},{10,... | collective-permute-start | bytes 208904 | tf_op jit(solution)/shard_map/ppermute | solution.py:35
  13.5 0.0 collective-permute-done.2.refs_2_
  13.5 0.8 %collective-permute-done.3.refs_3_ = f32[256,128]{1,0:T(8,128)S(1)} collective-permute-done((f32[256,128]{1,0:T(8,128)S(1)}, f32[256,128]{1,0:T(8,128)S(1)}, u32[]{:S(2)}, u32[]{:S(2)}) %collective-permute-start.3) | collective-permute-done | bytes 131104 | tf_op jit(solution)/shard_map/ppermute | solution.py:35
  14.4 2.8 %collective-permute-start.5 = (f32[128,128]{1,0:T(8,128)S(1)}, f32[128,128]{1,0:T(8,128)S(1)}, u32[]{:S(2)}, u32[]{:S(2)}) collective-permute-start(f32[128,128]{1,0:T(8,128)S(1)} %get-tuple-element.32.mine_ref), channel_id=1, source_target_pairs={{0,4},{1,5},{2,6},{3,7},{4,0},{5,1},{6,2},{7,3},{8,12},{9,13},{10,... | collective-permute-start | bytes 196616 | tf_op jit(solution)/shard_map/ppermute | solution.py:35
  17.2 1.6 %collective-permute-start.4 = (f32[128,128]{1,0:T(8,128)S(1)}, f32[128,128]{1,0:T(8,128)S(1)}, u32[]{:S(2)}, u32[]{:S(2)}) collective-permute-start(f32[128,128]{1,0:T(8,128)S(1)} %get-tuple-element.31._.mine_ref.x_ref), channel_id=1, source_target_pairs={{0,2},{1,3},{2,0},{3,1},{4,6},{5,7},{6,4},{7,5},{8,10},{9,11},{10,... | collective-permute-start | bytes 196616 | tf_op jit(solution)/shard_map/ppermute | solution.py:35
  18.7 0.0 collective-permute-done.9.refs_1_.refs_3_
  18.7 1.0 %collective-permute-done.8.refs_0_.refs_2_ = f32[1,136,128]{2,1,0:T(8,128)S(1)} collective-permute-done((f32[1,136,128]{2,1,0:T(8,128)S(1)}, f32[1,136,128]{2,1,0:T(8,128)S(1)}, u32[]{:S(2)}, u32[]{:S(2)}) %collective-permute-start.8) | collective-permute-done | bytes 69664 | tf_op jit(solution)/shard_map/ppermute | solution.py:35
  19.7 0.0 collective-permute-done.10.refs_1_
  19.8 1.7 %collective-permute-start.15 = (f32[4,128,128]{2,1,0:T(8,128)S(1)}, f32[4,128,128]{2,1,0:T(8,128)S(1)}, u32[]{:S(2)}, u32[]{:S(2)}) collective-permute-start(f32[4,128,128]{2,1,0:T(8,128)S(1)} %get-tuple-element.39), channel_id=1, source_target_pairs={{0,1},{1,0},{2,3},{3,2},{4,5},{5,4},{6,7},{7,6},{8,9},{9,8},{10,11... | collective-permute-start | bytes 786440 | tf_op jit(solution)/shard_map/ppermute | solution.py:35
  21.4 0.0 collective-permute-done.5.other_ref
  21.4 0.4 %collective-permute-start.7 = (f32[128,128]{1,0:T(8,128)S(1)}, f32[128,128]{1,0:T(8,128)S(1)}, u32[]{:S(2)}, u32[]{:S(2)}) collective-permute-start(f32[128,128]{1,0:T(8,128)S(1)} %shard_map.130._.refs_2_), channel_id=1, source_target_pairs={{0,2},{1,3},{2,0},{3,1},{4,6},{5,7},{6,4},{7,5},{8,10},{9,11},{10,... | collective-permute-start | bytes 196616 | tf_op jit(solution)/shard_map/ppermute | solution.py:35
  21.9 0.0 collective-permute-done.4.other_ref
  21.9 2.8 %collective-permute-start.6 = (f32[128,128]{1,0:T(8,128)S(1)}, f32[128,128]{1,0:T(8,128)S(1)}, u32[]{:S(2)}, u32[]{:S(2)}) collective-permute-start(f32[128,128]{1,0:T(8,128)S(1)} %shard_map.131.refs_0_), channel_id=1, source_target_pairs={{0,4},{1,5},{2,6},{3,7},{4,0},{5,1},{6,2},{7,3},{8,12},{9,13},{10,... | collective-permute-start | bytes 196616 | tf_op jit(solution)/shard_map/ppermute | solution.py:35
  24.7 1.3 %collective-permute-done.7.refs_3_ = f32[128,128]{1,0:T(8,128)S(1)} collective-permute-done((f32[128,128]{1,0:T(8,128)S(1)}, f32[128,128]{1,0:T(8,128)S(1)}, u32[]{:S(2)}, u32[]{:S(2)}) %collective-permute-start.7) | collective-permute-done | bytes 65568 | tf_op jit(solution)/shard_map/ppermute | solution.py:35
  26.0 1.1 %collective-permute-done.6.refs_1_ = f32[128,128]{1,0:T(8,128)S(1)} collective-permute-done((f32[128,128]{1,0:T(8,128)S(1)}, f32[128,128]{1,0:T(8,128)S(1)}, u32[]{:S(2)}, u32[]{:S(2)}) %collective-permute-start.6) | collective-permute-done | bytes 65568 | tf_op jit(solution)/shard_map/ppermute | solution.py:35
  27.1 0.1 shard_map.135
  27.3 0.1 collective-permute-start.11
  27.3 1.2 %collective-permute-done.11.other_ref = f32[32,128]{1,0:T(8,128)S(1)} collective-permute-done((f32[32,128]{1,0:T(8,128)S(1)}, f32[32,128]{1,0:T(8,128)S(1)}, u32[]{:S(2)}, u32[]{:S(2)}) %collective-permute-start.11) | collective-permute-done | bytes 16416 | tf_op jit(solution)/shard_map/ppermute | solution.py:35
  28.5 1.4 %collective-permute-start.12 = (f32[320,128]{1,0:T(8,128)S(1)}, f32[320,128]{1,0:T(8,128)S(1)}, u32[]{:S(2)}, u32[]{:S(2)}) collective-permute-start(f32[320,128]{1,0:T(8,128)S(1)} %get-tuple-element.37), channel_id=1, source_target_pairs={{0,1},{1,0},{2,3},{3,2},{4,5},{5,4},{6,7},{7,6},{8,9},{9,8},{10,11... | collective-permute-start | bytes 491528 | tf_op jit(solution)/shard_map/ppermute | solution.py:35
  29.9 1.4 %collective-permute-start.14 = (f32[32,128]{1,0:T(8,128)S(1)}, f32[32,128]{1,0:T(8,128)S(1)}, u32[]{:S(2)}, u32[]{:S(2)}) collective-permute-start(f32[32,128]{1,0:T(8,128)S(1)} %get-tuple-element.38._), channel_id=1, source_target_pairs={{0,17},{1,16},{2,19},{3,18},{4,21},{5,20},{6,23},{7,22},{8,25},{9,... | collective-permute-start | bytes 49160 | tf_op jit(solution)/shard_map/ppermute | solution.py:35
  31.3 0.7 %collective-permute-start.13 = (f32[8,128]{1,0:T(8,128)S(1)}, f32[8,128]{1,0:T(8,128)S(1)}, u32[]{:S(2)}, u32[]{:S(2)}) collective-permute-start(f32[8,128]{1,0:T(8,128)S(1)} %get-tuple-element.36.refs_0_), channel_id=1, source_target_pairs={{0,16},{1,17},{2,18},{3,19},{4,20},{5,21},{6,22},{7,23},{8,24},{9,... | collective-permute-start | bytes 12296 | tf_op jit(solution)/shard_map/ppermute | solution.py:35
  32.7 0.1 shard_map.137.refs_7_
  32.8 2.1 %collective-permute-done.13.refs_2_ = f32[8,128]{1,0:T(8,128)S(1)} collective-permute-done((f32[8,128]{1,0:T(8,128)S(1)}, f32[8,128]{1,0:T(8,128)S(1)}, u32[]{:S(2)}, u32[]{:S(2)}) %collective-permute-start.13) | collective-permute-done | bytes 4128 | tf_op jit(solution)/shard_map/ppermute | solution.py:35
  34.9 0.0 collective-permute-done.14.refs_3_
  34.9 0.0 collective-permute-done.15.refs_6_
  34.9 0.3 collective-permute-done.12.refs_1_
  35.2 1.3 %shard_map.138 = (f32[64,128]{1,0:T(8,128)}, bf16[512,128]{1,0:T(8,128)(2,1)}, f32[64,128]{1,0:T(8,128)}, f32[64,128]{1,0:T(8,128)}, f32[64,128]{1,0:T(8,128)}, /*index=5*/f32[1,5]{1,0:T(1,128)}, f32[1,5]{1,0:T(1,128)}) custom-call(f32[8,128]{1,0:T(8,128)S(1)} %get-tuple-element.36.refs_0_, f32[320,128]{1,0:T(8,128)S(1)} %collective-permute-done.12.refs_1_, ...), custom_call_target="tpu_custom_call" | custom-call | tf_op jit(solution)/shard_map/pallas_call | solution.py:52
  (6 shorter events, 0.1 us)
Async XLA Ops:
  1.8 1.7 %collective-permute-start = (bf16[1024,128]{1,0:T(8,128)(2,1)S(1)}, bf16[1024,128]{1,0:T(8,128)(2,1)S(1)}, u32[]{:S(2)}, u32[]{:S(2)}) collective-permute-start(bf16[1024,128]{1,0:T(8,128)(2,1)S(1)} %shard_map.127), channel_id=1, source_target_pairs={{0,8},{1,9},{2,10},{3,11},{4,12},{5,13},{6,14},{7,15},{8,0},{9,1},... | collective-permute-start | bytes 786440 | tf_op jit(solution)/shard_map/ppermute | solution.py:35
  3.4 4.6 %copy-start = (s32[8192]{0:T(1024)S(1)}, s32[8192]{0:T(1024)}, u32[]{:S(2)}) copy-start(s32[8192]{0:T(1024)} %param.8) | copy-start | bytes 98308
  3.4 4.6 %copy-start.1 = (s32[8192]{0:T(1024)S(1)}, s32[8192]{0:T(1024)}, u32[]{:S(2)}) copy-start(s32[8192]{0:T(1024)} %param.9) | copy-start | bytes 98308
  3.4 4.6 %copy-start.2 = (f32[8192]{0:T(1024)S(1)}, f32[8192]{0:T(1024)}, u32[]{:S(2)}) copy-start(f32[8192]{0:T(1024)} %param.12) | copy-start | bytes 98308
  3.5 9.3 %collective-permute-start.1 = (f32[256,128]{1,0:T(8,128)S(1)}, f32[256,128]{1,0:T(8,128)S(1)}, u32[]{:S(2)}, u32[]{:S(2)}) collective-permute-start(f32[256,128]{1,0:T(8,128)S(1)} %get-tuple-element.28), channel_id=1, source_target_pairs={{0,1},{1,0},{2,3},{3,2},{4,5},{5,4},{6,7},{7,6},{8,9},{9,8},{10,11... | collective-permute-start | bytes 393224 | tf_op jit(solution)/shard_map/ppermute | solution.py:35
  6.5 7.0 %collective-permute-start.2 = (f32[256,128]{1,0:T(8,128)S(1)}, f32[256,128]{1,0:T(8,128)S(1)}, u32[]{:S(2)}, u32[]{:S(2)}) collective-permute-start(f32[256,128]{1,0:T(8,128)S(1)} %get-tuple-element.29), channel_id=1, source_target_pairs={{0,16},{1,17},{2,18},{3,19},{4,20},{5,21},{6,22},{7,23},{8,24},{9,... | collective-permute-start | bytes 393224 | tf_op jit(solution)/shard_map/ppermute | solution.py:35
  7.9 6.4 %collective-permute-start.3 = (f32[256,128]{1,0:T(8,128)S(1)}, f32[256,128]{1,0:T(8,128)S(1)}, u32[]{:S(2)}, u32[]{:S(2)}) collective-permute-start(f32[256,128]{1,0:T(8,128)S(1)} %get-tuple-element.30), channel_id=1, source_target_pairs={{0,17},{1,16},{2,19},{3,18},{4,21},{5,20},{6,23},{7,22},{8,25},{9,... | collective-permute-start | bytes 393224 | tf_op jit(solution)/shard_map/ppermute | solution.py:35
  8.0 0.7 %copy-start.3 = (f32[5]{0:T(128)S(1)}, f32[5]{0:T(128)}, u32[]{:S(2)}) copy-start(f32[5]{0:T(128)} %param.10) | copy-start | bytes 64
  8.0 0.7 %copy-start.4 = (f32[5]{0:T(128)S(1)}, f32[5]{0:T(128)}, u32[]{:S(2)}) copy-start(f32[5]{0:T(128)} %param.11) | copy-start | bytes 64
  8.7 10.0 %collective-permute-start.9 = (f32[1,136,128]{2,1,0:T(8,128)S(1)}, f32[1,136,128]{2,1,0:T(8,128)S(1)}, u32[]{:S(2)}, u32[]{:S(2)}) collective-permute-start(f32[1,136,128]{2,1,0:T(8,128)S(1)} %shard_map.132.refs_0_), channel_id=1, source_target_pairs={{0,6},{1,7},{2,4},{3,5},{4,2},{5,3},{6,0},{7,1},{8,14},{9,15},{10,... | collective-permute-start | bytes 208904 | tf_op jit(solution)/shard_map/ppermute | solution.py:35
  12.8 6.9 %collective-permute-start.8 = (f32[1,136,128]{2,1,0:T(8,128)S(1)}, f32[1,136,128]{2,1,0:T(8,128)S(1)}, u32[]{:S(2)}, u32[]{:S(2)}) collective-permute-start(f32[1,136,128]{2,1,0:T(8,128)S(1)} %shard_map.132.refs_0_), channel_id=1, source_target_pairs={{0,4},{1,5},{2,6},{3,7},{4,0},{5,1},{6,2},{7,3},{8,12},{9,13},{10,... | collective-permute-start | bytes 208904 | tf_op jit(solution)/shard_map/ppermute | solution.py:35
  12.8 6.9 %collective-permute-start.10 = (f32[1,136,128]{2,1,0:T(8,128)S(1)}, f32[1,136,128]{2,1,0:T(8,128)S(1)}, u32[]{:S(2)}, u32[]{:S(2)}) collective-permute-start(f32[1,136,128]{2,1,0:T(8,128)S(1)} %shard_map.132.refs_0_), channel_id=1, source_target_pairs={{0,2},{1,3},{2,0},{3,1},{4,6},{5,7},{6,4},{7,5},{8,10},{9,11},{10,... | collective-permute-start | bytes 208904 | tf_op jit(solution)/shard_map/ppermute | solution.py:35
  14.4 7.1 %collective-permute-start.5 = (f32[128,128]{1,0:T(8,128)S(1)}, f32[128,128]{1,0:T(8,128)S(1)}, u32[]{:S(2)}, u32[]{:S(2)}) collective-permute-start(f32[128,128]{1,0:T(8,128)S(1)} %get-tuple-element.32.mine_ref), channel_id=1, source_target_pairs={{0,4},{1,5},{2,6},{3,7},{4,0},{5,1},{6,2},{7,3},{8,12},{9,13},{10,... | collective-permute-start | bytes 196616 | tf_op jit(solution)/shard_map/ppermute | solution.py:35
  17.2 4.7 %collective-permute-start.4 = (f32[128,128]{1,0:T(8,128)S(1)}, f32[128,128]{1,0:T(8,128)S(1)}, u32[]{:S(2)}, u32[]{:S(2)}) collective-permute-start(f32[128,128]{1,0:T(8,128)S(1)} %get-tuple-element.31._.mine_ref.x_ref), channel_id=1, source_target_pairs={{0,2},{1,3},{2,0},{3,1},{4,6},{5,7},{6,4},{7,5},{8,10},{9,11},{10,... | collective-permute-start | bytes 196616 | tf_op jit(solution)/shard_map/ppermute | solution.py:35
  19.8 15.2 %collective-permute-start.15 = (f32[4,128,128]{2,1,0:T(8,128)S(1)}, f32[4,128,128]{2,1,0:T(8,128)S(1)}, u32[]{:S(2)}, u32[]{:S(2)}) collective-permute-start(f32[4,128,128]{2,1,0:T(8,128)S(1)} %get-tuple-element.39), channel_id=1, source_target_pairs={{0,1},{1,0},{2,3},{3,2},{4,5},{5,4},{6,7},{7,6},{8,9},{9,8},{10,11... | collective-permute-start | bytes 786440 | tf_op jit(solution)/shard_map/ppermute | solution.py:35
  21.4 4.6 %collective-permute-start.7 = (f32[128,128]{1,0:T(8,128)S(1)}, f32[128,128]{1,0:T(8,128)S(1)}, u32[]{:S(2)}, u32[]{:S(2)}) collective-permute-start(f32[128,128]{1,0:T(8,128)S(1)} %shard_map.130._.refs_2_), channel_id=1, source_target_pairs={{0,2},{1,3},{2,0},{3,1},{4,6},{5,7},{6,4},{7,5},{8,10},{9,11},{10,... | collective-permute-start | bytes 196616 | tf_op jit(solution)/shard_map/ppermute | solution.py:35
  21.9 5.2 %collective-permute-start.6 = (f32[128,128]{1,0:T(8,128)S(1)}, f32[128,128]{1,0:T(8,128)S(1)}, u32[]{:S(2)}, u32[]{:S(2)}) collective-permute-start(f32[128,128]{1,0:T(8,128)S(1)} %shard_map.131.refs_0_), channel_id=1, source_target_pairs={{0,4},{1,5},{2,6},{3,7},{4,0},{5,1},{6,2},{7,3},{8,12},{9,13},{10,... | collective-permute-start | bytes 196616 | tf_op jit(solution)/shard_map/ppermute | solution.py:35
  27.3 1.2 %collective-permute-start.11 = (f32[32,128]{1,0:T(8,128)S(1)}, f32[32,128]{1,0:T(8,128)S(1)}, u32[]{:S(2)}, u32[]{:S(2)}) collective-permute-start(f32[32,128]{1,0:T(8,128)S(1)} %get-tuple-element.34.mine_ref), channel_id=1, source_target_pairs={{0,8},{1,9},{2,10},{3,11},{4,12},{5,13},{6,14},{7,15},{8,0},{9,1},... | collective-permute-start | bytes 49160 | tf_op jit(solution)/shard_map/ppermute | solution.py:35
  28.5 6.7 %collective-permute-start.12 = (f32[320,128]{1,0:T(8,128)S(1)}, f32[320,128]{1,0:T(8,128)S(1)}, u32[]{:S(2)}, u32[]{:S(2)}) collective-permute-start(f32[320,128]{1,0:T(8,128)S(1)} %get-tuple-element.37), channel_id=1, source_target_pairs={{0,1},{1,0},{2,3},{3,2},{4,5},{5,4},{6,7},{7,6},{8,9},{9,8},{10,11... | collective-permute-start | bytes 491528 | tf_op jit(solution)/shard_map/ppermute | solution.py:35
  29.9 5.0 %collective-permute-start.14 = (f32[32,128]{1,0:T(8,128)S(1)}, f32[32,128]{1,0:T(8,128)S(1)}, u32[]{:S(2)}, u32[]{:S(2)}) collective-permute-start(f32[32,128]{1,0:T(8,128)S(1)} %get-tuple-element.38._), channel_id=1, source_target_pairs={{0,17},{1,16},{2,19},{3,18},{4,21},{5,20},{6,23},{7,22},{8,25},{9,... | collective-permute-start | bytes 49160 | tf_op jit(solution)/shard_map/ppermute | solution.py:35
  31.3 3.6 %collective-permute-start.13 = (f32[8,128]{1,0:T(8,128)S(1)}, f32[8,128]{1,0:T(8,128)S(1)}, u32[]{:S(2)}, u32[]{:S(2)}) collective-permute-start(f32[8,128]{1,0:T(8,128)S(1)} %get-tuple-element.36.refs_0_), channel_id=1, source_target_pairs={{0,16},{1,17},{2,18},{3,19},{4,20},{5,21},{6,22},{7,23},{8,24},{9,... | collective-permute-start | bytes 12296 | tf_op jit(solution)/shard_map/ppermute | solution.py:35

commit v5 on v4

--- a/solution.py
+++ b/solution.py
@@ -207,18 +207,14 @@
         edge(plan.zs - 1, plan.rows - EDGE)
 
 
-def core_kernel(plan, mine_ref, other_ref, sum_ref, state_ref, norm_ref, relay_ref, wide_ref):
+def core_kernel(mine_ref, other_ref, sum_ref, norm_ref, relay_ref, wide_ref):
     norm = mine_ref[0:8, :] + other_ref[0:8, :]
     norm_ref[...] = norm
     size = relay_ref.shape[0]
     for ref in (relay_ref, wide_ref):
         ref[0:8, :] = norm
         ref[8:size, :] = other_ref[8:, :]
-    end = size + sum_ref.shape[0]
-    wide_ref[size:end, :] = sum_ref[...]
-    scales = state_ref.shape[1] - 2 * plan.rows
-    for z in range(plan.zs):
-        wide_ref[end + z * scales : end + (z + 1) * scales, :] = state_ref[z, 2 * plan.rows :, :]
+    wide_ref[size:, :] = sum_ref[...]
 
 
 def main_kernel(plan, total_params, *refs):
@@ -226,8 +222,7 @@
     (sum_mine, state_mine, state_other, fix_ref) = refs[:4]
     (master_out, weights_out, update_out, mn_out, vn_out, mt_out, vt_out) = refs[4:11]
     m_buf, v_buf, far = refs[11:]
-    sums_at, scales_at = 8 + 3 * EDGE, 8 + 3 * EDGE + plan.zs * plan.rows
-    sum_other = norms[1].at[sums_at:scales_at]
+    sum_other = norms[1].at[pl.ds(8 + 3 * EDGE, plan.zs * plan.rows)]
     x, core, z, y = place()
     rows = plan.rows
     slots = mt_out.shape[1]
@@ -237,8 +232,7 @@
         return state_mine.at[k, 2 * rows :]
 
     def scales_other(k):
-        size = scale_rows(slots)
-        return norms[1].at[pl.ds(scales_at + k * size, size)]
+        return state_other.at[k, 2 * rows :]
 
     first, second = fix_ref[0:1, :], fix_ref[1:2, :]
 
@@ -372,7 +366,7 @@
     gate = call(token_kernel, struct((8, LANES), F32), [gate, *near[2:]], [VMEM] + [ANY] * (zs - 2))
     state_mine, state_send = call(
         functools.partial(order_kernel, plan),
-        [struct((zs, *state_shape), F32), struct((zs, 2 * rows, LANES), F32)],
+        [struct((zs, *state_shape), F32), struct((zs, *state_shape), F32)],
         [gate, *near],
         [ANY] + [VMEM] * zs,
     )
@@ -384,11 +378,11 @@
         [low, low_other, high, high_other, state_mine],
     )
 
-    wide_rows = send_rows + zs * (rows + scale_rows(slots))
+    wide_rows = send_rows + zs * rows
     norm, relay, wide = call(
-        functools.partial(core_kernel, plan),
+        core_kernel,
         [struct((n, LANES), F32) for n in (8, send_rows, wide_rows)],
-        [send, plan.swap(send, core=1), sum_mine, state_mine],
+        [send, plan.swap(send, core=1), sum_mine],
     )
     wide = plan.swap(wide, group=1)
     norms = [norm, wide] + [plan.swap(relay if k % 2 else norm, group=k) for k in range(2, groups)]

time: 36.7 us -> 36.4 us (level)
  transfers between devices with their start and end apart: 16 -> 16, of which waited for: 8 -> 7; matrix products, arithmetic and copies ran while one was open for 0% -> 0% of each run, Pallas kernels for 4% -> 4%
where the time goes in v5:
time: 36.4 us; the launch traced here: 36.2 us
  starting transfers between devices  22.6 us (62%)
  waiting for transfers between devices  7.62 us (21%)
  Pallas kernels  3.97 us (11%)
  between operations  1.38 us (4%)
  local copies, waits for them, and re-layouts  0.66 us (2%)
    ppermute x16, starting transfers between devices, swap(): lax.ppermute(value, ALL, [(i, i ^ mask) for i in range(self.devices)])  22.6 us
    ppermute x16, waiting for transfers between devices, swap(): lax.ppermute(value, ALL, [(i, i ^ mask) for i in range(self.devices)])  7.62 us
    pallas_call x13, Pallas kernels, call(): pl.pallas_call(kernel, out_shape=outs, in_specs=in_specs or [VMEM] * len(...  3.97 us
  transfers between devices with their start and end apart: 16, of which 7 were waited for; matrix products, arithmetic and copies ran while one was open for 0% of the time, Pallas kernels for 4%

profile of v5, /device:TPU:0, one launch (start us, length us, event | category | flops | bytes accessed | tf_op | source)
XLA Modules:
  0.0 36.2 jit_solution(379390653378035687)
XLA Ops:
  0.6 1.1 %shard_map.127 = bf16[1024,128]{1,0:T(8,128)(2,1)S(1)} custom-call(bf16[1,262144]{1,0:T(2,128)(2,1)} %bitcast.20), custom_call_target="tpu_custom_call" | custom-call | tf_op jit(solution)/shard_map/pallas_call | solution.py:52
  1.8 0.5 %collective-permute-start = (bf16[1024,128]{1,0:T(8,128)(2,1)S(1)}, bf16[1024,128]{1,0:T(8,128)(2,1)S(1)}, u32[]{:S(2)}, u32[]{:S(2)}) collective-permute-start(bf16[1024,128]{1,0:T(8,128)(2,1)S(1)} %shard_map.127), channel_id=1, source_target_pairs={{0,8},{1,9},{2,10},{3,11},{4,12},{5,13},{6,14},{7,15},{8,0},{9,1},... | collective-permute-start | bytes 786440 | tf_op jit(solution)/shard_map/ppermute | solution.py:35
  2.3 1.1 %shard_map.126.mine_ref = bf16[1024,128]{1,0:T(8,128)(2,1)S(1)} custom-call(bf16[1,262144]{1,0:T(2,128)(2,1)} %bitcast.21), custom_call_target="tpu_custom_call" | custom-call | tf_op jit(solution)/shard_map/pallas_call | solution.py:52
  3.4 0.1 collective-permute-done.other_ref
  3.4 0.0 copy-start
  3.4 0.0 copy-start.1
  3.4 0.0 copy-start.2
  3.4 0.1 shard_map.128
  3.5 2.9 %collective-permute-start.1 = (f32[256,128]{1,0:T(8,128)S(1)}, f32[256,128]{1,0:T(8,128)S(1)}, u32[]{:S(2)}, u32[]{:S(2)}) collective-permute-start(f32[256,128]{1,0:T(8,128)S(1)} %get-tuple-element.28), channel_id=1, source_target_pairs={{0,1},{1,0},{2,3},{3,2},{4,5},{5,4},{6,7},{7,6},{8,9},{9,8},{10,11... | collective-permute-start | bytes 393224 | tf_op jit(solution)/shard_map/ppermute | solution.py:35
  6.5 1.5 %collective-permute-start.2 = (f32[256,128]{1,0:T(8,128)S(1)}, f32[256,128]{1,0:T(8,128)S(1)}, u32[]{:S(2)}, u32[]{:S(2)}) collective-permute-start(f32[256,128]{1,0:T(8,128)S(1)} %get-tuple-element.29), channel_id=1, source_target_pairs={{0,16},{1,17},{2,18},{3,19},{4,20},{5,21},{6,22},{7,23},{8,24},{9,... | collective-permute-start | bytes 393224 | tf_op jit(solution)/shard_map/ppermute | solution.py:35
  7.9 0.0 collective-permute-start.3
  8.0 0.0 copy-start.3
  8.0 0.0 copy-start.4
  8.0 0.0 copy-done
  8.0 0.0 copy-done.1
  8.0 0.0 copy-done.2
  8.0 0.6 %copy-done.3 = f32[5]{0:T(128)S(1)} copy-done((f32[5]{0:T(128)S(1)}, f32[5]{0:T(128)}, u32[]{:S(2)}) %copy-start.3) | copy-done | bytes 44
  8.6 0.0 copy-done.4
  8.7 0.1 shard_map.132.refs_0_
  8.7 4.1 %collective-permute-start.9 = (f32[1,136,128]{2,1,0:T(8,128)S(1)}, f32[1,136,128]{2,1,0:T(8,128)S(1)}, u32[]{:S(2)}, u32[]{:S(2)}) collective-permute-start(f32[1,136,128]{2,1,0:T(8,128)S(1)} %shard_map.132.refs_0_), channel_id=1, source_target_pairs={{0,6},{1,7},{2,4},{3,5},{4,2},{5,3},{6,0},{7,1},{8,14},{9,15},{10,... | collective-permute-start | bytes 208904 | tf_op jit(solution)/shard_map/ppermute | solution.py:35
  12.8 0.0 collective-permute-start.8
  12.8 0.0 collective-permute-done.1.refs_1_
  12.8 0.6 %collective-permute-start.10 = (f32[1,136,128]{2,1,0:T(8,128)S(1)}, f32[1,136,128]{2,1,0:T(8,128)S(1)}, u32[]{:S(2)}, u32[]{:S(2)}) collective-permute-start(f32[1,136,128]{2,1,0:T(8,128)S(1)} %shard_map.132.refs_0_), channel_id=1, source_target_pairs={{0,2},{1,3},{2,0},{3,1},{4,6},{5,7},{6,4},{7,5},{8,10},{9,11},{10,... | collective-permute-start | bytes 208904 | tf_op jit(solution)/shard_map/ppermute | solution.py:35
  13.5 0.0 collective-permute-done.2.refs_2_
  13.5 0.8 %collective-permute-done.3.refs_3_ = f32[256,128]{1,0:T(8,128)S(1)} collective-permute-done((f32[256,128]{1,0:T(8,128)S(1)}, f32[256,128]{1,0:T(8,128)S(1)}, u32[]{:S(2)}, u32[]{:S(2)}) %collective-permute-start.3) | collective-permute-done | bytes 131104 | tf_op jit(solution)/shard_map/ppermute | solution.py:35
  14.4 2.8 %collective-permute-start.5 = (f32[128,128]{1,0:T(8,128)S(1)}, f32[128,128]{1,0:T(8,128)S(1)}, u32[]{:S(2)}, u32[]{:S(2)}) collective-permute-start(f32[128,128]{1,0:T(8,128)S(1)} %get-tuple-element.32.mine_ref), channel_id=1, source_target_pairs={{0,4},{1,5},{2,6},{3,7},{4,0},{5,1},{6,2},{7,3},{8,12},{9,13},{10,... | collective-permute-start | bytes 196616 | tf_op jit(solution)/shard_map/ppermute | solution.py:35
  17.2 1.6 %collective-permute-start.4 = (f32[128,128]{1,0:T(8,128)S(1)}, f32[128,128]{1,0:T(8,128)S(1)}, u32[]{:S(2)}, u32[]{:S(2)}) collective-permute-start(f32[128,128]{1,0:T(8,128)S(1)} %get-tuple-element.31._.mine_ref.x_ref), channel_id=1, source_target_pairs={{0,2},{1,3},{2,0},{3,1},{4,6},{5,7},{6,4},{7,5},{8,10},{9,11},{10,... | collective-permute-start | bytes 196616 | tf_op jit(solution)/shard_map/ppermute | solution.py:35
  18.7 0.0 collective-permute-done.9.refs_1_.refs_3_
  18.7 1.0 %collective-permute-done.8.refs_0_.refs_2_ = f32[1,136,128]{2,1,0:T(8,128)S(1)} collective-permute-done((f32[1,136,128]{2,1,0:T(8,128)S(1)}, f32[1,136,128]{2,1,0:T(8,128)S(1)}, u32[]{:S(2)}, u32[]{:S(2)}) %collective-permute-start.8) | collective-permute-done | bytes 69664 | tf_op jit(solution)/shard_map/ppermute | solution.py:35
  19.7 0.0 collective-permute-done.10.refs_1_
  19.8 1.7 %collective-permute-start.15 = (f32[4,136,128]{2,1,0:T(8,128)S(1)}, f32[4,136,128]{2,1,0:T(8,128)S(1)}, u32[]{:S(2)}, u32[]{:S(2)}) collective-permute-start(f32[4,136,128]{2,1,0:T(8,128)S(1)} %get-tuple-element.39), channel_id=1, source_target_pairs={{0,1},{1,0},{2,3},{3,2},{4,5},{5,4},{6,7},{7,6},{8,9},{9,8},{10,11... | collective-permute-start | bytes 835592 | tf_op jit(solution)/shard_map/ppermute | solution.py:35
  21.4 0.0 collective-permute-done.5.other_ref
  21.4 0.4 %collective-permute-start.7 = (f32[128,128]{1,0:T(8,128)S(1)}, f32[128,128]{1,0:T(8,128)S(1)}, u32[]{:S(2)}, u32[]{:S(2)}) collective-permute-start(f32[128,128]{1,0:T(8,128)S(1)} %shard_map.130._.refs_2_), channel_id=1, source_target_pairs={{0,2},{1,3},{2,0},{3,1},{4,6},{5,7},{6,4},{7,5},{8,10},{9,11},{10,... | collective-permute-start | bytes 196616 | tf_op jit(solution)/shard_map/ppermute | solution.py:35
  21.9 0.0 collective-permute-done.4.other_ref
  21.9 2.8 %collective-permute-start.6 = (f32[128,128]{1,0:T(8,128)S(1)}, f32[128,128]{1,0:T(8,128)S(1)}, u32[]{:S(2)}, u32[]{:S(2)}) collective-permute-start(f32[128,128]{1,0:T(8,128)S(1)} %shard_map.131.refs_0_), channel_id=1, source_target_pairs={{0,4},{1,5},{2,6},{3,7},{4,0},{5,1},{6,2},{7,3},{8,12},{9,13},{10,... | collective-permute-start | bytes 196616 | tf_op jit(solution)/shard_map/ppermute | solution.py:35
  24.7 1.4 %collective-permute-done.7.refs_3_ = f32[128,128]{1,0:T(8,128)S(1)} collective-permute-done((f32[128,128]{1,0:T(8,128)S(1)}, f32[128,128]{1,0:T(8,128)S(1)}, u32[]{:S(2)}, u32[]{:S(2)}) %collective-permute-start.7) | collective-permute-done | bytes 65568 | tf_op jit(solution)/shard_map/ppermute | solution.py:35
  26.0 1.1 %collective-permute-done.6.refs_1_ = f32[128,128]{1,0:T(8,128)S(1)} collective-permute-done((f32[128,128]{1,0:T(8,128)S(1)}, f32[128,128]{1,0:T(8,128)S(1)}, u32[]{:S(2)}, u32[]{:S(2)}) %collective-permute-start.6) | collective-permute-done | bytes 65568 | tf_op jit(solution)/shard_map/ppermute | solution.py:35
  27.1 0.1 shard_map.135
  27.3 0.1 collective-permute-start.11
  27.3 1.2 %collective-permute-done.11.other_ref = f32[32,128]{1,0:T(8,128)S(1)} collective-permute-done((f32[32,128]{1,0:T(8,128)S(1)}, f32[32,128]{1,0:T(8,128)S(1)}, u32[]{:S(2)}, u32[]{:S(2)}) %collective-permute-start.11) | collective-permute-done | bytes 16416 | tf_op jit(solution)/shard_map/ppermute | solution.py:35
  28.5 1.4 %collective-permute-start.12 = (f32[288,128]{1,0:T(8,128)S(1)}, f32[288,128]{1,0:T(8,128)S(1)}, u32[]{:S(2)}, u32[]{:S(2)}) collective-permute-start(f32[288,128]{1,0:T(8,128)S(1)} %get-tuple-element.37), channel_id=1, source_target_pairs={{0,1},{1,0},{2,3},{3,2},{4,5},{5,4},{6,7},{7,6},{8,9},{9,8},{10,11... | collective-permute-start | bytes 442376 | tf_op jit(solution)/shard_map/ppermute | solution.py:35
  29.9 1.4 %collective-permute-start.14 = (f32[32,128]{1,0:T(8,128)S(1)}, f32[32,128]{1,0:T(8,128)S(1)}, u32[]{:S(2)}, u32[]{:S(2)}) collective-permute-start(f32[32,128]{1,0:T(8,128)S(1)} %get-tuple-element.38._), channel_id=1, source_target_pairs={{0,17},{1,16},{2,19},{3,18},{4,21},{5,20},{6,23},{7,22},{8,25},{9,... | collective-permute-start | bytes 49160 | tf_op jit(solution)/shard_map/ppermute | solution.py:35
  31.3 0.7 %collective-permute-start.13 = (f32[8,128]{1,0:T(8,128)S(1)}, f32[8,128]{1,0:T(8,128)S(1)}, u32[]{:S(2)}, u32[]{:S(2)}) collective-permute-start(f32[8,128]{1,0:T(8,128)S(1)} %get-tuple-element.36.refs_0_), channel_id=1, source_target_pairs={{0,16},{1,17},{2,18},{3,19},{4,20},{5,21},{6,22},{7,23},{8,24},{9,... | collective-permute-start | bytes 12296 | tf_op jit(solution)/shard_map/ppermute | solution.py:35
  32.7 0.1 shard_map.137.refs_7_
  32.8 2.1 %collective-permute-done.13.refs_2_ = f32[8,128]{1,0:T(8,128)S(1)} collective-permute-done((f32[8,128]{1,0:T(8,128)S(1)}, f32[8,128]{1,0:T(8,128)S(1)}, u32[]{:S(2)}, u32[]{:S(2)}) %collective-permute-start.13) | collective-permute-done | bytes 4128 | tf_op jit(solution)/shard_map/ppermute | solution.py:35
  34.9 0.0 collective-permute-done.14.refs_3_
  34.9 0.0 collective-permute-done.15.refs_6_
  34.9 0.0 collective-permute-done.12.refs_1_
  35.0 1.3 %shard_map.138 = (f32[64,128]{1,0:T(8,128)}, bf16[512,128]{1,0:T(8,128)(2,1)}, f32[64,128]{1,0:T(8,128)}, f32[64,128]{1,0:T(8,128)}, f32[64,128]{1,0:T(8,128)}, /*index=5*/f32[1,5]{1,0:T(1,128)}, f32[1,5]{1,0:T(1,128)}) custom-call(f32[8,128]{1,0:T(8,128)S(1)} %get-tuple-element.36.refs_0_, f32[288,128]{1,0:T(8,128)S(1)} %collective-permute-done.12.refs_1_, ...), custom_call_target="tpu_custom_call" | custom-call | tf_op jit(solution)/shard_map/pallas_call | solution.py:52
  (6 shorter events, 0.1 us)
Async XLA Ops:
  1.8 1.7 %collective-permute-start = (bf16[1024,128]{1,0:T(8,128)(2,1)S(1)}, bf16[1024,128]{1,0:T(8,128)(2,1)S(1)}, u32[]{:S(2)}, u32[]{:S(2)}) collective-permute-start(bf16[1024,128]{1,0:T(8,128)(2,1)S(1)} %shard_map.127), channel_id=1, source_target_pairs={{0,8},{1,9},{2,10},{3,11},{4,12},{5,13},{6,14},{7,15},{8,0},{9,1},... | collective-permute-start | bytes 786440 | tf_op jit(solution)/shard_map/ppermute | solution.py:35
  3.4 4.6 %copy-start = (s32[8192]{0:T(1024)S(1)}, s32[8192]{0:T(1024)}, u32[]{:S(2)}) copy-start(s32[8192]{0:T(1024)} %param.8) | copy-start | bytes 98308
  3.4 4.6 %copy-start.1 = (s32[8192]{0:T(1024)S(1)}, s32[8192]{0:T(1024)}, u32[]{:S(2)}) copy-start(s32[8192]{0:T(1024)} %param.9) | copy-start | bytes 98308
  3.4 4.6 %copy-start.2 = (f32[8192]{0:T(1024)S(1)}, f32[8192]{0:T(1024)}, u32[]{:S(2)}) copy-start(f32[8192]{0:T(1024)} %param.12) | copy-start | bytes 98308
  3.5 9.3 %collective-permute-start.1 = (f32[256,128]{1,0:T(8,128)S(1)}, f32[256,128]{1,0:T(8,128)S(1)}, u32[]{:S(2)}, u32[]{:S(2)}) collective-permute-start(f32[256,128]{1,0:T(8,128)S(1)} %get-tuple-element.28), channel_id=1, source_target_pairs={{0,1},{1,0},{2,3},{3,2},{4,5},{5,4},{6,7},{7,6},{8,9},{9,8},{10,11... | collective-permute-start | bytes 393224 | tf_op jit(solution)/shard_map/ppermute | solution.py:35
  6.5 7.0 %collective-permute-start.2 = (f32[256,128]{1,0:T(8,128)S(1)}, f32[256,128]{1,0:T(8,128)S(1)}, u32[]{:S(2)}, u32[]{:S(2)}) collective-permute-start(f32[256,128]{1,0:T(8,128)S(1)} %get-tuple-element.29), channel_id=1, source_target_pairs={{0,16},{1,17},{2,18},{3,19},{4,20},{5,21},{6,22},{7,23},{8,24},{9,... | collective-permute-start | bytes 393224 | tf_op jit(solution)/shard_map/ppermute | solution.py:35
  7.9 6.4 %collective-permute-start.3 = (f32[256,128]{1,0:T(8,128)S(1)}, f32[256,128]{1,0:T(8,128)S(1)}, u32[]{:S(2)}, u32[]{:S(2)}) collective-permute-start(f32[256,128]{1,0:T(8,128)S(1)} %get-tuple-element.30), channel_id=1, source_target_pairs={{0,17},{1,16},{2,19},{3,18},{4,21},{5,20},{6,23},{7,22},{8,25},{9,... | collective-permute-start | bytes 393224 | tf_op jit(solution)/shard_map/ppermute | solution.py:35
  8.0 0.7 %copy-start.3 = (f32[5]{0:T(128)S(1)}, f32[5]{0:T(128)}, u32[]{:S(2)}) copy-start(f32[5]{0:T(128)} %param.10) | copy-start | bytes 64
  8.0 0.7 %copy-start.4 = (f32[5]{0:T(128)S(1)}, f32[5]{0:T(128)}, u32[]{:S(2)}) copy-start(f32[5]{0:T(128)} %param.11) | copy-start | bytes 64
  8.7 10.0 %collective-permute-start.9 = (f32[1,136,128]{2,1,0:T(8,128)S(1)}, f32[1,136,128]{2,1,0:T(8,128)S(1)}, u32[]{:S(2)}, u32[]{:S(2)}) collective-permute-start(f32[1,136,128]{2,1,0:T(8,128)S(1)} %shard_map.132.refs_0_), channel_id=1, source_target_pairs={{0,6},{1,7},{2,4},{3,5},{4,2},{5,3},{6,0},{7,1},{8,14},{9,15},{10,... | collective-permute-start | bytes 208904 | tf_op jit(solution)/shard_map/ppermute | solution.py:35
  12.8 6.9 %collective-permute-start.8 = (f32[1,136,128]{2,1,0:T(8,128)S(1)}, f32[1,136,128]{2,1,0:T(8,128)S(1)}, u32[]{:S(2)}, u32[]{:S(2)}) collective-permute-start(f32[1,136,128]{2,1,0:T(8,128)S(1)} %shard_map.132.refs_0_), channel_id=1, source_target_pairs={{0,4},{1,5},{2,6},{3,7},{4,0},{5,1},{6,2},{7,3},{8,12},{9,13},{10,... | collective-permute-start | bytes 208904 | tf_op jit(solution)/shard_map/ppermute | solution.py:35
  12.8 6.9 %collective-permute-start.10 = (f32[1,136,128]{2,1,0:T(8,128)S(1)}, f32[1,136,128]{2,1,0:T(8,128)S(1)}, u32[]{:S(2)}, u32[]{:S(2)}) collective-permute-start(f32[1,136,128]{2,1,0:T(8,128)S(1)} %shard_map.132.refs_0_), channel_id=1, source_target_pairs={{0,2},{1,3},{2,0},{3,1},{4,6},{5,7},{6,4},{7,5},{8,10},{9,11},{10,... | collective-permute-start | bytes 208904 | tf_op jit(solution)/shard_map/ppermute | solution.py:35
  14.4 7.1 %collective-permute-start.5 = (f32[128,128]{1,0:T(8,128)S(1)}, f32[128,128]{1,0:T(8,128)S(1)}, u32[]{:S(2)}, u32[]{:S(2)}) collective-permute-start(f32[128,128]{1,0:T(8,128)S(1)} %get-tuple-element.32.mine_ref), channel_id=1, source_target_pairs={{0,4},{1,5},{2,6},{3,7},{4,0},{5,1},{6,2},{7,3},{8,12},{9,13},{10,... | collective-permute-start | bytes 196616 | tf_op jit(solution)/shard_map/ppermute | solution.py:35
  17.2 4.7 %collective-permute-start.4 = (f32[128,128]{1,0:T(8,128)S(1)}, f32[128,128]{1,0:T(8,128)S(1)}, u32[]{:S(2)}, u32[]{:S(2)}) collective-permute-start(f32[128,128]{1,0:T(8,128)S(1)} %get-tuple-element.31._.mine_ref.x_ref), channel_id=1, source_target_pairs={{0,2},{1,3},{2,0},{3,1},{4,6},{5,7},{6,4},{7,5},{8,10},{9,11},{10,... | collective-permute-start | bytes 196616 | tf_op jit(solution)/shard_map/ppermute | solution.py:35
  19.8 15.2 %collective-permute-start.15 = (f32[4,136,128]{2,1,0:T(8,128)S(1)}, f32[4,136,128]{2,1,0:T(8,128)S(1)}, u32[]{:S(2)}, u32[]{:S(2)}) collective-permute-start(f32[4,136,128]{2,1,0:T(8,128)S(1)} %get-tuple-element.39), channel_id=1, source_target_pairs={{0,1},{1,0},{2,3},{3,2},{4,5},{5,4},{6,7},{7,6},{8,9},{9,8},{10,11... | collective-permute-start | bytes 835592 | tf_op jit(solution)/shard_map/ppermute | solution.py:35
  21.4 4.6 %collective-permute-start.7 = (f32[128,128]{1,0:T(8,128)S(1)}, f32[128,128]{1,0:T(8,128)S(1)}, u32[]{:S(2)}, u32[]{:S(2)}) collective-permute-start(f32[128,128]{1,0:T(8,128)S(1)} %shard_map.130._.refs_2_), channel_id=1, source_target_pairs={{0,2},{1,3},{2,0},{3,1},{4,6},{5,7},{6,4},{7,5},{8,10},{9,11},{10,... | collective-permute-start | bytes 196616 | tf_op jit(solution)/shard_map/ppermute | solution.py:35
  21.9 5.2 %collective-permute-start.6 = (f32[128,128]{1,0:T(8,128)S(1)}, f32[128,128]{1,0:T(8,128)S(1)}, u32[]{:S(2)}, u32[]{:S(2)}) collective-permute-start(f32[128,128]{1,0:T(8,128)S(1)} %shard_map.131.refs_0_), channel_id=1, source_target_pairs={{0,4},{1,5},{2,6},{3,7},{4,0},{5,1},{6,2},{7,3},{8,12},{9,13},{10,... | collective-permute-start | bytes 196616 | tf_op jit(solution)/shard_map/ppermute | solution.py:35
  27.3 1.2 %collective-permute-start.11 = (f32[32,128]{1,0:T(8,128)S(1)}, f32[32,128]{1,0:T(8,128)S(1)}, u32[]{:S(2)}, u32[]{:S(2)}) collective-permute-start(f32[32,128]{1,0:T(8,128)S(1)} %get-tuple-element.34.mine_ref), channel_id=1, source_target_pairs={{0,8},{1,9},{2,10},{3,11},{4,12},{5,13},{6,14},{7,15},{8,0},{9,1},... | collective-permute-start | bytes 49160 | tf_op jit(solution)/shard_map/ppermute | solution.py:35
  28.5 6.4 %collective-permute-start.12 = (f32[288,128]{1,0:T(8,128)S(1)}, f32[288,128]{1,0:T(8,128)S(1)}, u32[]{:S(2)}, u32[]{:S(2)}) collective-permute-start(f32[288,128]{1,0:T(8,128)S(1)} %get-tuple-element.37), channel_id=1, source_target_pairs={{0,1},{1,0},{2,3},{3,2},{4,5},{5,4},{6,7},{7,6},{8,9},{9,8},{10,11... | collective-permute-start | bytes 442376 | tf_op jit(solution)/shard_map/ppermute | solution.py:35
  29.9 5.0 %collective-permute-start.14 = (f32[32,128]{1,0:T(8,128)S(1)}, f32[32,128]{1,0:T(8,128)S(1)}, u32[]{:S(2)}, u32[]{:S(2)}) collective-permute-start(f32[32,128]{1,0:T(8,128)S(1)} %get-tuple-element.38._), channel_id=1, source_target_pairs={{0,17},{1,16},{2,19},{3,18},{4,21},{5,20},{6,23},{7,22},{8,25},{9,... | collective-permute-start | bytes 49160 | tf_op jit(solution)/shard_map/ppermute | solution.py:35
  31.3 3.6 %collective-permute-start.13 = (f32[8,128]{1,0:T(8,128)S(1)}, f32[8,128]{1,0:T(8,128)S(1)}, u32[]{:S(2)}, u32[]{:S(2)}) collective-permute-start(f32[8,128]{1,0:T(8,128)S(1)} %get-tuple-element.36.refs_0_), channel_id=1, source_target_pairs={{0,16},{1,17},{2,18},{3,19},{4,20},{5,21},{6,22},{7,23},{8,24},{9,... | collective-permute-start | bytes 12296 | tf_op jit(solution)/shard_map/ppermute | solution.py:35

commit v6 on v5

--- a/solution.py
+++ b/solution.py
@@ -148,8 +148,10 @@
 
 def decayed(state, scales, low, high):
     slot = (low + EDGE) // (2 * EDGE)
-    scale = scales[slot : slot + 1, :]
-    pair = state[low:high, :]
+    return decode(state[low:high, :], scales[slot : slot + 1, :])
+
+
+def decode(pair, scale):
     v_code = jnp.floor(pair * (1.0 / 256.0))
     m_code = pair - (v_code * 256.0 + 128.0)
     m_scale, v_scale = scale[:, 0:1] * (0.9 / 127.0), scale[:, LANES // 2 : LANES // 2 + 1] * (0.95 / 255.0)
@@ -221,7 +223,7 @@
     norms, refs = refs[: plan.groups], refs[plan.groups :]
     (sum_mine, state_mine, state_other, fix_ref) = refs[:4]
     (master_out, weights_out, update_out, mn_out, vn_out, mt_out, vt_out) = refs[4:11]
-    m_buf, v_buf, far = refs[11:]
+    m_buf, v_buf = refs[11:]
     sum_other = norms[1].at[pl.ds(8 + 3 * EDGE, plan.zs * plan.rows)]
     x, core, z, y = place()
     rows = plan.rows
@@ -262,45 +264,24 @@
         m_buf[low:high, :] = m
         v_buf[low:high, :] = v
 
-    far[...] = jnp.zeros_like(far)
-
-    def near(side, at_z, start):
+    def near(at_z, last):
+        start = pl.multiple_of(last * (rows - EDGE), EDGE)
         grad = sum_other[pl.ds(pl.multiple_of(at_z * rows + start, EDGE), EDGE), :]
-        em, ev = moments(grad, *decayed(state_other.at[at_z], scales_other(at_z), start, start + EDGE))
-        far[side, 0], far[side, 1] = jnp.abs(em), jnp.abs(ev)
-
-    def across(side, shard):
-        for k in range(1, plan.groups, 2):
-            @pl.when((shard >= 0) & (shard < plan.shards) & ((x ^ (k >> 1)) == shard // 2))
-            def _():
-                em, ev = moments(*(norms[k][8 + j * EDGE : 8 + (j + 1) * EDGE, :] for j in range(3)))
-                far[side, 0], far[side, 1] = jnp.abs(em), jnp.abs(ev)
-
-    shard = 2 * x + core
-
-    @pl.when(y == 0)
-    def _():
-        near(1, z, 0)
-
-        @pl.when(z > 0)
-        def _():
-            near(0, z - 1, rows - EDGE)
-
-        @pl.when(z == 0)
-        def _():
-            across(0, shard - 1)
-
-    @pl.when(y == 1)
-    def _():
-        near(0, z, rows - EDGE)
-
-        @pl.when(z < plan.zs - 1)
-        def _():
-            near(1, z + 1, 0)
-
-        @pl.when(z == plan.zs - 1)
-        def _():
-            across(1, shard + 1)
+        pair = state_other[at_z, pl.ds(start, EDGE), :]
+        scale = state_other[at_z, pl.ds(2 * rows + last * (slots - 1), 1), :]
+        return grad, *decode(pair, scale)
+
+    beside = [jnp.abs(value) for value in moments(*near(z, y))]
+    next_z, shard = z - 1 + 2 * y, 2 * x + core - 1 + 2 * y
+    inside = (next_z >= 0) & (next_z < plan.zs)
+    terms = near(jnp.clip(next_z, 0, plan.zs - 1), 1 - y)
+    for k in range(1, plan.groups, 2):
+        here = jnp.logical_not(inside) & ((x ^ (k >> 1)) == shard // 2)
+        terms = [jnp.where(here, norms[k][8 + j * EDGE : 8 + (j + 1) * EDGE, :], term) for j, term in enumerate(terms)]
+    exists = inside | ((shard >= 0) & (shard < plan.shards))
+    beyond = [jnp.where(exists, jnp.abs(value), 0.0) for value in moments(*terms)]
+    first_far = [jnp.where(y == 0, p, q) for p, q in zip(beyond, beside)]
+    last_far = [jnp.where(y == 0, q, p) for p, q in zip(beyond, beside)]
 
     lane = lax.broadcasted_iota(jnp.int32, (1, LANES), 1)
     for which, (buf, table, norm_out) in enumerate(((m_buf, mt_out, mn_out), (v_buf, vt_out, vn_out))):
@@ -309,9 +290,9 @@
             values = buf[low:high, :]
             top = jnp.max(jnp.abs(values).reshape(-1, 8, LANES), axis=0)
             if j == 0:
-                top = jnp.maximum(top, far[0, which])
+                top = jnp.maximum(top, first_far[which])
             if j == slots - 1:
-                top = jnp.maximum(top, far[1, which])
+                top = jnp.maximum(top, last_far[which])
             top = jnp.max(top, keepdims=True)
             line = jnp.where(lane == j, top, line)
             norm_out[low:high, :] = values / (top + 1e-06)
@@ -397,7 +378,7 @@
         functools.partial(main_kernel, plan, total_params),
         [own, struct((plan.reps * rows, LANES), BF16), own, own, own, table, table],
         ins,
-        scratch=[pltpu.VMEM(shape, F32), pltpu.VMEM(shape, F32), pltpu.VMEM((2, 2, EDGE, LANES), F32)],
+        scratch=[pltpu.VMEM(shape, F32), pltpu.VMEM(shape, F32)],
     )
     return (
         new_master.reshape(-1),

time: 36.4 us -> 36.3 us (level)
  no operation moved by 1% of the time
where the time goes in v6:
time: 36.3 us; the launch traced here: 36.1 us
  starting transfers between devices  22.6 us (62%)
  waiting for transfers between devices  7.62 us (21%)
  Pallas kernels  3.85 us (11%)
  between operations  1.38 us (4%)
  local copies, waits for them, and re-layouts  0.66 us (2%)
    ppermute x16, starting transfers between devices, swap(): lax.ppermute(value, ALL, [(i, i ^ mask) for i in range(self.devices)])  22.6 us
    ppermute x16, waiting for transfers between devices, swap(): lax.ppermute(value, ALL, [(i, i ^ mask) for i in range(self.devices)])  7.62 us
    pallas_call x13, Pallas kernels, call(): pl.pallas_call(kernel, out_shape=outs, in_specs=in_specs or [VMEM] * len(...  3.85 us
  transfers between devices with their start and end apart: 16, of which 7 were waited for; matrix products, arithmetic and copies ran while one was open for 0% of the time, Pallas kernels for 4%

profile of v6, /device:TPU:0, one launch (start us, length us, event | category | flops | bytes accessed | tf_op | source)
XLA Modules:
  0.0 36.1 jit_solution(17410502027614094479)
XLA Ops:
  0.6 1.1 %shard_map.127 = bf16[1024,128]{1,0:T(8,128)(2,1)S(1)} custom-call(bf16[1,262144]{1,0:T(2,128)(2,1)} %bitcast.20), custom_call_target="tpu_custom_call" | custom-call | tf_op jit(solution)/shard_map/pallas_call | solution.py:52
  1.8 0.5 %collective-permute-start = (bf16[1024,128]{1,0:T(8,128)(2,1)S(1)}, bf16[1024,128]{1,0:T(8,128)(2,1)S(1)}, u32[]{:S(2)}, u32[]{:S(2)}) collective-permute-start(bf16[1024,128]{1,0:T(8,128)(2,1)S(1)} %shard_map.127), channel_id=1, source_target_pairs={{0,8},{1,9},{2,10},{3,11},{4,12},{5,13},{6,14},{7,15},{8,0},{9,1},... | collective-permute-start | bytes 786440 | tf_op jit(solution)/shard_map/ppermute | solution.py:35
  2.3 1.1 %shard_map.126.mine_ref = bf16[1024,128]{1,0:T(8,128)(2,1)S(1)} custom-call(bf16[1,262144]{1,0:T(2,128)(2,1)} %bitcast.21), custom_call_target="tpu_custom_call" | custom-call | tf_op jit(solution)/shard_map/pallas_call | solution.py:52
  3.4 0.1 collective-permute-done.other_ref
  3.4 0.0 copy-start
  3.4 0.0 copy-start.1
  3.4 0.0 copy-start.2
  3.4 0.1 shard_map.128
  3.5 2.9 %collective-permute-start.1 = (f32[256,128]{1,0:T(8,128)S(1)}, f32[256,128]{1,0:T(8,128)S(1)}, u32[]{:S(2)}, u32[]{:S(2)}) collective-permute-start(f32[256,128]{1,0:T(8,128)S(1)} %get-tuple-element.28), channel_id=1, source_target_pairs={{0,1},{1,0},{2,3},{3,2},{4,5},{5,4},{6,7},{7,6},{8,9},{9,8},{10,11... | collective-permute-start | bytes 393224 | tf_op jit(solution)/shard_map/ppermute | solution.py:35
  6.5 1.5 %collective-permute-start.2 = (f32[256,128]{1,0:T(8,128)S(1)}, f32[256,128]{1,0:T(8,128)S(1)}, u32[]{:S(2)}, u32[]{:S(2)}) collective-permute-start(f32[256,128]{1,0:T(8,128)S(1)} %get-tuple-element.29), channel_id=1, source_target_pairs={{0,16},{1,17},{2,18},{3,19},{4,20},{5,21},{6,22},{7,23},{8,24},{9,... | collective-permute-start | bytes 393224 | tf_op jit(solution)/shard_map/ppermute | solution.py:35
  7.9 0.0 collective-permute-start.3
  8.0 0.0 copy-start.3
  8.0 0.0 copy-start.4
  8.0 0.0 copy-done
  8.0 0.0 copy-done.1
  8.0 0.0 copy-done.2
  8.0 0.6 %copy-done.3 = f32[5]{0:T(128)S(1)} copy-done((f32[5]{0:T(128)S(1)}, f32[5]{0:T(128)}, u32[]{:S(2)}) %copy-start.3) | copy-done | bytes 44
  8.6 0.0 copy-done.4
  8.7 0.1 shard_map.132.refs_0_
  8.7 4.1 %collective-permute-start.9 = (f32[1,136,128]{2,1,0:T(8,128)S(1)}, f32[1,136,128]{2,1,0:T(8,128)S(1)}, u32[]{:S(2)}, u32[]{:S(2)}) collective-permute-start(f32[1,136,128]{2,1,0:T(8,128)S(1)} %shard_map.132.refs_0_), channel_id=1, source_target_pairs={{0,6},{1,7},{2,4},{3,5},{4,2},{5,3},{6,0},{7,1},{8,14},{9,15},{10,... | collective-permute-start | bytes 208904 | tf_op jit(solution)/shard_map/ppermute | solution.py:35
  12.8 0.0 collective-permute-start.8
  12.8 0.0 collective-permute-done.1.refs_1_
  12.8 0.6 %collective-permute-start.10 = (f32[1,136,128]{2,1,0:T(8,128)S(1)}, f32[1,136,128]{2,1,0:T(8,128)S(1)}, u32[]{:S(2)}, u32[]{:S(2)}) collective-permute-start(f32[1,136,128]{2,1,0:T(8,128)S(1)} %shard_map.132.refs_0_), channel_id=1, source_target_pairs={{0,2},{1,3},{2,0},{3,1},{4,6},{5,7},{6,4},{7,5},{8,10},{9,11},{10,... | collective-permute-start | bytes 208904 | tf_op jit(solution)/shard_map/ppermute | solution.py:35
  13.5 0.0 collective-permute-done.2.refs_2_
  13.5 0.8 %collective-permute-done.3.refs_3_ = f32[256,128]{1,0:T(8,128)S(1)} collective-permute-done((f32[256,128]{1,0:T(8,128)S(1)}, f32[256,128]{1,0:T(8,128)S(1)}, u32[]{:S(2)}, u32[]{:S(2)}) %collective-permute-start.3) | collective-permute-done | bytes 131104 | tf_op jit(solution)/shard_map/ppermute | solution.py:35
  14.4 2.8 %collective-permute-start.5 = (f32[128,128]{1,0:T(8,128)S(1)}, f32[128,128]{1,0:T(8,128)S(1)}, u32[]{:S(2)}, u32[]{:S(2)}) collective-permute-start(f32[128,128]{1,0:T(8,128)S(1)} %get-tuple-element.32.mine_ref), channel_id=1, source_target_pairs={{0,4},{1,5},{2,6},{3,7},{4,0},{5,1},{6,2},{7,3},{8,12},{9,13},{10,... | collective-permute-start | bytes 196616 | tf_op jit(solution)/shard_map/ppermute | solution.py:35
  17.2 1.6 %collective-permute-start.4 = (f32[128,128]{1,0:T(8,128)S(1)}, f32[128,128]{1,0:T(8,128)S(1)}, u32[]{:S(2)}, u32[]{:S(2)}) collective-permute-start(f32[128,128]{1,0:T(8,128)S(1)} %get-tuple-element.31._.mine_ref.x_ref), channel_id=1, source_target_pairs={{0,2},{1,3},{2,0},{3,1},{4,6},{5,7},{6,4},{7,5},{8,10},{9,11},{10,... | collective-permute-start | bytes 196616 | tf_op jit(solution)/shard_map/ppermute | solution.py:35
  18.7 0.0 collective-permute-done.9.refs_1_.refs_3_
  18.7 1.0 %collective-permute-done.8.refs_0_.refs_2_ = f32[1,136,128]{2,1,0:T(8,128)S(1)} collective-permute-done((f32[1,136,128]{2,1,0:T(8,128)S(1)}, f32[1,136,128]{2,1,0:T(8,128)S(1)}, u32[]{:S(2)}, u32[]{:S(2)}) %collective-permute-start.8) | collective-permute-done | bytes 69664 | tf_op jit(solution)/shard_map/ppermute | solution.py:35
  19.7 0.0 collective-permute-done.10.refs_1_
  19.8 1.7 %collective-permute-start.15 = (f32[4,136,128]{2,1,0:T(8,128)S(1)}, f32[4,136,128]{2,1,0:T(8,128)S(1)}, u32[]{:S(2)}, u32[]{:S(2)}) collective-permute-start(f32[4,136,128]{2,1,0:T(8,128)S(1)} %get-tuple-element.39), channel_id=1, source_target_pairs={{0,1},{1,0},{2,3},{3,2},{4,5},{5,4},{6,7},{7,6},{8,9},{9,8},{10,11... | collective-permute-start | bytes 835592 | tf_op jit(solution)/shard_map/ppermute | solution.py:35
  21.4 0.0 collective-permute-done.5.other_ref
  21.4 0.4 %collective-permute-start.7 = (f32[128,128]{1,0:T(8,128)S(1)}, f32[128,128]{1,0:T(8,128)S(1)}, u32[]{:S(2)}, u32[]{:S(2)}) collective-permute-start(f32[128,128]{1,0:T(8,128)S(1)} %shard_map.130._.refs_2_), channel_id=1, source_target_pairs={{0,2},{1,3},{2,0},{3,1},{4,6},{5,7},{6,4},{7,5},{8,10},{9,11},{10,... | collective-permute-start | bytes 196616 | tf_op jit(solution)/shard_map/ppermute | solution.py:35
  21.9 0.0 collective-permute-done.4.other_ref
  21.9 2.8 %collective-permute-start.6 = (f32[128,128]{1,0:T(8,128)S(1)}, f32[128,128]{1,0:T(8,128)S(1)}, u32[]{:S(2)}, u32[]{:S(2)}) collective-permute-start(f32[128,128]{1,0:T(8,128)S(1)} %shard_map.131.refs_0_), channel_id=1, source_target_pairs={{0,4},{1,5},{2,6},{3,7},{4,0},{5,1},{6,2},{7,3},{8,12},{9,13},{10,... | collective-permute-start | bytes 196616 | tf_op jit(solution)/shard_map/ppermute | solution.py:35
  24.7 1.4 %collective-permute-done.7.refs_3_ = f32[128,128]{1,0:T(8,128)S(1)} collective-permute-done((f32[128,128]{1,0:T(8,128)S(1)}, f32[128,128]{1,0:T(8,128)S(1)}, u32[]{:S(2)}, u32[]{:S(2)}) %collective-permute-start.7) | collective-permute-done | bytes 65568 | tf_op jit(solution)/shard_map/ppermute | solution.py:35
  26.0 1.1 %collective-permute-done.6.refs_1_ = f32[128,128]{1,0:T(8,128)S(1)} collective-permute-done((f32[128,128]{1,0:T(8,128)S(1)}, f32[128,128]{1,0:T(8,128)S(1)}, u32[]{:S(2)}, u32[]{:S(2)}) %collective-permute-start.6) | collective-permute-done | bytes 65568 | tf_op jit(solution)/shard_map/ppermute | solution.py:35
  27.1 0.1 shard_map.135
  27.3 0.1 collective-permute-start.11
  27.3 1.2 %collective-permute-done.11.other_ref = f32[32,128]{1,0:T(8,128)S(1)} collective-permute-done((f32[32,128]{1,0:T(8,128)S(1)}, f32[32,128]{1,0:T(8,128)S(1)}, u32[]{:S(2)}, u32[]{:S(2)}) %collective-permute-start.11) | collective-permute-done | bytes 16416 | tf_op jit(solution)/shard_map/ppermute | solution.py:35
  28.5 1.4 %collective-permute-start.12 = (f32[288,128]{1,0:T(8,128)S(1)}, f32[288,128]{1,0:T(8,128)S(1)}, u32[]{:S(2)}, u32[]{:S(2)}) collective-permute-start(f32[288,128]{1,0:T(8,128)S(1)} %get-tuple-element.37), channel_id=1, source_target_pairs={{0,1},{1,0},{2,3},{3,2},{4,5},{5,4},{6,7},{7,6},{8,9},{9,8},{10,11... | collective-permute-start | bytes 442376 | tf_op jit(solution)/shard_map/ppermute | solution.py:35
  29.9 1.4 %collective-permute-start.14 = (f32[32,128]{1,0:T(8,128)S(1)}, f32[32,128]{1,0:T(8,128)S(1)}, u32[]{:S(2)}, u32[]{:S(2)}) collective-permute-start(f32[32,128]{1,0:T(8,128)S(1)} %get-tuple-element.38._), channel_id=1, source_target_pairs={{0,17},{1,16},{2,19},{3,18},{4,21},{5,20},{6,23},{7,22},{8,25},{9,... | collective-permute-start | bytes 49160 | tf_op jit(solution)/shard_map/ppermute | solution.py:35
  31.3 0.7 %collective-permute-start.13 = (f32[8,128]{1,0:T(8,128)S(1)}, f32[8,128]{1,0:T(8,128)S(1)}, u32[]{:S(2)}, u32[]{:S(2)}) collective-permute-start(f32[8,128]{1,0:T(8,128)S(1)} %get-tuple-element.36.refs_0_), channel_id=1, source_target_pairs={{0,16},{1,17},{2,18},{3,19},{4,20},{5,21},{6,22},{7,23},{8,24},{9,... | collective-permute-start | bytes 12296 | tf_op jit(solution)/shard_map/ppermute | solution.py:35
  32.7 0.1 shard_map.137.refs_7_
  32.8 2.1 %collective-permute-done.13.refs_2_ = f32[8,128]{1,0:T(8,128)S(1)} collective-permute-done((f32[8,128]{1,0:T(8,128)S(1)}, f32[8,128]{1,0:T(8,128)S(1)}, u32[]{:S(2)}, u32[]{:S(2)}) %collective-permute-start.13) | collective-permute-done | bytes 4128 | tf_op jit(solution)/shard_map/ppermute | solution.py:35
  34.9 0.0 collective-permute-done.14.refs_3_
  34.9 0.0 collective-permute-done.15.refs_6_
  34.9 0.0 collective-permute-done.12.refs_1_
  35.0 1.2 %shard_map.138 = (f32[64,128]{1,0:T(8,128)}, bf16[512,128]{1,0:T(8,128)(2,1)}, f32[64,128]{1,0:T(8,128)}, f32[64,128]{1,0:T(8,128)}, f32[64,128]{1,0:T(8,128)}, /*index=5*/f32[1,5]{1,0:T(1,128)}, f32[1,5]{1,0:T(1,128)}) custom-call(f32[8,128]{1,0:T(8,128)S(1)} %get-tuple-element.36.refs_0_, f32[288,128]{1,0:T(8,128)S(1)} %collective-permute-done.12.refs_1_, ...), custom_call_target="tpu_custom_call" | custom-call | tf_op jit(solution)/shard_map/pallas_call | solution.py:52
  (6 shorter events, 0.1 us)
Async XLA Ops:
  1.8 1.7 %collective-permute-start = (bf16[1024,128]{1,0:T(8,128)(2,1)S(1)}, bf16[1024,128]{1,0:T(8,128)(2,1)S(1)}, u32[]{:S(2)}, u32[]{:S(2)}) collective-permute-start(bf16[1024,128]{1,0:T(8,128)(2,1)S(1)} %shard_map.127), channel_id=1, source_target_pairs={{0,8},{1,9},{2,10},{3,11},{4,12},{5,13},{6,14},{7,15},{8,0},{9,1},... | collective-permute-start | bytes 786440 | tf_op jit(solution)/shard_map/ppermute | solution.py:35
  3.4 4.6 %copy-start = (s32[8192]{0:T(1024)S(1)}, s32[8192]{0:T(1024)}, u32[]{:S(2)}) copy-start(s32[8192]{0:T(1024)} %param.8) | copy-start | bytes 98308
  3.4 4.6 %copy-start.1 = (s32[8192]{0:T(1024)S(1)}, s32[8192]{0:T(1024)}, u32[]{:S(2)}) copy-start(s32[8192]{0:T(1024)} %param.9) | copy-start | bytes 98308
  3.4 4.6 %copy-start.2 = (f32[8192]{0:T(1024)S(1)}, f32[8192]{0:T(1024)}, u32[]{:S(2)}) copy-start(f32[8192]{0:T(1024)} %param.12) | copy-start | bytes 98308
  3.5 9.3 %collective-permute-start.1 = (f32[256,128]{1,0:T(8,128)S(1)}, f32[256,128]{1,0:T(8,128)S(1)}, u32[]{:S(2)}, u32[]{:S(2)}) collective-permute-start(f32[256,128]{1,0:T(8,128)S(1)} %get-tuple-element.28), channel_id=1, source_target_pairs={{0,1},{1,0},{2,3},{3,2},{4,5},{5,4},{6,7},{7,6},{8,9},{9,8},{10,11... | collective-permute-start | bytes 393224 | tf_op jit(solution)/shard_map/ppermute | solution.py:35
  6.5 7.0 %collective-permute-start.2 = (f32[256,128]{1,0:T(8,128)S(1)}, f32[256,128]{1,0:T(8,128)S(1)}, u32[]{:S(2)}, u32[]{:S(2)}) collective-permute-start(f32[256,128]{1,0:T(8,128)S(1)} %get-tuple-element.29), channel_id=1, source_target_pairs={{0,16},{1,17},{2,18},{3,19},{4,20},{5,21},{6,22},{7,23},{8,24},{9,... | collective-permute-start | bytes 393224 | tf_op jit(solution)/shard_map/ppermute | solution.py:35
  7.9 6.4 %collective-permute-start.3 = (f32[256,128]{1,0:T(8,128)S(1)}, f32[256,128]{1,0:T(8,128)S(1)}, u32[]{:S(2)}, u32[]{:S(2)}) collective-permute-start(f32[256,128]{1,0:T(8,128)S(1)} %get-tuple-element.30), channel_id=1, source_target_pairs={{0,17},{1,16},{2,19},{3,18},{4,21},{5,20},{6,23},{7,22},{8,25},{9,... | collective-permute-start | bytes 393224 | tf_op jit(solution)/shard_map/ppermute | solution.py:35
  8.0 0.7 %copy-start.3 = (f32[5]{0:T(128)S(1)}, f32[5]{0:T(128)}, u32[]{:S(2)}) copy-start(f32[5]{0:T(128)} %param.10) | copy-start | bytes 64
  8.0 0.7 %copy-start.4 = (f32[5]{0:T(128)S(1)}, f32[5]{0:T(128)}, u32[]{:S(2)}) copy-start(f32[5]{0:T(128)} %param.11) | copy-start | bytes 64
  8.7 10.0 %collective-permute-start.9 = (f32[1,136,128]{2,1,0:T(8,128)S(1)}, f32[1,136,128]{2,1,0:T(8,128)S(1)}, u32[]{:S(2)}, u32[]{:S(2)}) collective-permute-start(f32[1,136,128]{2,1,0:T(8,128)S(1)} %shard_map.132.refs_0_), channel_id=1, source_target_pairs={{0,6},{1,7},{2,4},{3,5},{4,2},{5,3},{6,0},{7,1},{8,14},{9,15},{10,... | collective-permute-start | bytes 208904 | tf_op jit(solution)/shard_map/ppermute | solution.py:35
  12.8 6.9 %collective-permute-start.8 = (f32[1,136,128]{2,1,0:T(8,128)S(1)}, f32[1,136,128]{2,1,0:T(8,128)S(1)}, u32[]{:S(2)}, u32[]{:S(2)}) collective-permute-start(f32[1,136,128]{2,1,0:T(8,128)S(1)} %shard_map.132.refs_0_), channel_id=1, source_target_pairs={{0,4},{1,5},{2,6},{3,7},{4,0},{5,1},{6,2},{7,3},{8,12},{9,13},{10,... | collective-permute-start | bytes 208904 | tf_op jit(solution)/shard_map/ppermute | solution.py:35
  12.8 6.9 %collective-permute-start.10 = (f32[1,136,128]{2,1,0:T(8,128)S(1)}, f32[1,136,128]{2,1,0:T(8,128)S(1)}, u32[]{:S(2)}, u32[]{:S(2)}) collective-permute-start(f32[1,136,128]{2,1,0:T(8,128)S(1)} %shard_map.132.refs_0_), channel_id=1, source_target_pairs={{0,2},{1,3},{2,0},{3,1},{4,6},{5,7},{6,4},{7,5},{8,10},{9,11},{10,... | collective-permute-start | bytes 208904 | tf_op jit(solution)/shard_map/ppermute | solution.py:35
  14.4 7.1 %collective-permute-start.5 = (f32[128,128]{1,0:T(8,128)S(1)}, f32[128,128]{1,0:T(8,128)S(1)}, u32[]{:S(2)}, u32[]{:S(2)}) collective-permute-start(f32[128,128]{1,0:T(8,128)S(1)} %get-tuple-element.32.mine_ref), channel_id=1, source_target_pairs={{0,4},{1,5},{2,6},{3,7},{4,0},{5,1},{6,2},{7,3},{8,12},{9,13},{10,... | collective-permute-start | bytes 196616 | tf_op jit(solution)/shard_map/ppermute | solution.py:35
  17.2 4.7 %collective-permute-start.4 = (f32[128,128]{1,0:T(8,128)S(1)}, f32[128,128]{1,0:T(8,128)S(1)}, u32[]{:S(2)}, u32[]{:S(2)}) collective-permute-start(f32[128,128]{1,0:T(8,128)S(1)} %get-tuple-element.31._.mine_ref.x_ref), channel_id=1, source_target_pairs={{0,2},{1,3},{2,0},{3,1},{4,6},{5,7},{6,4},{7,5},{8,10},{9,11},{10,... | collective-permute-start | bytes 196616 | tf_op jit(solution)/shard_map/ppermute | solution.py:35
  19.8 15.2 %collective-permute-start.15 = (f32[4,136,128]{2,1,0:T(8,128)S(1)}, f32[4,136,128]{2,1,0:T(8,128)S(1)}, u32[]{:S(2)}, u32[]{:S(2)}) collective-permute-start(f32[4,136,128]{2,1,0:T(8,128)S(1)} %get-tuple-element.39), channel_id=1, source_target_pairs={{0,1},{1,0},{2,3},{3,2},{4,5},{5,4},{6,7},{7,6},{8,9},{9,8},{10,11... | collective-permute-start | bytes 835592 | tf_op jit(solution)/shard_map/ppermute | solution.py:35
  21.4 4.6 %collective-permute-start.7 = (f32[128,128]{1,0:T(8,128)S(1)}, f32[128,128]{1,0:T(8,128)S(1)}, u32[]{:S(2)}, u32[]{:S(2)}) collective-permute-start(f32[128,128]{1,0:T(8,128)S(1)} %shard_map.130._.refs_2_), channel_id=1, source_target_pairs={{0,2},{1,3},{2,0},{3,1},{4,6},{5,7},{6,4},{7,5},{8,10},{9,11},{10,... | collective-permute-start | bytes 196616 | tf_op jit(solution)/shard_map/ppermute | solution.py:35
  21.9 5.2 %collective-permute-start.6 = (f32[128,128]{1,0:T(8,128)S(1)}, f32[128,128]{1,0:T(8,128)S(1)}, u32[]{:S(2)}, u32[]{:S(2)}) collective-permute-start(f32[128,128]{1,0:T(8,128)S(1)} %shard_map.131.refs_0_), channel_id=1, source_target_pairs={{0,4},{1,5},{2,6},{3,7},{4,0},{5,1},{6,2},{7,3},{8,12},{9,13},{10,... | collective-permute-start | bytes 196616 | tf_op jit(solution)/shard_map/ppermute | solution.py:35
  27.3 1.2 %collective-permute-start.11 = (f32[32,128]{1,0:T(8,128)S(1)}, f32[32,128]{1,0:T(8,128)S(1)}, u32[]{:S(2)}, u32[]{:S(2)}) collective-permute-start(f32[32,128]{1,0:T(8,128)S(1)} %get-tuple-element.34.mine_ref), channel_id=1, source_target_pairs={{0,8},{1,9},{2,10},{3,11},{4,12},{5,13},{6,14},{7,15},{8,0},{9,1},... | collective-permute-start | bytes 49160 | tf_op jit(solution)/shard_map/ppermute | solution.py:35
  28.5 6.4 %collective-permute-start.12 = (f32[288,128]{1,0:T(8,128)S(1)}, f32[288,128]{1,0:T(8,128)S(1)}, u32[]{:S(2)}, u32[]{:S(2)}) collective-permute-start(f32[288,128]{1,0:T(8,128)S(1)} %get-tuple-element.37), channel_id=1, source_target_pairs={{0,1},{1,0},{2,3},{3,2},{4,5},{5,4},{6,7},{7,6},{8,9},{9,8},{10,11... | collective-permute-start | bytes 442376 | tf_op jit(solution)/shard_map/ppermute | solution.py:35
  29.9 5.0 %collective-permute-start.14 = (f32[32,128]{1,0:T(8,128)S(1)}, f32[32,128]{1,0:T(8,128)S(1)}, u32[]{:S(2)}, u32[]{:S(2)}) collective-permute-start(f32[32,128]{1,0:T(8,128)S(1)} %get-tuple-element.38._), channel_id=1, source_target_pairs={{0,17},{1,16},{2,19},{3,18},{4,21},{5,20},{6,23},{7,22},{8,25},{9,... | collective-permute-start | bytes 49160 | tf_op jit(solution)/shard_map/ppermute | solution.py:35
  31.3 3.6 %collective-permute-start.13 = (f32[8,128]{1,0:T(8,128)S(1)}, f32[8,128]{1,0:T(8,128)S(1)}, u32[]{:S(2)}, u32[]{:S(2)}) collective-permute-start(f32[8,128]{1,0:T(8,128)S(1)} %get-tuple-element.36.refs_0_), channel_id=1, source_target_pairs={{0,16},{1,17},{2,18},{3,19},{4,20},{5,21},{6,22},{7,23},{8,24},{9,... | collective-permute-start | bytes 12296 | tf_op jit(solution)/shard_map/ppermute | solution.py:35

commit v7 on v6

--- a/solution.py
+++ b/solution.py
@@ -184,7 +184,7 @@
     return jnp.sum((values * values).reshape(-1, 8, LANES), axis=0)
 
 
-def total_kernel(plan, *refs):
+def total_kernel(plan, slots, *refs):
     low_ref, low_other, high_ref, high_other, state_ref, sum_ref, send_ref = refs
     _, _, _, y = place()
     half = low_ref.shape[0]
@@ -193,20 +193,12 @@
     sum_ref[half:, :] = high
     send_ref[0:8, :] = squares(low) + squares(high)
 
-    def edge(z, start):
-        send_ref[8 : 8 + EDGE, :] = sum_ref[z * plan.rows + start : z * plan.rows + start + EDGE, :]
-        state = state_ref.at[z]
-        old = decayed(state, state.at[2 * plan.rows :], start, start + EDGE)
-        for k in range(2):
-            send_ref[8 + (k + 1) * EDGE : 8 + (k + 2) * EDGE, :] = old[k]
-
-    @pl.when(y == 0)
-    def _():
-        edge(0, 0)
-
-    @pl.when(y == 1)
-    def _():
-        edge(plan.zs - 1, plan.rows - EDGE)
+    at_z, start = y * (plan.zs - 1), pl.multiple_of(y * (plan.rows - EDGE), EDGE)
+    pair = state_ref[at_z, pl.ds(start, EDGE), :]
+    scale = state_ref[at_z, pl.ds(2 * plan.rows + y * (slots - 1), 1), :]
+    edge = sum_ref[pl.ds(pl.multiple_of(at_z * plan.rows + start, EDGE), EDGE), :]
+    for k, value in enumerate((edge, *decode(pair, scale))):
+        send_ref[8 + k * EDGE : 8 + (k + 1) * EDGE, :] = value
 
 
 def core_kernel(mine_ref, other_ref, sum_ref, norm_ref, relay_ref, wide_ref):
@@ -344,7 +336,7 @@
         if bit < bits - 1:
             high = call(add_kernel, half_shape, [high, high_other, low], [VMEM, VMEM, ANY])
             low = call(add_kernel, half_shape, [low, low_other, high], [VMEM, VMEM, ANY])
-    gate = call(token_kernel, struct((8, LANES), F32), [gate, *near[2:]], [VMEM] + [ANY] * (zs - 2))
+    gate = call(token_kernel, struct((8, LANES), F32), [gate, *near[3:]], [VMEM] + [ANY] * (zs - 3))
     state_mine, state_send = call(
         functools.partial(order_kernel, plan),
         [struct((zs, *state_shape), F32), struct((zs, *state_shape), F32)],
@@ -354,7 +346,7 @@
     state_other = plan.swap(state_send, group=1)
     send_rows = 8 + 3 * EDGE
     sum_mine, send = call(
-        functools.partial(total_kernel, plan),
+        functools.partial(total_kernel, plan, slots),
         [part_shape, struct((send_rows, LANES), F32)],
         [low, low_other, high, high_other, state_mine],
     )

time: 36.3 us -> 36.3 us (level)
  no operation moved by 1% of the time
where the time goes in v7:
time: 36.3 us; the launch traced here: 36.1 us
  starting transfers between devices  22.6 us (62%)
  waiting for transfers between devices  7.62 us (21%)
  Pallas kernels  3.85 us (11%)
  between operations  1.37 us (4%)
  local copies, waits for them, and re-layouts  0.66 us (2%)
    ppermute x16, starting transfers between devices, swap(): lax.ppermute(value, ALL, [(i, i ^ mask) for i in range(self.devices)])  22.6 us
    ppermute x16, waiting for transfers between devices, swap(): lax.ppermute(value, ALL, [(i, i ^ mask) for i in range(self.devices)])  7.62 us
    pallas_call x13, Pallas kernels, call(): pl.pallas_call(kernel, out_shape=outs, in_specs=in_specs or [VMEM] * len(...  3.85 us
  transfers between devices with their start and end apart: 16, of which 7 were waited for; matrix products, arithmetic and copies ran while one was open for 0% of the time, Pallas kernels for 4%

profile of v7, /device:TPU:0, one launch (start us, length us, event | category | flops | bytes accessed | tf_op | source)
XLA Modules:
  0.0 36.1 jit_solution(4551884984398028726)
XLA Ops:
  0.6 1.1 %shard_map.127 = bf16[1024,128]{1,0:T(8,128)(2,1)S(1)} custom-call(bf16[1,262144]{1,0:T(2,128)(2,1)} %bitcast.20), custom_call_target="tpu_custom_call" | custom-call | tf_op jit(solution)/shard_map/pallas_call | solution.py:52
  1.8 0.5 %collective-permute-start = (bf16[1024,128]{1,0:T(8,128)(2,1)S(1)}, bf16[1024,128]{1,0:T(8,128)(2,1)S(1)}, u32[]{:S(2)}, u32[]{:S(2)}) collective-permute-start(bf16[1024,128]{1,0:T(8,128)(2,1)S(1)} %shard_map.127), channel_id=1, source_target_pairs={{0,8},{1,9},{2,10},{3,11},{4,12},{5,13},{6,14},{7,15},{8,0},{9,1},... | collective-permute-start | bytes 786440 | tf_op jit(solution)/shard_map/ppermute | solution.py:35
  2.3 1.1 %shard_map.126.mine_ref = bf16[1024,128]{1,0:T(8,128)(2,1)S(1)} custom-call(bf16[1,262144]{1,0:T(2,128)(2,1)} %bitcast.21), custom_call_target="tpu_custom_call" | custom-call | tf_op jit(solution)/shard_map/pallas_call | solution.py:52
  3.4 0.1 collective-permute-done.other_ref
  3.4 0.0 copy-start
  3.4 0.0 copy-start.1
  3.4 0.0 copy-start.2
  3.4 0.1 shard_map.128
  3.5 2.9 %collective-permute-start.1 = (f32[256,128]{1,0:T(8,128)S(1)}, f32[256,128]{1,0:T(8,128)S(1)}, u32[]{:S(2)}, u32[]{:S(2)}) collective-permute-start(f32[256,128]{1,0:T(8,128)S(1)} %get-tuple-element.28), channel_id=1, source_target_pairs={{0,1},{1,0},{2,3},{3,2},{4,5},{5,4},{6,7},{7,6},{8,9},{9,8},{10,11... | collective-permute-start | bytes 393224 | tf_op jit(solution)/shard_map/ppermute | solution.py:35
  6.5 1.5 %collective-permute-start.2 = (f32[256,128]{1,0:T(8,128)S(1)}, f32[256,128]{1,0:T(8,128)S(1)}, u32[]{:S(2)}, u32[]{:S(2)}) collective-permute-start(f32[256,128]{1,0:T(8,128)S(1)} %get-tuple-element.29), channel_id=1, source_target_pairs={{0,16},{1,17},{2,18},{3,19},{4,20},{5,21},{6,22},{7,23},{8,24},{9,... | collective-permute-start | bytes 393224 | tf_op jit(solution)/shard_map/ppermute | solution.py:35
  7.9 0.0 collective-permute-start.3
  8.0 0.0 copy-start.3
  8.0 0.0 copy-start.4
  8.0 0.0 copy-done
  8.0 0.0 copy-done.1
  8.0 0.0 copy-done.2
  8.0 0.6 %copy-done.3 = f32[5]{0:T(128)S(1)} copy-done((f32[5]{0:T(128)S(1)}, f32[5]{0:T(128)}, u32[]{:S(2)}) %copy-start.3) | copy-done | bytes 44
  8.6 0.0 copy-done.4
  8.7 0.1 shard_map.132.refs_0_
  8.7 4.1 %collective-permute-start.8 = (f32[1,136,128]{2,1,0:T(8,128)S(1)}, f32[1,136,128]{2,1,0:T(8,128)S(1)}, u32[]{:S(2)}, u32[]{:S(2)}) collective-permute-start(f32[1,136,128]{2,1,0:T(8,128)S(1)} %shard_map.132.refs_0_), channel_id=1, source_target_pairs={{0,6},{1,7},{2,4},{3,5},{4,2},{5,3},{6,0},{7,1},{8,14},{9,15},{10,... | collective-permute-start | bytes 208904 | tf_op jit(solution)/shard_map/ppermute | solution.py:35
  12.8 0.0 collective-permute-start.10
  12.8 0.0 collective-permute-done.1.refs_1_
  12.8 0.6 %collective-permute-start.9 = (f32[1,136,128]{2,1,0:T(8,128)S(1)}, f32[1,136,128]{2,1,0:T(8,128)S(1)}, u32[]{:S(2)}, u32[]{:S(2)}) collective-permute-start(f32[1,136,128]{2,1,0:T(8,128)S(1)} %shard_map.132.refs_0_), channel_id=1, source_target_pairs={{0,2},{1,3},{2,0},{3,1},{4,6},{5,7},{6,4},{7,5},{8,10},{9,11},{10,... | collective-permute-start | bytes 208904 | tf_op jit(solution)/shard_map/ppermute | solution.py:35
  13.5 0.0 collective-permute-done.2.refs_2_
  13.5 0.8 %collective-permute-done.3.refs_3_ = f32[256,128]{1,0:T(8,128)S(1)} collective-permute-done((f32[256,128]{1,0:T(8,128)S(1)}, f32[256,128]{1,0:T(8,128)S(1)}, u32[]{:S(2)}, u32[]{:S(2)}) %collective-permute-start.3) | collective-permute-done | bytes 131104 | tf_op jit(solution)/shard_map/ppermute | solution.py:35
  14.4 2.8 %collective-permute-start.5 = (f32[128,128]{1,0:T(8,128)S(1)}, f32[128,128]{1,0:T(8,128)S(1)}, u32[]{:S(2)}, u32[]{:S(2)}) collective-permute-start(f32[128,128]{1,0:T(8,128)S(1)} %get-tuple-element.32.mine_ref), channel_id=1, source_target_pairs={{0,4},{1,5},{2,6},{3,7},{4,0},{5,1},{6,2},{7,3},{8,12},{9,13},{10,... | collective-permute-start | bytes 196616 | tf_op jit(solution)/shard_map/ppermute | solution.py:35
  17.2 1.6 %collective-permute-start.4 = (f32[128,128]{1,0:T(8,128)S(1)}, f32[128,128]{1,0:T(8,128)S(1)}, u32[]{:S(2)}, u32[]{:S(2)}) collective-permute-start(f32[128,128]{1,0:T(8,128)S(1)} %get-tuple-element.31._.mine_ref.x_ref), channel_id=1, source_target_pairs={{0,2},{1,3},{2,0},{3,1},{4,6},{5,7},{6,4},{7,5},{8,10},{9,11},{10,... | collective-permute-start | bytes 196616 | tf_op jit(solution)/shard_map/ppermute | solution.py:35
  18.7 0.0 collective-permute-done.8.refs_0_.refs_3_
  18.7 1.0 %collective-permute-done.10.refs_2_ = f32[1,136,128]{2,1,0:T(8,128)S(1)} collective-permute-done((f32[1,136,128]{2,1,0:T(8,128)S(1)}, f32[1,136,128]{2,1,0:T(8,128)S(1)}, u32[]{:S(2)}, u32[]{:S(2)}) %collective-permute-start.10) | collective-permute-done | bytes 69664 | tf_op jit(solution)/shard_map/ppermute | solution.py:35
  19.7 0.0 collective-permute-done.9.refs_1_
  19.7 0.1 shard_map.134
  19.8 1.7 %collective-permute-start.15 = (f32[4,136,128]{2,1,0:T(8,128)S(1)}, f32[4,136,128]{2,1,0:T(8,128)S(1)}, u32[]{:S(2)}, u32[]{:S(2)}) collective-permute-start(f32[4,136,128]{2,1,0:T(8,128)S(1)} %get-tuple-element.39), channel_id=1, source_target_pairs={{0,1},{1,0},{2,3},{3,2},{4,5},{5,4},{6,7},{7,6},{8,9},{9,8},{10,11... | collective-permute-start | bytes 835592 | tf_op jit(solution)/shard_map/ppermute | solution.py:35
  21.4 0.0 collective-permute-done.5.other_ref
  21.4 0.4 %collective-permute-start.7 = (f32[128,128]{1,0:T(8,128)S(1)}, f32[128,128]{1,0:T(8,128)S(1)}, u32[]{:S(2)}, u32[]{:S(2)}) collective-permute-start(f32[128,128]{1,0:T(8,128)S(1)} %shard_map.130._.refs_2_), channel_id=1, source_target_pairs={{0,2},{1,3},{2,0},{3,1},{4,6},{5,7},{6,4},{7,5},{8,10},{9,11},{10,... | collective-permute-start | bytes 196616 | tf_op jit(solution)/shard_map/ppermute | solution.py:35
  21.9 0.0 collective-permute-done.4.other_ref
  21.9 2.8 %collective-permute-start.6 = (f32[128,128]{1,0:T(8,128)S(1)}, f32[128,128]{1,0:T(8,128)S(1)}, u32[]{:S(2)}, u32[]{:S(2)}) collective-permute-start(f32[128,128]{1,0:T(8,128)S(1)} %shard_map.131.refs_0_), channel_id=1, source_target_pairs={{0,4},{1,5},{2,6},{3,7},{4,0},{5,1},{6,2},{7,3},{8,12},{9,13},{10,... | collective-permute-start | bytes 196616 | tf_op jit(solution)/shard_map/ppermute | solution.py:35
  24.7 1.3 %collective-permute-done.7.refs_3_ = f32[128,128]{1,0:T(8,128)S(1)} collective-permute-done((f32[128,128]{1,0:T(8,128)S(1)}, f32[128,128]{1,0:T(8,128)S(1)}, u32[]{:S(2)}, u32[]{:S(2)}) %collective-permute-start.7) | collective-permute-done | bytes 65568 | tf_op jit(solution)/shard_map/ppermute | solution.py:35
  26.0 1.1 %collective-permute-done.6.refs_1_ = f32[128,128]{1,0:T(8,128)S(1)} collective-permute-done((f32[128,128]{1,0:T(8,128)S(1)}, f32[128,128]{1,0:T(8,128)S(1)}, u32[]{:S(2)}, u32[]{:S(2)}) %collective-permute-start.6) | collective-permute-done | bytes 65568 | tf_op jit(solution)/shard_map/ppermute | solution.py:35
  27.1 0.1 shard_map.135
  27.2 0.1 collective-permute-start.11
  27.3 1.2 %collective-permute-done.11.other_ref = f32[32,128]{1,0:T(8,128)S(1)} collective-permute-done((f32[32,128]{1,0:T(8,128)S(1)}, f32[32,128]{1,0:T(8,128)S(1)}, u32[]{:S(2)}, u32[]{:S(2)}) %collective-permute-start.11) | collective-permute-done | bytes 16416 | tf_op jit(solution)/shard_map/ppermute | solution.py:35
  28.5 1.4 %collective-permute-start.12 = (f32[288,128]{1,0:T(8,128)S(1)}, f32[288,128]{1,0:T(8,128)S(1)}, u32[]{:S(2)}, u32[]{:S(2)}) collective-permute-start(f32[288,128]{1,0:T(8,128)S(1)} %get-tuple-element.37), channel_id=1, source_target_pairs={{0,1},{1,0},{2,3},{3,2},{4,5},{5,4},{6,7},{7,6},{8,9},{9,8},{10,11... | collective-permute-start | bytes 442376 | tf_op jit(solution)/shard_map/ppermute | solution.py:35
  29.9 1.4 %collective-permute-start.14 = (f32[32,128]{1,0:T(8,128)S(1)}, f32[32,128]{1,0:T(8,128)S(1)}, u32[]{:S(2)}, u32[]{:S(2)}) collective-permute-start(f32[32,128]{1,0:T(8,128)S(1)} %get-tuple-element.38._), channel_id=1, source_target_pairs={{0,17},{1,16},{2,19},{3,18},{4,21},{5,20},{6,23},{7,22},{8,25},{9,... | collective-permute-start | bytes 49160 | tf_op jit(solution)/shard_map/ppermute | solution.py:35
  31.3 0.7 %collective-permute-start.13 = (f32[8,128]{1,0:T(8,128)S(1)}, f32[8,128]{1,0:T(8,128)S(1)}, u32[]{:S(2)}, u32[]{:S(2)}) collective-permute-start(f32[8,128]{1,0:T(8,128)S(1)} %get-tuple-element.36.refs_0_), channel_id=1, source_target_pairs={{0,16},{1,17},{2,18},{3,19},{4,20},{5,21},{6,22},{7,23},{8,24},{9,... | collective-permute-start | bytes 12296 | tf_op jit(solution)/shard_map/ppermute | solution.py:35
  32.7 0.1 shard_map.137.refs_7_
  32.8 2.1 %collective-permute-done.13.refs_2_ = f32[8,128]{1,0:T(8,128)S(1)} collective-permute-done((f32[8,128]{1,0:T(8,128)S(1)}, f32[8,128]{1,0:T(8,128)S(1)}, u32[]{:S(2)}, u32[]{:S(2)}) %collective-permute-start.13) | collective-permute-done | bytes 4128 | tf_op jit(solution)/shard_map/ppermute | solution.py:35
  34.9 0.0 collective-permute-done.14.refs_3_
  34.9 0.0 collective-permute-done.15.refs_6_
  34.9 0.0 collective-permute-done.12.refs_1_
  34.9 1.2 %shard_map.138 = (f32[64,128]{1,0:T(8,128)}, bf16[512,128]{1,0:T(8,128)(2,1)}, f32[64,128]{1,0:T(8,128)}, f32[64,128]{1,0:T(8,128)}, f32[64,128]{1,0:T(8,128)}, /*index=5*/f32[1,5]{1,0:T(1,128)}, f32[1,5]{1,0:T(1,128)}) custom-call(f32[8,128]{1,0:T(8,128)S(1)} %get-tuple-element.36.refs_0_, f32[288,128]{1,0:T(8,128)S(1)} %collective-permute-done.12.refs_1_, ...), custom_call_target="tpu_custom_call" | custom-call | tf_op jit(solution)/shard_map/pallas_call | solution.py:52
  (5 shorter events, 0.1 us)
Async XLA Ops:
  1.8 1.7 %collective-permute-start = (bf16[1024,128]{1,0:T(8,128)(2,1)S(1)}, bf16[1024,128]{1,0:T(8,128)(2,1)S(1)}, u32[]{:S(2)}, u32[]{:S(2)}) collective-permute-start(bf16[1024,128]{1,0:T(8,128)(2,1)S(1)} %shard_map.127), channel_id=1, source_target_pairs={{0,8},{1,9},{2,10},{3,11},{4,12},{5,13},{6,14},{7,15},{8,0},{9,1},... | collective-permute-start | bytes 786440 | tf_op jit(solution)/shard_map/ppermute | solution.py:35
  3.4 4.6 %copy-start = (s32[8192]{0:T(1024)S(1)}, s32[8192]{0:T(1024)}, u32[]{:S(2)}) copy-start(s32[8192]{0:T(1024)} %param.8) | copy-start | bytes 98308
  3.4 4.6 %copy-start.1 = (s32[8192]{0:T(1024)S(1)}, s32[8192]{0:T(1024)}, u32[]{:S(2)}) copy-start(s32[8192]{0:T(1024)} %param.9) | copy-start | bytes 98308
  3.4 4.6 %copy-start.2 = (f32[8192]{0:T(1024)S(1)}, f32[8192]{0:T(1024)}, u32[]{:S(2)}) copy-start(f32[8192]{0:T(1024)} %param.12) | copy-start | bytes 98308
  3.5 9.3 %collective-permute-start.1 = (f32[256,128]{1,0:T(8,128)S(1)}, f32[256,128]{1,0:T(8,128)S(1)}, u32[]{:S(2)}, u32[]{:S(2)}) collective-permute-start(f32[256,128]{1,0:T(8,128)S(1)} %get-tuple-element.28), channel_id=1, source_target_pairs={{0,1},{1,0},{2,3},{3,2},{4,5},{5,4},{6,7},{7,6},{8,9},{9,8},{10,11... | collective-permute-start | bytes 393224 | tf_op jit(solution)/shard_map/ppermute | solution.py:35
  6.5 7.0 %collective-permute-start.2 = (f32[256,128]{1,0:T(8,128)S(1)}, f32[256,128]{1,0:T(8,128)S(1)}, u32[]{:S(2)}, u32[]{:S(2)}) collective-permute-start(f32[256,128]{1,0:T(8,128)S(1)} %get-tuple-element.29), channel_id=1, source_target_pairs={{0,16},{1,17},{2,18},{3,19},{4,20},{5,21},{6,22},{7,23},{8,24},{9,... | collective-permute-start | bytes 393224 | tf_op jit(solution)/shard_map/ppermute | solution.py:35
  7.9 6.4 %collective-permute-start.3 = (f32[256,128]{1,0:T(8,128)S(1)}, f32[256,128]{1,0:T(8,128)S(1)}, u32[]{:S(2)}, u32[]{:S(2)}) collective-permute-start(f32[256,128]{1,0:T(8,128)S(1)} %get-tuple-element.30), channel_id=1, source_target_pairs={{0,17},{1,16},{2,19},{3,18},{4,21},{5,20},{6,23},{7,22},{8,25},{9,... | collective-permute-start | bytes 393224 | tf_op jit(solution)/shard_map/ppermute | solution.py:35
  8.0 0.7 %copy-start.3 = (f32[5]{0:T(128)S(1)}, f32[5]{0:T(128)}, u32[]{:S(2)}) copy-start(f32[5]{0:T(128)} %param.10) | copy-start | bytes 64
  8.0 0.7 %copy-start.4 = (f32[5]{0:T(128)S(1)}, f32[5]{0:T(128)}, u32[]{:S(2)}) copy-start(f32[5]{0:T(128)} %param.11) | copy-start | bytes 64
  8.7 10.0 %collective-permute-start.8 = (f32[1,136,128]{2,1,0:T(8,128)S(1)}, f32[1,136,128]{2,1,0:T(8,128)S(1)}, u32[]{:S(2)}, u32[]{:S(2)}) collective-permute-start(f32[1,136,128]{2,1,0:T(8,128)S(1)} %shard_map.132.refs_0_), channel_id=1, source_target_pairs={{0,6},{1,7},{2,4},{3,5},{4,2},{5,3},{6,0},{7,1},{8,14},{9,15},{10,... | collective-permute-start | bytes 208904 | tf_op jit(solution)/shard_map/ppermute | solution.py:35
  12.8 6.9 %collective-permute-start.10 = (f32[1,136,128]{2,1,0:T(8,128)S(1)}, f32[1,136,128]{2,1,0:T(8,128)S(1)}, u32[]{:S(2)}, u32[]{:S(2)}) collective-permute-start(f32[1,136,128]{2,1,0:T(8,128)S(1)} %shard_map.132.refs_0_), channel_id=1, source_target_pairs={{0,4},{1,5},{2,6},{3,7},{4,0},{5,1},{6,2},{7,3},{8,12},{9,13},{10,... | collective-permute-start | bytes 208904 | tf_op jit(solution)/shard_map/ppermute | solution.py:35
  12.8 6.8 %collective-permute-start.9 = (f32[1,136,128]{2,1,0:T(8,128)S(1)}, f32[1,136,128]{2,1,0:T(8,128)S(1)}, u32[]{:S(2)}, u32[]{:S(2)}) collective-permute-start(f32[1,136,128]{2,1,0:T(8,128)S(1)} %shard_map.132.refs_0_), channel_id=1, source_target_pairs={{0,2},{1,3},{2,0},{3,1},{4,6},{5,7},{6,4},{7,5},{8,10},{9,11},{10,... | collective-permute-start | bytes 208904 | tf_op jit(solution)/shard_map/ppermute | solution.py:35
  14.4 7.1 %collective-permute-start.5 = (f32[128,128]{1,0:T(8,128)S(1)}, f32[128,128]{1,0:T(8,128)S(1)}, u32[]{:S(2)}, u32[]{:S(2)}) collective-permute-start(f32[128,128]{1,0:T(8,128)S(1)} %get-tuple-element.32.mine_ref), channel_id=1, source_target_pairs={{0,4},{1,5},{2,6},{3,7},{4,0},{5,1},{6,2},{7,3},{8,12},{9,13},{10,... | collective-permute-start | bytes 196616 | tf_op jit(solution)/shard_map/ppermute | solution.py:35
  17.2 4.7 %collective-permute-start.4 = (f32[128,128]{1,0:T(8,128)S(1)}, f32[128,128]{1,0:T(8,128)S(1)}, u32[]{:S(2)}, u32[]{:S(2)}) collective-permute-start(f32[128,128]{1,0:T(8,128)S(1)} %get-tuple-element.31._.mine_ref.x_ref), channel_id=1, source_target_pairs={{0,2},{1,3},{2,0},{3,1},{4,6},{5,7},{6,4},{7,5},{8,10},{9,11},{10,... | collective-permute-start | bytes 196616 | tf_op jit(solution)/shard_map/ppermute | solution.py:35
  19.8 15.2 %collective-permute-start.15 = (f32[4,136,128]{2,1,0:T(8,128)S(1)}, f32[4,136,128]{2,1,0:T(8,128)S(1)}, u32[]{:S(2)}, u32[]{:S(2)}) collective-permute-start(f32[4,136,128]{2,1,0:T(8,128)S(1)} %get-tuple-element.39), channel_id=1, source_target_pairs={{0,1},{1,0},{2,3},{3,2},{4,5},{5,4},{6,7},{7,6},{8,9},{9,8},{10,11... | collective-permute-start | bytes 835592 | tf_op jit(solution)/shard_map/ppermute | solution.py:35
  21.4 4.6 %collective-permute-start.7 = (f32[128,128]{1,0:T(8,128)S(1)}, f32[128,128]{1,0:T(8,128)S(1)}, u32[]{:S(2)}, u32[]{:S(2)}) collective-permute-start(f32[128,128]{1,0:T(8,128)S(1)} %shard_map.130._.refs_2_), channel_id=1, source_target_pairs={{0,2},{1,3},{2,0},{3,1},{4,6},{5,7},{6,4},{7,5},{8,10},{9,11},{10,... | collective-permute-start | bytes 196616 | tf_op jit(solution)/shard_map/ppermute | solution.py:35
  21.9 5.2 %collective-permute-start.6 = (f32[128,128]{1,0:T(8,128)S(1)}, f32[128,128]{1,0:T(8,128)S(1)}, u32[]{:S(2)}, u32[]{:S(2)}) collective-permute-start(f32[128,128]{1,0:T(8,128)S(1)} %shard_map.131.refs_0_), channel_id=1, source_target_pairs={{0,4},{1,5},{2,6},{3,7},{4,0},{5,1},{6,2},{7,3},{8,12},{9,13},{10,... | collective-permute-start | bytes 196616 | tf_op jit(solution)/shard_map/ppermute | solution.py:35
  27.2 1.2 %collective-permute-start.11 = (f32[32,128]{1,0:T(8,128)S(1)}, f32[32,128]{1,0:T(8,128)S(1)}, u32[]{:S(2)}, u32[]{:S(2)}) collective-permute-start(f32[32,128]{1,0:T(8,128)S(1)} %get-tuple-element.34.mine_ref), channel_id=1, source_target_pairs={{0,8},{1,9},{2,10},{3,11},{4,12},{5,13},{6,14},{7,15},{8,0},{9,1},... | collective-permute-start | bytes 49160 | tf_op jit(solution)/shard_map/ppermute | solution.py:35
  28.5 6.4 %collective-permute-start.12 = (f32[288,128]{1,0:T(8,128)S(1)}, f32[288,128]{1,0:T(8,128)S(1)}, u32[]{:S(2)}, u32[]{:S(2)}) collective-permute-start(f32[288,128]{1,0:T(8,128)S(1)} %get-tuple-element.37), channel_id=1, source_target_pairs={{0,1},{1,0},{2,3},{3,2},{4,5},{5,4},{6,7},{7,6},{8,9},{9,8},{10,11... | collective-permute-start | bytes 442376 | tf_op jit(solution)/shard_map/ppermute | solution.py:35
  29.9 5.0 %collective-permute-start.14 = (f32[32,128]{1,0:T(8,128)S(1)}, f32[32,128]{1,0:T(8,128)S(1)}, u32[]{:S(2)}, u32[]{:S(2)}) collective-permute-start(f32[32,128]{1,0:T(8,128)S(1)} %get-tuple-element.38._), channel_id=1, source_target_pairs={{0,17},{1,16},{2,19},{3,18},{4,21},{5,20},{6,23},{7,22},{8,25},{9,... | collective-permute-start | bytes 49160 | tf_op jit(solution)/shard_map/ppermute | solution.py:35
  31.3 3.6 %collective-permute-start.13 = (f32[8,128]{1,0:T(8,128)S(1)}, f32[8,128]{1,0:T(8,128)S(1)}, u32[]{:S(2)}, u32[]{:S(2)}) collective-permute-start(f32[8,128]{1,0:T(8,128)S(1)} %get-tuple-element.36.refs_0_), channel_id=1, source_target_pairs={{0,16},{1,17},{2,18},{3,19},{4,20},{5,21},{6,22},{7,23},{8,24},{9,... | collective-permute-start | bytes 12296 | tf_op jit(solution)/shard_map/ppermute | solution.py:35

commit v8 on v6

--- a/solution.py
+++ b/solution.py
@@ -151,10 +151,17 @@
     return decode(state[low:high, :], scales[slot : slot + 1, :])
 
 
+def codes(pair):
+    v_code = jnp.floor(pair * (1.0 / 256.0))
+    return pair - (v_code * 256.0 + 128.0), v_code
+
+
+def factors(scale):
+    return scale[:, 0:1] * (0.9 / 127.0), scale[:, LANES // 2 : LANES // 2 + 1] * (0.95 / 255.0)
+
+
 def decode(pair, scale):
-    v_code = jnp.floor(pair * (1.0 / 256.0))
-    m_code = pair - (v_code * 256.0 + 128.0)
-    m_scale, v_scale = scale[:, 0:1] * (0.9 / 127.0), scale[:, LANES // 2 : LANES // 2 + 1] * (0.95 / 255.0)
+    (m_code, v_code), (m_scale, v_scale) = codes(pair), factors(scale)
     return m_code * m_scale, v_code * v_scale
 
 
@@ -248,12 +255,22 @@
         master = state[rows + low : rows + high, :]
         return m, v, update, master * (1.0 - 0.0001 * 0.1) - 0.0001 * update
 
+    m_gain, v_gain = 0.1 * clip * first, 0.05 * clip * clip * second
+
+    def weights(grads, state, scales, low, high):
+        slot = (low + EDGE) // (2 * EDGE)
+        m_scale, v_scale = factors(scales[slot : slot + 1, :])
+        (m_code, v_code), grad = codes(state[low:high, :]), grads[low:high, :]
+        m, v = m_code * (m_scale * first) + grad * m_gain, v_code * (v_scale * second) + grad * grad * v_gain
+        master = state[rows + low : rows + high, :]
+        return master * (1.0 - 0.0001 * 0.1) - 0.0001 * (m / (jnp.sqrt(v) + 1e-08))
+
     for k in range(plan.zs):
         sides = ((sum_mine, state_mine, scales_mine), (sum_other, state_other, scales_other))
         for flip, (sums, states, scales) in enumerate(sides):
             start = pl.multiple_of((2 * k + (y ^ flip)) * rows, rows)
             grads = sums.at[pl.ds(k * rows, rows)]
-            out = jnp.concatenate([step(grads, states.at[k], scales(k), *piece)[3] for piece in pieces(plan, slots)], axis=0)
+            out = jnp.concatenate([weights(grads, states.at[k], scales(k), *piece) for piece in pieces(plan, slots)], axis=0)
             weights_out[pl.ds(start, rows), :] = out.astype(BF16)
 
     grads = sum_mine.at[pl.ds(pl.multiple_of(z * rows, rows), rows)]

time: 36.3 us -> 36.3 us (level)
  no operation moved by 1% of the time
where the time goes in v8:
time: 36.3 us; the launch traced here: 36.1 us
  starting transfers between devices  22.6 us (62%)
  waiting for transfers between devices  7.62 us (21%)
  Pallas kernels  3.83 us (11%)
  between operations  1.38 us (4%)
  local copies, waits for them, and re-layouts  0.66 us (2%)
    ppermute x16, starting transfers between devices, swap(): lax.ppermute(value, ALL, [(i, i ^ mask) for i in range(self.devices)])  22.6 us
    ppermute x16, waiting for transfers between devices, swap(): lax.ppermute(value, ALL, [(i, i ^ mask) for i in range(self.devices)])  7.62 us
    pallas_call x13, Pallas kernels, call(): pl.pallas_call(kernel, out_shape=outs, in_specs=in_specs or [VMEM] * len(...  3.83 us
  transfers between devices with their start and end apart: 16, of which 7 were waited for; matrix products, arithmetic and copies ran while one was open for 0% of the time, Pallas kernels for 4%

profile of v8, /device:TPU:0, one launch (start us, length us, event | category | flops | bytes accessed | tf_op | source)
XLA Modules:
  0.0 36.1 jit_solution(1470867069297109775)
XLA Ops:
  0.6 1.1 %shard_map.127 = bf16[1024,128]{1,0:T(8,128)(2,1)S(1)} custom-call(bf16[1,262144]{1,0:T(2,128)(2,1)} %bitcast.20), custom_call_target="tpu_custom_call" | custom-call | tf_op jit(solution)/shard_map/pallas_call | solution.py:52
  1.8 0.5 %collective-permute-start = (bf16[1024,128]{1,0:T(8,128)(2,1)S(1)}, bf16[1024,128]{1,0:T(8,128)(2,1)S(1)}, u32[]{:S(2)}, u32[]{:S(2)}) collective-permute-start(bf16[1024,128]{1,0:T(8,128)(2,1)S(1)} %shard_map.127), channel_id=1, source_target_pairs={{0,8},{1,9},{2,10},{3,11},{4,12},{5,13},{6,14},{7,15},{8,0},{9,1},... | collective-permute-start | bytes 786440 | tf_op jit(solution)/shard_map/ppermute | solution.py:35
  2.3 1.1 %shard_map.126.mine_ref = bf16[1024,128]{1,0:T(8,128)(2,1)S(1)} custom-call(bf16[1,262144]{1,0:T(2,128)(2,1)} %bitcast.21), custom_call_target="tpu_custom_call" | custom-call | tf_op jit(solution)/shard_map/pallas_call | solution.py:52
  3.4 0.1 collective-permute-done.other_ref
  3.4 0.0 copy-start
  3.4 0.0 copy-start.1
  3.4 0.0 copy-start.2
  3.4 0.1 shard_map.128
  3.5 2.9 %collective-permute-start.1 = (f32[256,128]{1,0:T(8,128)S(1)}, f32[256,128]{1,0:T(8,128)S(1)}, u32[]{:S(2)}, u32[]{:S(2)}) collective-permute-start(f32[256,128]{1,0:T(8,128)S(1)} %get-tuple-element.28), channel_id=1, source_target_pairs={{0,1},{1,0},{2,3},{3,2},{4,5},{5,4},{6,7},{7,6},{8,9},{9,8},{10,11... | collective-permute-start | bytes 393224 | tf_op jit(solution)/shard_map/ppermute | solution.py:35
  6.5 1.5 %collective-permute-start.2 = (f32[256,128]{1,0:T(8,128)S(1)}, f32[256,128]{1,0:T(8,128)S(1)}, u32[]{:S(2)}, u32[]{:S(2)}) collective-permute-start(f32[256,128]{1,0:T(8,128)S(1)} %get-tuple-element.29), channel_id=1, source_target_pairs={{0,16},{1,17},{2,18},{3,19},{4,20},{5,21},{6,22},{7,23},{8,24},{9,... | collective-permute-start | bytes 393224 | tf_op jit(solution)/shard_map/ppermute | solution.py:35
  7.9 0.0 collective-permute-start.3
  8.0 0.0 copy-start.3
  8.0 0.0 copy-start.4
  8.0 0.0 copy-done
  8.0 0.0 copy-done.1
  8.0 0.0 copy-done.2
  8.0 0.6 %copy-done.3 = f32[5]{0:T(128)S(1)} copy-done((f32[5]{0:T(128)S(1)}, f32[5]{0:T(128)}, u32[]{:S(2)}) %copy-start.3) | copy-done | bytes 44
  8.6 0.0 copy-done.4
  8.7 0.1 shard_map.132.refs_0_
  8.7 4.1 %collective-permute-start.9 = (f32[1,136,128]{2,1,0:T(8,128)S(1)}, f32[1,136,128]{2,1,0:T(8,128)S(1)}, u32[]{:S(2)}, u32[]{:S(2)}) collective-permute-start(f32[1,136,128]{2,1,0:T(8,128)S(1)} %shard_map.132.refs_0_), channel_id=1, source_target_pairs={{0,6},{1,7},{2,4},{3,5},{4,2},{5,3},{6,0},{7,1},{8,14},{9,15},{10,... | collective-permute-start | bytes 208904 | tf_op jit(solution)/shard_map/ppermute | solution.py:35
  12.8 0.0 collective-permute-start.8
  12.8 0.0 collective-permute-done.1.refs_1_
  12.8 0.6 %collective-permute-start.10 = (f32[1,136,128]{2,1,0:T(8,128)S(1)}, f32[1,136,128]{2,1,0:T(8,128)S(1)}, u32[]{:S(2)}, u32[]{:S(2)}) collective-permute-start(f32[1,136,128]{2,1,0:T(8,128)S(1)} %shard_map.132.refs_0_), channel_id=1, source_target_pairs={{0,2},{1,3},{2,0},{3,1},{4,6},{5,7},{6,4},{7,5},{8,10},{9,11},{10,... | collective-permute-start | bytes 208904 | tf_op jit(solution)/shard_map/ppermute | solution.py:35
  13.5 0.0 collective-permute-done.2.refs_2_
  13.5 0.8 %collective-permute-done.3.refs_3_ = f32[256,128]{1,0:T(8,128)S(1)} collective-permute-done((f32[256,128]{1,0:T(8,128)S(1)}, f32[256,128]{1,0:T(8,128)S(1)}, u32[]{:S(2)}, u32[]{:S(2)}) %collective-permute-start.3) | collective-permute-done | bytes 131104 | tf_op jit(solution)/shard_map/ppermute | solution.py:35
  14.4 2.8 %collective-permute-start.5 = (f32[128,128]{1,0:T(8,128)S(1)}, f32[128,128]{1,0:T(8,128)S(1)}, u32[]{:S(2)}, u32[]{:S(2)}) collective-permute-start(f32[128,128]{1,0:T(8,128)S(1)} %get-tuple-element.32.mine_ref), channel_id=1, source_target_pairs={{0,4},{1,5},{2,6},{3,7},{4,0},{5,1},{6,2},{7,3},{8,12},{9,13},{10,... | collective-permute-start | bytes 196616 | tf_op jit(solution)/shard_map/ppermute | solution.py:35
  17.2 1.6 %collective-permute-start.4 = (f32[128,128]{1,0:T(8,128)S(1)}, f32[128,128]{1,0:T(8,128)S(1)}, u32[]{:S(2)}, u32[]{:S(2)}) collective-permute-start(f32[128,128]{1,0:T(8,128)S(1)} %get-tuple-element.31._.mine_ref.x_ref), channel_id=1, source_target_pairs={{0,2},{1,3},{2,0},{3,1},{4,6},{5,7},{6,4},{7,5},{8,10},{9,11},{10,... | collective-permute-start | bytes 196616 | tf_op jit(solution)/shard_map/ppermute | solution.py:35
  18.7 0.0 collective-permute-done.9.refs_1_.refs_3_
  18.7 1.0 %collective-permute-done.8.refs_0_.refs_2_ = f32[1,136,128]{2,1,0:T(8,128)S(1)} collective-permute-done((f32[1,136,128]{2,1,0:T(8,128)S(1)}, f32[1,136,128]{2,1,0:T(8,128)S(1)}, u32[]{:S(2)}, u32[]{:S(2)}) %collective-permute-start.8) | collective-permute-done | bytes 69664 | tf_op jit(solution)/shard_map/ppermute | solution.py:35
  19.7 0.0 collective-permute-done.10.refs_1_
  19.8 1.7 %collective-permute-start.15 = (f32[4,136,128]{2,1,0:T(8,128)S(1)}, f32[4,136,128]{2,1,0:T(8,128)S(1)}, u32[]{:S(2)}, u32[]{:S(2)}) collective-permute-start(f32[4,136,128]{2,1,0:T(8,128)S(1)} %get-tuple-element.39), channel_id=1, source_target_pairs={{0,1},{1,0},{2,3},{3,2},{4,5},{5,4},{6,7},{7,6},{8,9},{9,8},{10,11... | collective-permute-start | bytes 835592 | tf_op jit(solution)/shard_map/ppermute | solution.py:35
  21.4 0.0 collective-permute-done.5.other_ref
  21.4 0.4 %collective-permute-start.7 = (f32[128,128]{1,0:T(8,128)S(1)}, f32[128,128]{1,0:T(8,128)S(1)}, u32[]{:S(2)}, u32[]{:S(2)}) collective-permute-start(f32[128,128]{1,0:T(8,128)S(1)} %shard_map.130._.refs_2_), channel_id=1, source_target_pairs={{0,2},{1,3},{2,0},{3,1},{4,6},{5,7},{6,4},{7,5},{8,10},{9,11},{10,... | collective-permute-start | bytes 196616 | tf_op jit(solution)/shard_map/ppermute | solution.py:35
  21.9 0.0 collective-permute-done.4.other_ref
  21.9 2.8 %collective-permute-start.6 = (f32[128,128]{1,0:T(8,128)S(1)}, f32[128,128]{1,0:T(8,128)S(1)}, u32[]{:S(2)}, u32[]{:S(2)}) collective-permute-start(f32[128,128]{1,0:T(8,128)S(1)} %shard_map.131.refs_0_), channel_id=1, source_target_pairs={{0,4},{1,5},{2,6},{3,7},{4,0},{5,1},{6,2},{7,3},{8,12},{9,13},{10,... | collective-permute-start | bytes 196616 | tf_op jit(solution)/shard_map/ppermute | solution.py:35
  24.7 1.4 %collective-permute-done.7.refs_3_ = f32[128,128]{1,0:T(8,128)S(1)} collective-permute-done((f32[128,128]{1,0:T(8,128)S(1)}, f32[128,128]{1,0:T(8,128)S(1)}, u32[]{:S(2)}, u32[]{:S(2)}) %collective-permute-start.7) | collective-permute-done | bytes 65568 | tf_op jit(solution)/shard_map/ppermute | solution.py:35
  26.0 1.1 %collective-permute-done.6.refs_1_ = f32[128,128]{1,0:T(8,128)S(1)} collective-permute-done((f32[128,128]{1,0:T(8,128)S(1)}, f32[128,128]{1,0:T(8,128)S(1)}, u32[]{:S(2)}, u32[]{:S(2)}) %collective-permute-start.6) | collective-permute-done | bytes 65568 | tf_op jit(solution)/shard_map/ppermute | solution.py:35
  27.1 0.1 shard_map.135
  27.3 0.1 collective-permute-start.11
  27.3 1.2 %collective-permute-done.11.other_ref = f32[32,128]{1,0:T(8,128)S(1)} collective-permute-done((f32[32,128]{1,0:T(8,128)S(1)}, f32[32,128]{1,0:T(8,128)S(1)}, u32[]{:S(2)}, u32[]{:S(2)}) %collective-permute-start.11) | collective-permute-done | bytes 16416 | tf_op jit(solution)/shard_map/ppermute | solution.py:35
  28.5 1.4 %collective-permute-start.12 = (f32[288,128]{1,0:T(8,128)S(1)}, f32[288,128]{1,0:T(8,128)S(1)}, u32[]{:S(2)}, u32[]{:S(2)}) collective-permute-start(f32[288,128]{1,0:T(8,128)S(1)} %get-tuple-element.37), channel_id=1, source_target_pairs={{0,1},{1,0},{2,3},{3,2},{4,5},{5,4},{6,7},{7,6},{8,9},{9,8},{10,11... | collective-permute-start | bytes 442376 | tf_op jit(solution)/shard_map/ppermute | solution.py:35
  29.9 1.4 %collective-permute-start.14 = (f32[32,128]{1,0:T(8,128)S(1)}, f32[32,128]{1,0:T(8,128)S(1)}, u32[]{:S(2)}, u32[]{:S(2)}) collective-permute-start(f32[32,128]{1,0:T(8,128)S(1)} %get-tuple-element.38._), channel_id=1, source_target_pairs={{0,17},{1,16},{2,19},{3,18},{4,21},{5,20},{6,23},{7,22},{8,25},{9,... | collective-permute-start | bytes 49160 | tf_op jit(solution)/shard_map/ppermute | solution.py:35
  31.3 0.7 %collective-permute-start.13 = (f32[8,128]{1,0:T(8,128)S(1)}, f32[8,128]{1,0:T(8,128)S(1)}, u32[]{:S(2)}, u32[]{:S(2)}) collective-permute-start(f32[8,128]{1,0:T(8,128)S(1)} %get-tuple-element.36.refs_0_), channel_id=1, source_target_pairs={{0,16},{1,17},{2,18},{3,19},{4,20},{5,21},{6,22},{7,23},{8,24},{9,... | collective-permute-start | bytes 12296 | tf_op jit(solution)/shard_map/ppermute | solution.py:35
  32.7 0.1 shard_map.137.refs_7_
  32.8 2.1 %collective-permute-done.13.refs_2_ = f32[8,128]{1,0:T(8,128)S(1)} collective-permute-done((f32[8,128]{1,0:T(8,128)S(1)}, f32[8,128]{1,0:T(8,128)S(1)}, u32[]{:S(2)}, u32[]{:S(2)}) %collective-permute-start.13) | collective-permute-done | bytes 4128 | tf_op jit(solution)/shard_map/ppermute | solution.py:35
  34.9 0.0 collective-permute-done.14.refs_3_
  34.9 0.0 collective-permute-done.15.refs_6_
  34.9 0.0 collective-permute-done.12.refs_1_
  35.0 1.1 %shard_map.138 = (f32[64,128]{1,0:T(8,128)}, bf16[512,128]{1,0:T(8,128)(2,1)}, f32[64,128]{1,0:T(8,128)}, f32[64,128]{1,0:T(8,128)}, f32[64,128]{1,0:T(8,128)}, /*index=5*/f32[1,5]{1,0:T(1,128)}, f32[1,5]{1,0:T(1,128)}) custom-call(f32[8,128]{1,0:T(8,128)S(1)} %get-tuple-element.36.refs_0_, f32[288,128]{1,0:T(8,128)S(1)} %collective-permute-done.12.refs_1_, ...), custom_call_target="tpu_custom_call" | custom-call | tf_op jit(solution)/shard_map/pallas_call | solution.py:52
  (6 shorter events, 0.1 us)
Async XLA Ops:
  1.8 1.7 %collective-permute-start = (bf16[1024,128]{1,0:T(8,128)(2,1)S(1)}, bf16[1024,128]{1,0:T(8,128)(2,1)S(1)}, u32[]{:S(2)}, u32[]{:S(2)}) collective-permute-start(bf16[1024,128]{1,0:T(8,128)(2,1)S(1)} %shard_map.127), channel_id=1, source_target_pairs={{0,8},{1,9},{2,10},{3,11},{4,12},{5,13},{6,14},{7,15},{8,0},{9,1},... | collective-permute-start | bytes 786440 | tf_op jit(solution)/shard_map/ppermute | solution.py:35
  3.4 4.6 %copy-start = (s32[8192]{0:T(1024)S(1)}, s32[8192]{0:T(1024)}, u32[]{:S(2)}) copy-start(s32[8192]{0:T(1024)} %param.8) | copy-start | bytes 98308
  3.4 4.6 %copy-start.1 = (s32[8192]{0:T(1024)S(1)}, s32[8192]{0:T(1024)}, u32[]{:S(2)}) copy-start(s32[8192]{0:T(1024)} %param.9) | copy-start | bytes 98308
  3.4 4.6 %copy-start.2 = (f32[8192]{0:T(1024)S(1)}, f32[8192]{0:T(1024)}, u32[]{:S(2)}) copy-start(f32[8192]{0:T(1024)} %param.12) | copy-start | bytes 98308
  3.5 9.3 %collective-permute-start.1 = (f32[256,128]{1,0:T(8,128)S(1)}, f32[256,128]{1,0:T(8,128)S(1)}, u32[]{:S(2)}, u32[]{:S(2)}) collective-permute-start(f32[256,128]{1,0:T(8,128)S(1)} %get-tuple-element.28), channel_id=1, source_target_pairs={{0,1},{1,0},{2,3},{3,2},{4,5},{5,4},{6,7},{7,6},{8,9},{9,8},{10,11... | collective-permute-start | bytes 393224 | tf_op jit(solution)/shard_map/ppermute | solution.py:35
  6.5 7.0 %collective-permute-start.2 = (f32[256,128]{1,0:T(8,128)S(1)}, f32[256,128]{1,0:T(8,128)S(1)}, u32[]{:S(2)}, u32[]{:S(2)}) collective-permute-start(f32[256,128]{1,0:T(8,128)S(1)} %get-tuple-element.29), channel_id=1, source_target_pairs={{0,16},{1,17},{2,18},{3,19},{4,20},{5,21},{6,22},{7,23},{8,24},{9,... | collective-permute-start | bytes 393224 | tf_op jit(solution)/shard_map/ppermute | solution.py:35
  7.9 6.4 %collective-permute-start.3 = (f32[256,128]{1,0:T(8,128)S(1)}, f32[256,128]{1,0:T(8,128)S(1)}, u32[]{:S(2)}, u32[]{:S(2)}) collective-permute-start(f32[256,128]{1,0:T(8,128)S(1)} %get-tuple-element.30), channel_id=1, source_target_pairs={{0,17},{1,16},{2,19},{3,18},{4,21},{5,20},{6,23},{7,22},{8,25},{9,... | collective-permute-start | bytes 393224 | tf_op jit(solution)/shard_map/ppermute | solution.py:35
  8.0 0.7 %copy-start.3 = (f32[5]{0:T(128)S(1)}, f32[5]{0:T(128)}, u32[]{:S(2)}) copy-start(f32[5]{0:T(128)} %param.10) | copy-start | bytes 64
  8.0 0.7 %copy-start.4 = (f32[5]{0:T(128)S(1)}, f32[5]{0:T(128)}, u32[]{:S(2)}) copy-start(f32[5]{0:T(128)} %param.11) | copy-start | bytes 64
  8.7 10.0 %collective-permute-start.9 = (f32[1,136,128]{2,1,0:T(8,128)S(1)}, f32[1,136,128]{2,1,0:T(8,128)S(1)}, u32[]{:S(2)}, u32[]{:S(2)}) collective-permute-start(f32[1,136,128]{2,1,0:T(8,128)S(1)} %shard_map.132.refs_0_), channel_id=1, source_target_pairs={{0,6},{1,7},{2,4},{3,5},{4,2},{5,3},{6,0},{7,1},{8,14},{9,15},{10,... | collective-permute-start | bytes 208904 | tf_op jit(solution)/shard_map/ppermute | solution.py:35
  12.8 6.9 %collective-permute-start.8 = (f32[1,136,128]{2,1,0:T(8,128)S(1)}, f32[1,136,128]{2,1,0:T(8,128)S(1)}, u32[]{:S(2)}, u32[]{:S(2)}) collective-permute-start(f32[1,136,128]{2,1,0:T(8,128)S(1)} %shard_map.132.refs_0_), channel_id=1, source_target_pairs={{0,4},{1,5},{2,6},{3,7},{4,0},{5,1},{6,2},{7,3},{8,12},{9,13},{10,... | collective-permute-start | bytes 208904 | tf_op jit(solution)/shard_map/ppermute | solution.py:35
  12.8 6.9 %collective-permute-start.10 = (f32[1,136,128]{2,1,0:T(8,128)S(1)}, f32[1,136,128]{2,1,0:T(8,128)S(1)}, u32[]{:S(2)}, u32[]{:S(2)}) collective-permute-start(f32[1,136,128]{2,1,0:T(8,128)S(1)} %shard_map.132.refs_0_), channel_id=1, source_target_pairs={{0,2},{1,3},{2,0},{3,1},{4,6},{5,7},{6,4},{7,5},{8,10},{9,11},{10,... | collective-permute-start | bytes 208904 | tf_op jit(solution)/shard_map/ppermute | solution.py:35
  14.4 7.1 %collective-permute-start.5 = (f32[128,128]{1,0:T(8,128)S(1)}, f32[128,128]{1,0:T(8,128)S(1)}, u32[]{:S(2)}, u32[]{:S(2)}) collective-permute-start(f32[128,128]{1,0:T(8,128)S(1)} %get-tuple-element.32.mine_ref), channel_id=1, source_target_pairs={{0,4},{1,5},{2,6},{3,7},{4,0},{5,1},{6,2},{7,3},{8,12},{9,13},{10,... | collective-permute-start | bytes 196616 | tf_op jit(solution)/shard_map/ppermute | solution.py:35
  17.2 4.7 %collective-permute-start.4 = (f32[128,128]{1,0:T(8,128)S(1)}, f32[128,128]{1,0:T(8,128)S(1)}, u32[]{:S(2)}, u32[]{:S(2)}) collective-permute-start(f32[128,128]{1,0:T(8,128)S(1)} %get-tuple-element.31._.mine_ref.x_ref), channel_id=1, source_target_pairs={{0,2},{1,3},{2,0},{3,1},{4,6},{5,7},{6,4},{7,5},{8,10},{9,11},{10,... | collective-permute-start | bytes 196616 | tf_op jit(solution)/shard_map/ppermute | solution.py:35
  19.8 15.2 %collective-permute-start.15 = (f32[4,136,128]{2,1,0:T(8,128)S(1)}, f32[4,136,128]{2,1,0:T(8,128)S(1)}, u32[]{:S(2)}, u32[]{:S(2)}) collective-permute-start(f32[4,136,128]{2,1,0:T(8,128)S(1)} %get-tuple-element.39), channel_id=1, source_target_pairs={{0,1},{1,0},{2,3},{3,2},{4,5},{5,4},{6,7},{7,6},{8,9},{9,8},{10,11... | collective-permute-start | bytes 835592 | tf_op jit(solution)/shard_map/ppermute | solution.py:35
  21.4 4.6 %collective-permute-start.7 = (f32[128,128]{1,0:T(8,128)S(1)}, f32[128,128]{1,0:T(8,128)S(1)}, u32[]{:S(2)}, u32[]{:S(2)}) collective-permute-start(f32[128,128]{1,0:T(8,128)S(1)} %shard_map.130._.refs_2_), channel_id=1, source_target_pairs={{0,2},{1,3},{2,0},{3,1},{4,6},{5,7},{6,4},{7,5},{8,10},{9,11},{10,... | collective-permute-start | bytes 196616 | tf_op jit(solution)/shard_map/ppermute | solution.py:35
  21.9 5.2 %collective-permute-start.6 = (f32[128,128]{1,0:T(8,128)S(1)}, f32[128,128]{1,0:T(8,128)S(1)}, u32[]{:S(2)}, u32[]{:S(2)}) collective-permute-start(f32[128,128]{1,0:T(8,128)S(1)} %shard_map.131.refs_0_), channel_id=1, source_target_pairs={{0,4},{1,5},{2,6},{3,7},{4,0},{5,1},{6,2},{7,3},{8,12},{9,13},{10,... | collective-permute-start | bytes 196616 | tf_op jit(solution)/shard_map/ppermute | solution.py:35
  27.3 1.2 %collective-permute-start.11 = (f32[32,128]{1,0:T(8,128)S(1)}, f32[32,128]{1,0:T(8,128)S(1)}, u32[]{:S(2)}, u32[]{:S(2)}) collective-permute-start(f32[32,128]{1,0:T(8,128)S(1)} %get-tuple-element.34.mine_ref), channel_id=1, source_target_pairs={{0,8},{1,9},{2,10},{3,11},{4,12},{5,13},{6,14},{7,15},{8,0},{9,1},... | collective-permute-start | bytes 49160 | tf_op jit(solution)/shard_map/ppermute | solution.py:35
  28.5 6.4 %collective-permute-start.12 = (f32[288,128]{1,0:T(8,128)S(1)}, f32[288,128]{1,0:T(8,128)S(1)}, u32[]{:S(2)}, u32[]{:S(2)}) collective-permute-start(f32[288,128]{1,0:T(8,128)S(1)} %get-tuple-element.37), channel_id=1, source_target_pairs={{0,1},{1,0},{2,3},{3,2},{4,5},{5,4},{6,7},{7,6},{8,9},{9,8},{10,11... | collective-permute-start | bytes 442376 | tf_op jit(solution)/shard_map/ppermute | solution.py:35
  29.9 5.0 %collective-permute-start.14 = (f32[32,128]{1,0:T(8,128)S(1)}, f32[32,128]{1,0:T(8,128)S(1)}, u32[]{:S(2)}, u32[]{:S(2)}) collective-permute-start(f32[32,128]{1,0:T(8,128)S(1)} %get-tuple-element.38._), channel_id=1, source_target_pairs={{0,17},{1,16},{2,19},{3,18},{4,21},{5,20},{6,23},{7,22},{8,25},{9,... | collective-permute-start | bytes 49160 | tf_op jit(solution)/shard_map/ppermute | solution.py:35
  31.3 3.6 %collective-permute-start.13 = (f32[8,128]{1,0:T(8,128)S(1)}, f32[8,128]{1,0:T(8,128)S(1)}, u32[]{:S(2)}, u32[]{:S(2)}) collective-permute-start(f32[8,128]{1,0:T(8,128)S(1)} %get-tuple-element.36.refs_0_), channel_id=1, source_target_pairs={{0,16},{1,17},{2,18},{3,19},{4,20},{5,21},{6,22},{7,23},{8,24},{9,... | collective-permute-start | bytes 12296 | tf_op jit(solution)/shard_map/ppermute | solution.py:35
